TPU v7x, 256 devices: a whole 4x4x8 slice. The times are simulated.
256 devices in a mesh: wide: 64 (over y_lo, x, z), feat: 4 (over y_hi, core).
Axes of the slice: x: 4, y: 4 (y_hi: 2, y_lo: 2; y = y_hi * 2 + y_lo), z: 8, core: 2. Of those that a mesh axis runs over, the one named last changes fastest.
Arguments:
- features: bfloat16 [131072, 8192], P('wide', 'feat'), may hold values from -6 to 6
- queries: bfloat16 [128, 8192], replicated, may hold values from -0.0625 to 0.0625
- inverse_factor: bfloat16 [4, 2048, 8192], P('feat', 'wide'), may hold values from -0.3 to 1
Outputs:
- scores: float32 [131072, 128], P(('wide', 'feat'))
All inputs are finite; a program needn't handle non-finite values.
Results may differ from a plain program's by a relative error of at most 0.015.
Values may be sent and summed in bfloat16 or wider, within the bound.
No kernel may reach another device: no remote copies, remote signals or barrier semaphores. Data moves between devices by JAX's collectives and lax.ppermute only.
A program may use at most 64 MiB of HBM per device.

v0:
```python
import jax
import jax.numpy as jnp
from jax import lax
from jax.sharding import PartitionSpec as P


def on_device(features, queries, inverse_factor):
    factor = inverse_factor[0]
    row_count = features.shape[0]
    total_rows = row_count * lax.axis_size("wide")
    query_block = jnp.einsum("kc,mc->km", factor, queries, preferred_element_type=jnp.float32)
    query_cols = lax.all_gather(query_block.astype(jnp.bfloat16), "wide", axis=0, tiled=True)
    partial_rows = jnp.dot(features, query_cols, preferred_element_type=jnp.float32)
    row_weights = lax.psum(partial_rows, "feat").astype(jnp.bfloat16)
    gram_block = lax.psum_scatter(
        jnp.einsum("nk,nm->km", features, row_weights, preferred_element_type=jnp.float32),
        "wide",
        scatter_dimension=0,
        tiled=True,
    )
    residual_block = (gram_block / total_rows + 0.1 * query_block).astype(jnp.bfloat16)
    residual_feat = lax.all_gather(residual_block, "wide", axis=0, tiled=True)
    residual_whole = lax.all_gather(residual_feat, "feat", axis=0, tiled=True)
    corrected_block = (
        2.0 * query_block - jnp.dot(factor, residual_whole, preferred_element_type=jnp.float32)
    ).astype(jnp.bfloat16)
    corrected_cols = lax.all_gather(corrected_block, "wide", axis=0, tiled=True)
    partial_scores = jnp.dot(features, corrected_cols, preferred_element_type=jnp.float32)
    return lax.psum_scatter(
        partial_scores.astype(jnp.bfloat16), "feat", scatter_dimension=0, tiled=True
    ).astype(jnp.float32)


def solution(mesh):
    in_specs = (P("wide", "feat"), P(), P("feat", "wide", None))
    out_specs = P(("wide", "feat"), None)
    return jax.shard_map(
        on_device, mesh=mesh, in_specs=in_specs, out_specs=out_specs, check_vma=False
    )
```

profile of v0, /device:TPU:1, one launch (start us, length us, event | category | flops | bytes accessed | tf_op | source)
XLA Modules:
  0.0 916.5 jit_solution(16830240364277676171)
XLA Ops:
  6.5 0.0 copy-start
  6.5 0.0 reduce-scatter.3.cloned.1.call-start
  6.5 1.6 copy-done
  8.1 1.8 fusion.7
  10.0 134.4 %all_gather.12 = bf16[2048,128]{1,0:T(8,128)(2,1)S(1)} all-gather(bf16[32,128]{1,0:T(8,128)(2,1)S(1)} %get-tuple-element.5), channel_id=1, replica_groups=mesh['wide'=64,'feat'=4] {'wide'}, dimensions={0}, use_global_device_ids=true | all-gather | bytes 532480 | tf_op jit(solution)/shard_map/all_gather | solution.py:12
  144.3 6.3 convolution_bitcast_fusion.1
  150.7 58.7 %all-reduce.1 = bf16[2048,128]{0,1:T(8,128)(2,1)} all-reduce(f32[2048,128]{0,1:T(8,128)S(1)} %convolution_bitcast_fusion.1), channel_id=1, replica_groups=mesh['wide'=64,'feat'=4] {'feat'}, use_global_device_ids=true, to_apply=%region_0.0 | all-reduce | flops 262144 | bytes 1572864 | tf_op jit(solution)/shard_map/psum | solution.py:14
  209.3 0.0 copy-start.1
  209.3 7.9 convolution_bitcast_fusion
  217.3 0.0 reduce-scatter.3.cloned.1.call-update
  217.3 0.0 all-gather.2.cloned.1.call-start
  217.4 257.1 %reduce-scatter.3.cloned.1.call-done = f32[32,128]{1,0:T(8,128)} async-done(((f32[2048,128]{1,0:T(8,128)}), f32[32,128]{1,0:T(8,128)}) %reduce-scatter.3.cloned.1.call-update) | async-done | bytes 16400 | tf_op jit(solution)/shard_map/reduce_scatter | solution.py:15
  474.5 0.7 add_convert_fusion
  475.2 136.3 %all_gather.13 = bf16[2048,128]{1,0:T(8,128)(2,1)} all-gather(bf16[32,128]{1,0:T(8,128)(2,1)S(1)} %add_convert_fusion), channel_id=1, replica_groups=mesh['wide'=64,'feat'=4] {'wide'}, dimensions={0}, use_global_device_ids=true | all-gather | bytes 532480 | tf_op jit(solution)/shard_map/all_gather | solution.py:22
  611.5 0.0 all-gather.2.cloned.1.call-update
  611.5 0.0 reduce-scatter.5.cloned.1.call-start
  611.6 103.2 %all-gather.2.cloned.1.call-done = bf16[8192,128]{1,0:T(8,128)(2,1)} async-done(((bf16[2048,128]{1,0:T(8,128)(2,1)}), bf16[8192,128]{1,0:T(8,128)(2,1)}) %all-gather.2.cloned.1.call-update) | async-done | bytes 2097168 | tf_op jit(solution)/shard_map/all_gather | solution.py:23
  714.8 0.0 copy-done.1
  714.8 2.0 fusion.2
  716.8 130.2 %all_gather.15 = bf16[2048,128]{1,0:T(8,128)(2,1)S(1)} all-gather(bf16[32,128]{1,0:T(8,128)(2,1)S(1)} %fusion.2), channel_id=1, replica_groups=mesh['wide'=64,'feat'=4] {'wide'}, dimensions={0}, use_global_device_ids=true | all-gather | bytes 532480 | tf_op jit(solution)/shard_map/all_gather | solution.py:27
  847.1 7.1 fusion
  854.2 0.0 reduce-scatter.5.cloned.1.call-update
  854.2 54.0 %reduce-scatter.5.cloned.1.call-done = bf16[512,128]{0,1:T(8,128)(2,1)} async-done(((bf16[2048,128]{0,1:T(8,128)(2,1)}), bf16[512,128]{0,1:T(8,128)(2,1)}) %reduce-scatter.5.cloned.1.call-update) | async-done | bytes 131088 | tf_op jit(solution)/shard_map/reduce_scatter | solution.py:29
  908.2 1.7 copy.4
Async XLA Ops:
  6.5 1.6 copy-start
  6.5 467.9 %reduce-scatter.3.cloned.1.call-start = ((), (), s32[]{:S(2)}) async-start(), calls=%async_computation.2 | async-start | bytes 1064960 | tf_op jit(solution)/shard_map/reduce_scatter | solution.py:15
  209.3 505.5 %copy-start.1 = (bf16[1,32,8192]{2,1,0:T(8,128)(2,1)S(1)}, bf16[1,32,8192]{2,1,0:T(8,128)(2,1)}, u32[]{:S(2)}) copy-start(bf16[1,32,8192]{2,1,0:T(8,128)(2,1)} %param.5) | copy-start | bytes 1572868
  217.3 497.5 %all-gather.2.cloned.1.call-start = ((), (), s32[]{:S(2)}) async-start(), calls=%async_computation.3 | async-start | bytes 2621440 | tf_op jit(solution)/shard_map/all_gather | solution.py:23
  611.5 296.7 %reduce-scatter.5.cloned.1.call-start = ((), (), s32[]{:S(2)}) async-start(), calls=%async_computation.4 | async-start | bytes 655360 | tf_op jit(solution)/shard_map/reduce_scatter | solution.py:29
Sparse Core Ops, SparseCore 0:
  217.4 257.0 reduce-scatter.2
  611.6 103.1 all-gather.1
  854.3 53.8 reduce-scatter.4
where the time goes:
time: 917 us; the launch traced here: 916 us
  blocking collectives  460 us (50%)
  waiting for transfers between devices  414 us (45%)
  matrix products  25.3 us (3%)
  between operations  13.1 us (1%)
    reduce_scatter x1, waiting for transfers between devices, on_device(): lax.psum_scatter(jnp.einsum('nk,nm->km', features, row_weights, preferred...  257 us
    all_gather x1, blocking collectives, on_device(): residual_feat = lax.all_gather(residual_block, 'wide', axis=0, tiled=True)  136 us
    all_gather x1, blocking collectives, on_device(): lax.all_gather(query_block.astype(jnp.bfloat16), 'wide', axis=0, tiled=True)  134 us
    all_gather x1, blocking collectives, on_device(): corrected_cols = lax.all_gather(corrected_block, 'wide', axis=0, tiled=True)  130 us
    all_gather x1, waiting for transfers between devices, on_device(): residual_whole = lax.all_gather(residual_feat, 'feat', axis=0, tiled=True)  103 us
    psum x1, blocking collectives, on_device(): row_weights = lax.psum(partial_rows, 'feat').astype(jnp.bfloat16)  58.7 us
    reduce_scatter x1, waiting for transfers between devices, on_device(): lax.psum_scatter(partial_scores.astype(jnp.bfloat16), 'feat', scatter_dim...  54 us
  transfers between devices with their start and end apart: 3, of which 3 were waited for; matrix products, arithmetic and copies ran while one was open for 0% of the time, Pallas kernels for 0%

commit v1 on v0

v1 whole, which is shorter than its diff:
```python
import jax
import jax.numpy as jnp
from jax import lax
from jax.sharding import PartitionSpec as P

CORE_SWAP = [(0, 1), (1, 0), (2, 3), (3, 2)]
CHIP_SWAP = [(0, 2), (2, 0), (1, 3), (3, 1)]


def swap_core(block):
    return lax.ppermute(block, "feat", CORE_SWAP)


def swap_chip(block):
    return lax.ppermute(block, "feat", CHIP_SWAP)


def gather_wide(block):
    width = lax.axis_size("wide")
    copies = jnp.tile(block, (width, 1))
    return lax.all_to_all(copies, "wide", 0, 0, tiled=True)


def half(block, which, axis=0):
    size = block.shape[axis] // 2
    return lax.dynamic_slice_in_dim(block, which * size, size, axis)


def on_device(features, queries, inverse_factor):
    f32, bf16 = jnp.float32, jnp.bfloat16
    factor = inverse_factor[0]
    width = lax.axis_size("wide")
    row_count, cols = features.shape
    depth = factor.shape[0]
    total_rows = row_count * width
    place = lax.axis_index("feat")
    chip, core = place // 2, place % 2

    by_core = factor.reshape(depth, 2, 2, cols).transpose(2, 1, 0, 3)
    keep = lax.dynamic_index_in_dim(by_core, core, 0, keepdims=False)
    give = lax.dynamic_index_in_dim(by_core, 1 - core, 0, keepdims=False)
    got = swap_core(give)
    both = jnp.where(core == 0, jnp.stack([keep, got], 1), jnp.stack([got, keep], 1))
    keep = lax.dynamic_index_in_dim(both, chip, 0, keepdims=False)
    give = lax.dynamic_index_in_dim(both, 1 - chip, 0, keepdims=False)
    got = swap_chip(give)
    own_cols = jnp.where(chip == 0, jnp.stack([keep, got]), jnp.stack([got, keep]))
    own_cols = own_cols.reshape(4 * depth, cols)

    query_block = jnp.einsum("kc,mc->km", factor, queries, preferred_element_type=f32)
    query_cols = gather_wide(query_block.astype(bf16))

    partial = jnp.dot(features, query_cols, preferred_element_type=f32).astype(bf16)
    got = swap_core(half(partial, 1 - core))
    chip_sum = (half(partial, core).astype(f32) + got.astype(f32)).astype(bf16)
    got = swap_chip(chip_sum)
    mine = (chip_sum.astype(f32) + got.astype(f32)).astype(bf16)
    other = swap_core(mine)
    row_weights = jnp.concatenate(
        [jnp.where(core == 0, mine, other), jnp.where(core == 0, other, mine)], 0
    )

    gram_part = jnp.einsum("nk,nm->km", features, row_weights, preferred_element_type=f32)
    gram_parts = lax.all_to_all(gram_part.astype(bf16), "wide", 0, 0, tiled=True)
    gram_block = jnp.sum(gram_parts.reshape(width, depth, -1).astype(f32), axis=0)
    residual_block = (gram_block / total_rows + 0.1 * query_block).astype(bf16)
    residual_cols = gather_wide(residual_block)

    product = jnp.dot(own_cols, residual_cols, preferred_element_type=f32)
    product = product.reshape(2, 2, depth, -1)
    give = lax.dynamic_index_in_dim(product, 1 - core, 1, keepdims=False)
    keep = lax.dynamic_index_in_dim(product, core, 1, keepdims=False)
    product = keep + swap_core(give)
    give = lax.dynamic_index_in_dim(product, 1 - chip, 0, keepdims=False)
    keep = lax.dynamic_index_in_dim(product, chip, 0, keepdims=False)
    product = keep + swap_chip(give)
    corrected_block = (2.0 * query_block - product).astype(bf16)
    corrected_cols = gather_wide(corrected_block)

    partial = jnp.dot(features, corrected_cols, preferred_element_type=f32).astype(bf16)
    quarters = partial.reshape(2, 2, row_count // 4, -1)
    give = lax.dynamic_index_in_dim(quarters, 1 - core, 1, keepdims=False)
    keep = lax.dynamic_index_in_dim(quarters, core, 1, keepdims=False)
    chip_sum = keep.astype(f32) + swap_core(give).astype(f32)
    give = lax.dynamic_index_in_dim(chip_sum, 1 - chip, 0, keepdims=False).astype(bf16)
    keep = lax.dynamic_index_in_dim(chip_sum, chip, 0, keepdims=False)
    return keep + swap_chip(give).astype(f32)


def solution(mesh):
    in_specs = (P("wide", "feat"), P(), P("feat", "wide", None))
    out_specs = P(("wide", "feat"), None)
    return jax.shard_map(
        on_device, mesh=mesh, in_specs=in_specs, out_specs=out_specs, check_vma=False
    )
```

time: 917 us -> 166 us (0.18)
  blocking collectives: 460 us -> 24.5 us
  waiting for transfers between devices: 414 us -> 61.6 us
  starting transfers between devices: 0.09 us -> 46.1 us
  between operations: 13.1 us -> 0.25 us
    all_gather x3 -> x0, blocking collectives: 401 us -> none  [the longest x1 136 us: on_device(): residual_feat = lax.all_gather(residual_block, 'wide', axis=0, tiled=True)]
    reduce_scatter x2 -> x0, waiting for transfers between devices: 311 us -> none  [the longest x1 257 us: on_device(): lax.psum_scatter(jnp.einsum('nk,nm->km', features, row_weights, preferred...]
    all_gather x1 -> x0, waiting for transfers between devices: 103 us -> none  [on_device(): residual_whole = lax.all_gather(residual_feat, 'feat', axis=0, tiled=True)]
    psum x1 -> x0, blocking collectives: 58.7 us -> none  [on_device(): row_weights = lax.psum(partial_rows, 'feat').astype(jnp.bfloat16)]
    all_to_all x0 -> x3, waiting for transfers between devices: none -> 34.1 us  [the longest x1 17.3 us: on_device(): lax.all_to_all(gram_part.astype(bf16), 'wide', 0, 0, tiled=True)]
    ppermute x0 -> x9, waiting for transfers between devices: none -> 27.5 us  [the longest x4 22.8 us: swap_chip(): return lax.ppermute(block, 'feat', CHIP_SWAP)]
    all_to_all x0 -> x3, starting transfers between devices: none -> 24.5 us  [the longest x2 19 us: gather_wide(): return lax.all_to_all(copies, 'wide', 0, 0, tiled=True)]
    all_to_all x0 -> x1, blocking collectives: none -> 24.5 us  [gather_wide(): return lax.all_to_all(copies, 'wide', 0, 0, tiled=True)]
  transfers between devices with their start and end apart: 3 -> 12, of which waited for: 3 -> 11; matrix products, arithmetic and copies ran while one was open for 0% -> 2% of each run, Pallas kernels for 0% -> 0%
where the time goes in v1:
time: 166 us
  waiting for transfers between devices  61.6 us (37%)
  starting transfers between devices  46.1 us (28%)
  blocking collectives  24.5 us (15%)
  matrix products  20.5 us (12%)
  local copies, waits for them, and re-layouts  10.6 us (6%)
  other arithmetic  2.17 us (1%)
    all_to_all x1, blocking collectives, gather_wide(): return lax.all_to_all(copies, 'wide', 0, 0, tiled=True)  24.5 us
    ppermute x4, waiting for transfers between devices, swap_chip(): return lax.ppermute(block, 'feat', CHIP_SWAP)  22.8 us
    all_to_all x2, starting transfers between devices, gather_wide(): return lax.all_to_all(copies, 'wide', 0, 0, tiled=True)  19 us
    all_to_all x1, waiting for transfers between devices, on_device(): lax.all_to_all(gram_part.astype(bf16), 'wide', 0, 0, tiled=True)  17.3 us
    all_to_all x2, waiting for transfers between devices, gather_wide(): return lax.all_to_all(copies, 'wide', 0, 0, tiled=True)  16.8 us
    ppermute x5, starting transfers between devices, swap_core(): return lax.ppermute(block, 'feat', CORE_SWAP)  11 us
    ppermute x4, starting transfers between devices, swap_chip(): return lax.ppermute(block, 'feat', CHIP_SWAP)  10.6 us
    dot_general x1, matrix products, on_device(): jnp.dot(features, corrected_cols, preferred_element_type=f32).astype(bf16)  6.32 us
  transfers between devices with their start and end apart: 12, of which 11 were waited for; matrix products, arithmetic and copies ran while one was open for 2% of the time, Pallas kernels for 0%

profile of v1, /device:TPU:1, one launch (start us, length us, event | category | flops | bytes accessed | tf_op | source)
XLA Modules:
  0.0 165.7 jit_solution(2288403736191945310)
XLA Ops:
  0.0 1.6 copy-done
  1.6 1.8 %fusion.20 = (bf16[32,128]{1,0:T(8,128)(2,1)S(1)}, f32[32,128]{1,0:T(8,128)S(1)}) fusion(bf16[128,8192]{1,0:T(8,128)(2,1)S(1)} %copy-done, bf16[1,32,8192]{2,1,0:T(8,128)(2,1)} %param.5), kind=kOutput, calls=%fused_computation.47 | convolution fusion | flops 67112960 | bytes 2646016 | tf_op jit(solution)/shard_map/kc,mc->km/dot_general | solution.py:50
  4.3 13.5 %all-to-all-start = ((bf16[64,32,128]{2,1,0:T(8,128)(2,1)}), bf16[64,32,128]{2,1,0:T(8,128)(2,1)S(1)}, u32[]{:S(2)}, u32[]{:S(2)}) async-start(bf16[64,32,128]{2,1,0:T(8,128)(2,1)} %tile.6), calls=%async_computation | async-start | bytes 1048576 | tf_op jit(solution)/shard_map/all_to_all | solution.py:21
  17.8 16.8 %all-to-all-done = bf16[64,32,128]{2,1,0:T(8,128)(2,1)S(1)} async-done(((bf16[64,32,128]{2,1,0:T(8,128)(2,1)}), bf16[64,32,128]{2,1,0:T(8,128)(2,1)S(1)}, u32[]{:S(2)}, u32[]{:S(2)}) %all-to-all-start) | async-done | bytes 524320 | tf_op jit(solution)/shard_map/all_to_all | solution.py:21
  34.6 6.3 %convolution_convert_fusion.2 = bf16[128,2048]{1,0:T(8,128)(2,1)S(1)} fusion(bf16[2048,128]{1,0:T(8,128)(2,1)S(1)} %bitcast.66, bf16[2048,2048]{1,0:T(8,128)(2,1)} %param.3), kind=kOutput, calls=%fused_computation.2 | convolution fusion | flops 1074003968 | bytes 9437184 | tf_op jit(solution)/shard_map/dot_general | solution.py:53
  41.0 3.0 %collective-permute-start.2 = (bf16[1024,128]{0,1:T(8,128)(2,1)S(1)}, bf16[1024,128]{0,1:T(8,128)(2,1)S(1)}, u32[]{:S(2)}, u32[]{:S(2)}) collective-permute-start(bf16[1024,128]{0,1:T(8,128)(2,1)S(1)} %dynamic-slice_bitcast_fusion), channel_id=1, source_target_pairs={{0,1},{1,0},{2,3},{3,2},{4,5},{5,4},{6,7},{7,6},{8,9},{9,8},{10,11... | collective-permute-start | bytes 786440 | tf_op jit(solution)/shard_map/ppermute | solution.py:11
  44.0 1.2 collective-permute-done.2
  45.2 2.7 %collective-permute-start.3 = (bf16[1024,128]{0,1:T(8,128)(2,1)S(1)}, bf16[1024,128]{0,1:T(8,128)(2,1)S(1)}, u32[]{:S(2)}, u32[]{:S(2)}) collective-permute-start(bf16[1024,128]{0,1:T(8,128)(2,1)S(1)} %fusion.11), channel_id=1, source_target_pairs={{0,2},{2,0},{1,3},{3,1},{4,6},{6,4},{5,7},{7,5},{8,10},{10,8},{9,1... | collective-permute-start | bytes 786440 | tf_op jit(solution)/shard_map/ppermute | solution.py:15
  47.9 6.4 %collective-permute-done.3 = bf16[1024,128]{0,1:T(8,128)(2,1)S(1)} collective-permute-done((bf16[1024,128]{0,1:T(8,128)(2,1)S(1)}, bf16[1024,128]{0,1:T(8,128)(2,1)S(1)}, u32[]{:S(2)}, u32[]{:S(2)}) %collective-permute-start.3) | collective-permute-done | bytes 262176 | tf_op jit(solution)/shard_map/ppermute | solution.py:15
  54.4 1.3 collective-permute-start.4
  55.7 1.2 collective-permute-done.4
  56.9 4.7 %fusion = bf16[2048,128]{0,1:T(8,128)(2,1)S(1)} fusion(bf16[2048,2048]{1,0:T(8,128)(2,1)} %param.3, bf16[1024,128]{0,1:T(8,128)(2,1)S(1)} %get-tuple-element.12, bf16[1024,128]{0,1:T(8,128)(2,1)S(1)} %get-tuple-element.11), kind=kOutput, calls=%fused_computation.3 | convolution fusion | flops 1075052544 | bytes 9437184 | tf_op jit(solution)/shard_map/nk,nm->km/dot_general | solution.py:63
  61.6 1.0 copy.10
  62.6 5.5 %all-to-all-start.1 = ((bf16[64,32,128]{2,1,0:T(8,128)(2,1)}), bf16[64,32,128]{2,1,0:T(8,128)(2,1)}, u32[]{:S(2)}, u32[]{:S(2)}) async-start(bf16[64,32,128]{2,1,0:T(8,128)(2,1)} %bitcast.68), calls=%async_computation.1 | async-start | bytes 1048576 | tf_op jit(solution)/shard_map/all_to_all | solution.py:64
  68.5 17.3 %all-to-all-done.1 = bf16[64,32,128]{2,1,0:T(8,128)(2,1)} async-done(((bf16[64,32,128]{2,1,0:T(8,128)(2,1)}), bf16[64,32,128]{2,1,0:T(8,128)(2,1)}, u32[]{:S(2)}, u32[]{:S(2)}) %all-to-all-start.1) | async-done | bytes 524320 | tf_op jit(solution)/shard_map/all_to_all | solution.py:64
  85.8 1.1 convert_reduce_fusion
  87.9 5.5 %all-to-all-start.2 = ((bf16[64,32,128]{2,1,0:T(8,128)(2,1)}), bf16[64,32,128]{2,1,0:T(8,128)(2,1)}, u32[]{:S(2)}, u32[]{:S(2)}) async-start(bf16[64,32,128]{2,1,0:T(8,128)(2,1)} %tile.7), calls=%async_computation.2 | async-start | bytes 1048576 | tf_op jit(solution)/shard_map/all_to_all | solution.py:21
  93.4 1.1 constant_dynamic-slice_fusion.4
  94.8 1.9 %collective-permute-start = (bf16[2,32,2048]{2,1,0:T(8,128)(2,1)S(1)}, bf16[2,32,2048]{2,1,0:T(8,128)(2,1)S(1)}, u32[]{:S(2)}, u32[]{:S(2)}) collective-permute-start(bf16[2,32,2048]{2,1,0:T(8,128)(2,1)S(1)} %bitcast.70), channel_id=1, source_target_pairs={{0,1},{1,0},{2,3},{3,2},{4,5},{5,4},{6,7},{7,6},{8,9},{9,8},{10,11... | collective-permute-start | bytes 786440 | tf_op jit(solution)/shard_map/ppermute | solution.py:11
  97.9 2.9 %collective-permute-start.1 = (bf16[2,32,2048]{2,1,0:T(8,128)(2,1)S(1)}, bf16[2,32,2048]{2,1,0:T(8,128)(2,1)S(1)}, u32[]{:S(2)}, u32[]{:S(2)}) collective-permute-start(bf16[2,32,2048]{2,1,0:T(8,128)(2,1)S(1)} %get-tuple-element.8), channel_id=1, source_target_pairs={{0,2},{2,0},{1,3},{3,1},{4,6},{6,4},{5,7},{7,5},{8,10},{10,8},{9,1... | collective-permute-start | bytes 786440 | tf_op jit(solution)/shard_map/ppermute | solution.py:15
  100.8 10.9 %collective-permute-done.1 = bf16[2,32,2048]{2,1,0:T(8,128)(2,1)S(1)} collective-permute-done((bf16[2,32,2048]{2,1,0:T(8,128)(2,1)S(1)}, bf16[2,32,2048]{2,1,0:T(8,128)(2,1)S(1)}, u32[]{:S(2)}, u32[]{:S(2)}) %collective-permute-start.1) | collective-permute-done | bytes 262176 | tf_op jit(solution)/shard_map/ppermute | solution.py:15
  111.7 1.3 fusion.2
  113.1 1.3 collective-permute-start.5
  115.2 2.7 %collective-permute-start.6 = (f32[32,128]{1,0:T(8,128)S(1)}, f32[32,128]{1,0:T(8,128)S(1)}, u32[]{:S(2)}, u32[]{:S(2)}) collective-permute-start(f32[32,128]{1,0:T(8,128)S(1)} %dynamic-slice_bitcast_fusion.3), channel_id=1, source_target_pairs={{0,2},{2,0},{1,3},{3,1},{4,6},{6,4},{5,7},{7,5},{8,10},{10,8},{9,1... | collective-permute-start | bytes 49160 | tf_op jit(solution)/shard_map/ppermute | solution.py:15
  117.9 1.5 collective-permute-done.6
  119.5 24.5 %all_to_all.36 = bf16[64,32,128]{2,1,0:T(8,128)(2,1)S(1)} all-to-all(bf16[64,32,128]{2,1,0:T(8,128)(2,1)S(1)} %tile.8), channel_id=1, replica_groups=mesh['wide'=64,'feat'=4] {'wide'}, dimensions={0} | all-to-all | bytes 1048576 | tf_op jit(solution)/shard_map/all_to_all | solution.py:21
  144.0 6.3 %fusion.1 = bf16[2048,128]{0,1:T(8,128)(2,1)S(1)} fusion(bf16[2048,128]{1,0:T(8,128)(2,1)S(1)} %bitcast.67, bf16[2048,2048]{1,0:T(8,128)(2,1)} %param.3), kind=kOutput, calls=%fused_computation.4 | convolution fusion | flops 1074003968 | bytes 9437184 | tf_op jit(solution)/shard_map/dot_general | solution.py:80
  150.7 1.9 %constant_dynamic-slice_fusion.1 = (bf16[2,1,512,128]{2,1,0,3:T(2,128)(2,1)S(1)}, bf16[2,1,512,128]{2,1,0,3:T(2,128)(2,1)}) fusion(bf16[2,2,512,128]{2,1,0,3:T(2,128)(2,1)S(1)} %reshape.37, s32[]{:T(128)S(6)} %select_n.74, s32[]{:T(128)S(6)} %select_n.75), kind=kLoop, calls=%fused_computation.41 | loop fusion | bytes 1048584 | tf_op jit(solution)/shard_map/jit(dynamic_index_in_dim)/dynamic_slice | solution.py:83
  152.5 1.3 copy.12
  153.8 3.6 %collective-permute-start.7 = (bf16[2,512,128]{2,1,0:T(8,128)(2,1)S(1)}, bf16[2,512,128]{2,1,0:T(8,128)(2,1)S(1)}, u32[]{:S(2)}, u32[]{:S(2)}) collective-permute-start(bf16[2,512,128]{2,1,0:T(8,128)(2,1)S(1)} %bitcast.71), channel_id=1, source_target_pairs={{0,1},{1,0},{2,3},{3,2},{4,5},{5,4},{6,7},{7,6},{8,9},{9,8},{10,11... | collective-permute-start | bytes 786440 | tf_op jit(solution)/shard_map/ppermute | solution.py:11
  158.7 2.3 %collective-permute-start.8 = (bf16[512,128]{1,0:T(8,128)(2,1)S(1)}, bf16[512,128]{1,0:T(8,128)(2,1)S(1)}, u32[]{:S(2)}, u32[]{:S(2)}) collective-permute-start(bf16[512,128]{1,0:T(8,128)(2,1)S(1)} %fusion.15), channel_id=1, source_target_pairs={{0,2},{2,0},{1,3},{3,1},{4,6},{6,4},{5,7},{7,5},{8,10},{10,8},{9,1... | collective-permute-start | bytes 393224 | tf_op jit(solution)/shard_map/ppermute | solution.py:15
  161.0 4.0 %collective-permute-done.8 = bf16[512,128]{1,0:T(8,128)(2,1)S(1)} collective-permute-done((bf16[512,128]{1,0:T(8,128)(2,1)S(1)}, bf16[512,128]{1,0:T(8,128)(2,1)S(1)}, u32[]{:S(2)}, u32[]{:S(2)}) %collective-permute-start.8) | collective-permute-done | bytes 131104 | tf_op jit(solution)/shard_map/ppermute | solution.py:15
  (29 shorter events, 7.2 us)
Async XLA Ops:
  0.0 1.6 copy-start
  4.3 30.3 %all-to-all-start = ((bf16[64,32,128]{2,1,0:T(8,128)(2,1)}), bf16[64,32,128]{2,1,0:T(8,128)(2,1)S(1)}, u32[]{:S(2)}, u32[]{:S(2)}) async-start(bf16[64,32,128]{2,1,0:T(8,128)(2,1)} %tile.6), calls=%async_computation | async-start | bytes 1048576 | tf_op jit(solution)/shard_map/all_to_all | solution.py:21
  41.0 4.1 %collective-permute-start.2 = (bf16[1024,128]{0,1:T(8,128)(2,1)S(1)}, bf16[1024,128]{0,1:T(8,128)(2,1)S(1)}, u32[]{:S(2)}, u32[]{:S(2)}) collective-permute-start(bf16[1024,128]{0,1:T(8,128)(2,1)S(1)} %dynamic-slice_bitcast_fusion), channel_id=1, source_target_pairs={{0,1},{1,0},{2,3},{3,2},{4,5},{5,4},{6,7},{7,6},{8,9},{9,8},{10,11... | collective-permute-start | bytes 786440 | tf_op jit(solution)/shard_map/ppermute | solution.py:11
  45.2 9.1 %collective-permute-start.3 = (bf16[1024,128]{0,1:T(8,128)(2,1)S(1)}, bf16[1024,128]{0,1:T(8,128)(2,1)S(1)}, u32[]{:S(2)}, u32[]{:S(2)}) collective-permute-start(bf16[1024,128]{0,1:T(8,128)(2,1)S(1)} %fusion.11), channel_id=1, source_target_pairs={{0,2},{2,0},{1,3},{3,1},{4,6},{6,4},{5,7},{7,5},{8,10},{10,8},{9,1... | collective-permute-start | bytes 786440 | tf_op jit(solution)/shard_map/ppermute | solution.py:15
  54.4 2.5 %collective-permute-start.4 = (bf16[1024,128]{0,1:T(8,128)(2,1)S(1)}, bf16[1024,128]{0,1:T(8,128)(2,1)S(1)}, u32[]{:S(2)}, u32[]{:S(2)}) collective-permute-start(bf16[1024,128]{0,1:T(8,128)(2,1)S(1)} %add_convert_fusion), channel_id=1, source_target_pairs={{0,1},{1,0},{2,3},{3,2},{4,5},{5,4},{6,7},{7,6},{8,9},{9,8},{10,11... | collective-permute-start | bytes 786440 | tf_op jit(solution)/shard_map/ppermute | solution.py:11
  56.9 11.3 %copy-start.1 = (bf16[1,32,8192]{2,1,0:T(8,128)(2,1)S(1)}, bf16[1,32,8192]{2,1,0:T(8,128)(2,1)}, u32[]{:S(2)}) copy-start(bf16[1,32,8192]{2,1,0:T(8,128)(2,1)} %param.5) | copy-start | bytes 1572868
  62.6 23.2 %all-to-all-start.1 = ((bf16[64,32,128]{2,1,0:T(8,128)(2,1)}), bf16[64,32,128]{2,1,0:T(8,128)(2,1)}, u32[]{:S(2)}, u32[]{:S(2)}) async-start(bf16[64,32,128]{2,1,0:T(8,128)(2,1)} %bitcast.68), calls=%async_computation.1 | async-start | bytes 1048576 | tf_op jit(solution)/shard_map/all_to_all | solution.py:64
  87.9 23.8 %all-to-all-start.2 = ((bf16[64,32,128]{2,1,0:T(8,128)(2,1)}), bf16[64,32,128]{2,1,0:T(8,128)(2,1)}, u32[]{:S(2)}, u32[]{:S(2)}) async-start(bf16[64,32,128]{2,1,0:T(8,128)(2,1)} %tile.7), calls=%async_computation.2 | async-start | bytes 1048576 | tf_op jit(solution)/shard_map/all_to_all | solution.py:21
  94.8 3.0 %collective-permute-start = (bf16[2,32,2048]{2,1,0:T(8,128)(2,1)S(1)}, bf16[2,32,2048]{2,1,0:T(8,128)(2,1)S(1)}, u32[]{:S(2)}, u32[]{:S(2)}) collective-permute-start(bf16[2,32,2048]{2,1,0:T(8,128)(2,1)S(1)} %bitcast.70), channel_id=1, source_target_pairs={{0,1},{1,0},{2,3},{3,2},{4,5},{5,4},{6,7},{7,6},{8,9},{9,8},{10,11... | collective-permute-start | bytes 786440 | tf_op jit(solution)/shard_map/ppermute | solution.py:11
  97.9 13.8 %collective-permute-start.1 = (bf16[2,32,2048]{2,1,0:T(8,128)(2,1)S(1)}, bf16[2,32,2048]{2,1,0:T(8,128)(2,1)S(1)}, u32[]{:S(2)}, u32[]{:S(2)}) collective-permute-start(bf16[2,32,2048]{2,1,0:T(8,128)(2,1)S(1)} %get-tuple-element.8), channel_id=1, source_target_pairs={{0,2},{2,0},{1,3},{3,1},{4,6},{6,4},{5,7},{7,5},{8,10},{10,8},{9,1... | collective-permute-start | bytes 786440 | tf_op jit(solution)/shard_map/ppermute | solution.py:15
  113.1 2.2 %collective-permute-start.5 = (f32[2,32,128]{2,1,0:T(8,128)S(1)}, f32[2,32,128]{2,1,0:T(8,128)S(1)}, u32[]{:S(2)}, u32[]{:S(2)}) collective-permute-start(f32[2,32,128]{2,1,0:T(8,128)S(1)} %dynamic-slice_bitcast_fusion.2), channel_id=1, source_target_pairs={{0,1},{1,0},{2,3},{3,2},{4,5},{5,4},{6,7},{7,6},{8,9},{9,8},{10,11... | collective-permute-start | bytes 98312 | tf_op jit(solution)/shard_map/ppermute | solution.py:11
  115.2 4.2 %collective-permute-start.6 = (f32[32,128]{1,0:T(8,128)S(1)}, f32[32,128]{1,0:T(8,128)S(1)}, u32[]{:S(2)}, u32[]{:S(2)}) collective-permute-start(f32[32,128]{1,0:T(8,128)S(1)} %dynamic-slice_bitcast_fusion.3), channel_id=1, source_target_pairs={{0,2},{2,0},{1,3},{3,1},{4,6},{6,4},{5,7},{7,5},{8,10},{10,8},{9,1... | collective-permute-start | bytes 49160 | tf_op jit(solution)/shard_map/ppermute | solution.py:15
  153.8 4.7 %collective-permute-start.7 = (bf16[2,512,128]{2,1,0:T(8,128)(2,1)S(1)}, bf16[2,512,128]{2,1,0:T(8,128)(2,1)S(1)}, u32[]{:S(2)}, u32[]{:S(2)}) collective-permute-start(bf16[2,512,128]{2,1,0:T(8,128)(2,1)S(1)} %bitcast.71), channel_id=1, source_target_pairs={{0,1},{1,0},{2,3},{3,2},{4,5},{5,4},{6,7},{7,6},{8,9},{9,8},{10,11... | collective-permute-start | bytes 786440 | tf_op jit(solution)/shard_map/ppermute | solution.py:11
  158.7 6.3 %collective-permute-start.8 = (bf16[512,128]{1,0:T(8,128)(2,1)S(1)}, bf16[512,128]{1,0:T(8,128)(2,1)S(1)}, u32[]{:S(2)}, u32[]{:S(2)}) collective-permute-start(bf16[512,128]{1,0:T(8,128)(2,1)S(1)} %fusion.15), channel_id=1, source_target_pairs={{0,2},{2,0},{1,3},{3,1},{4,6},{6,4},{5,7},{7,5},{8,10},{10,8},{9,1... | collective-permute-start | bytes 393224 | tf_op jit(solution)/shard_map/ppermute | solution.py:15

commit v2 on v0

v2 whole, which is shorter than its diff:
```python
import functools
import jax
import jax.numpy as jnp
from jax import lax
from jax.experimental import pallas as pl
from jax.experimental.pallas import tpu as pltpu
from jax.sharding import PartitionSpec as P

CORE_SWAP = [(0, 1), (1, 0), (2, 3), (3, 2)]
CHIP_SWAP = [(0, 2), (2, 0), (1, 3), (3, 1)]
F32, BF16 = jnp.float32, jnp.bfloat16
IN_VMEM = pl.BlockSpec(memory_space=pltpu.VMEM)


def swap_core(block):
    return lax.ppermute(block, "feat", CORE_SWAP)


def swap_chip(block):
    return lax.ppermute(block, "feat", CHIP_SWAP)


def exchange_wide(blocks):
    return lax.all_to_all(blocks, "wide", 0, 0, tiled=True)


def local_call(body, operands, shapes, name):
    return pl.pallas_call(
        body,
        in_specs=[IN_VMEM] * len(operands),
        out_specs=[IN_VMEM] * len(shapes),
        out_shape=[jax.ShapeDtypeStruct(shape, dtype) for shape, dtype in shapes],
        compiler_params=pltpu.CompilerParams(vmem_limit_bytes=32 << 20),
        name=name,
    )(*operands)


def span(start, size):
    return pl.ds(pl.multiple_of(start, size), size)


def precond_body(steps, factor_ref, queries_ref, block_ref, total_ref):
    step = pl.program_id(0)

    @pl.when(step == 0)
    def _():
        total_ref[...] = jnp.zeros_like(total_ref)

    total_ref[...] += lax.dot_general(
        factor_ref[...], queries_ref[...], (((1,), (1,)), ((), ())), preferred_element_type=F32
    )

    @pl.when(step == steps - 1)
    def _():
        block_ref[...] = total_ref[...]


def precond(factor, queries):
    depth, width = factor.shape
    count = queries.shape[0]
    steps = 2
    piece = width // steps
    return pl.pallas_call(
        functools.partial(precond_body, steps),
        grid=(steps,),
        in_specs=[
            pl.BlockSpec((depth, piece), lambda i: (0, i)),
            pl.BlockSpec((count, piece), lambda i: (0, i)),
        ],
        out_specs=pl.BlockSpec((depth, count), lambda i: (0, 0)),
        out_shape=jax.ShapeDtypeStruct((depth, count), F32),
        scratch_shapes=[pltpu.VMEM((depth, count), F32)],
        name="precond",
    )(factor, queries)


def row_body(features_ref, cols_ref, give_ref, keep_ref):
    core = lax.axis_index("feat") % 2
    size = give_ref.shape[0]
    cols = cols_ref[...]
    for part, out_ref in ((1 - core, give_ref), (core, keep_ref)):
        rows = features_ref[span(part * size, size), :]
        out_ref[...] = jnp.dot(rows, cols, preferred_element_type=F32).astype(out_ref.dtype)


def gram_body(features_ref, mine_ref, other_ref, out_ref):
    core = lax.axis_index("feat") % 2
    size = mine_ref.shape[0]
    piece = 512
    mine, other = mine_ref[...].T, other_ref[...].T
    for i in range(out_ref.shape[0] // piece):
        cols = slice(i * piece, (i + 1) * piece)
        total = jnp.dot(
            mine, features_ref[span(core * size, size), cols], preferred_element_type=F32
        ) + jnp.dot(
            other, features_ref[span((1 - core) * size, size), cols], preferred_element_type=F32
        )
        out_ref[cols, :] = total.T.astype(out_ref.dtype)


def residual_body(total_rows, block_ref, parts_ref, out_ref):
    gram = jnp.sum(parts_ref[...].astype(F32), axis=0)
    residual = (gram / total_rows + 0.1 * block_ref[...]).astype(out_ref.dtype)
    out_ref[...] = jnp.broadcast_to(residual[None], out_ref.shape)


def product_body(factor_ref, cols_ref, give_ref, keep_ref):
    size = give_ref.shape[0]
    product = jnp.dot(factor_ref[...], cols_ref[...], preferred_element_type=F32)
    give_ref[...] = product[:size]
    keep_ref[...] = product[size:]


def score_body(features_ref, cols_ref, give_ref, keep_ref):
    place = lax.axis_index("feat")
    chip, core = place // 2, place % 2
    size = give_ref.shape[0] // 2
    cols = cols_ref[...]
    for whose, out_ref in ((1 - core, give_ref), (core, keep_ref)):
        for i, where in enumerate((1 - chip, chip)):
            rows = features_ref[span((where * 2 + whose) * size, size), :]
            product = jnp.dot(rows, cols, preferred_element_type=F32)
            out_ref[i * size : (i + 1) * size, :] = product.astype(out_ref.dtype)


def own_columns(factor, cols):
    place = lax.axis_index("feat")
    chip, core = place // 2, place % 2
    depth = factor.shape[0]
    by_core = factor.reshape(depth, 2, 2, cols)
    give = lax.dynamic_index_in_dim(by_core, 1 - core, 2, keepdims=False)
    keep = lax.dynamic_index_in_dim(by_core, core, 2, keepdims=False)
    both = jnp.stack([swap_core(give), keep])
    give = lax.dynamic_index_in_dim(both, 1 - chip, 2, keepdims=False)
    keep = lax.dynamic_index_in_dim(both, chip, 2, keepdims=False)
    whole = jnp.stack([swap_chip(give), keep], 1)
    return whole.reshape(4 * depth, cols)


def on_device(features, queries, inverse_factor):
    factor = inverse_factor[0]
    width = lax.axis_size("wide")
    row_count, cols = features.shape
    depth = factor.shape[0]
    count = queries.shape[0]
    total_rows = row_count * width

    query_block = precond(factor, queries)
    query_cols = exchange_wide(jnp.tile(query_block.astype(BF16), (width, 1)))
    factor_cols = own_columns(factor, cols)

    half = (row_count // 2, count)
    give, keep = local_call(row_body, (features, query_cols), [(half, BF16), (half, F32)], "rows")
    chip_sum = (keep + swap_core(give).astype(F32)).astype(BF16)
    mine = (chip_sum.astype(F32) + swap_chip(chip_sum).astype(F32)).astype(BF16)
    other = swap_core(mine)

    (gram_part,) = local_call(gram_body, (features, mine, other), [((cols, count), BF16)], "gram")
    gram_parts = exchange_wide(gram_part).reshape(width, depth, count)
    (residual,) = local_call(
        functools.partial(residual_body, total_rows),
        (query_block, gram_parts),
        [((width, depth, count), BF16)],
        "residual",
    )
    residual_cols = exchange_wide(residual.reshape(cols, count))

    part = (2 * depth, count)
    give, keep = local_call(
        product_body, (factor_cols, residual_cols), [(part, F32), (part, F32)], "product"
    )
    product = keep + swap_core(give)
    product = product[depth:] + swap_chip(product[:depth])
    corrected = (2.0 * query_block - product).astype(BF16)
    corrected_cols = exchange_wide(jnp.tile(corrected, (width, 1)))

    give, keep = local_call(
        score_body, (features, corrected_cols), [(half, BF16), (half, F32)], "scores"
    )
    scores = keep + swap_core(give).astype(F32)
    quarter = row_count // 4
    return scores[quarter:] + swap_chip(scores[:quarter].astype(BF16)).astype(F32)


def solution(mesh):
    in_specs = (P("wide", "feat"), P(), P("feat", "wide", None))
    out_specs = P(("wide", "feat"), None)
    return jax.shard_map(
        on_device, mesh=mesh, in_specs=in_specs, out_specs=out_specs, check_vma=False
    )
```

time: 917 us -> 154 us (0.17)
  blocking collectives: 460 us -> 54.3 us
  waiting for transfers between devices: 414 us -> 45 us
  starting transfers between devices: 0.09 us -> 32.3 us
  matrix products: 25.3 us -> 0 us
  between operations: 13.1 us -> 0.18 us
  Pallas kernels: 0 us -> 10.8 us
    all_gather x3 -> x0, blocking collectives: 401 us -> none  [the longest x1 136 us: on_device(): residual_feat = lax.all_gather(residual_block, 'wide', axis=0, tiled=True)]
    reduce_scatter x2 -> x0, waiting for transfers between devices: 311 us -> none  [the longest x1 257 us: on_device(): lax.psum_scatter(jnp.einsum('nk,nm->km', features, row_weights, preferred...]
    all_gather x1 -> x0, waiting for transfers between devices: 103 us -> none  [on_device(): residual_whole = lax.all_gather(residual_feat, 'feat', axis=0, tiled=True)]
    psum x1 -> x0, blocking collectives: 58.7 us -> none  [on_device(): row_weights = lax.psum(partial_rows, 'feat').astype(jnp.bfloat16)]
    all_to_all x0 -> x2, blocking collectives: none -> 54.3 us  [exchange_wide(): return lax.all_to_all(blocks, 'wide', 0, 0, tiled=True)]
    ppermute x0 -> x9, waiting for transfers between devices: none -> 28.1 us  [the longest x4 22.9 us: swap_chip(): return lax.ppermute(block, 'feat', CHIP_SWAP)]
    dot_general x5 -> x0, matrix products: 25.3 us -> none  [the longest x1 7.94 us: on_device(): jnp.einsum('nk,nm->km', features, row_weights, preferred_element_type=jnp...]
    ppermute x0 -> x9, starting transfers between devices: none -> 21.8 us  [the longest x5 11.4 us: swap_core(): return lax.ppermute(block, 'feat', CORE_SWAP)]
  transfers between devices with their start and end apart: 3 -> 11, of which waited for: 3 -> 10; matrix products, arithmetic and copies ran while one was open for 0% -> 1% of each run, Pallas kernels for 0% -> 0%
where the time goes in v2:
time: 154 us; the launch traced here: 153 us
  blocking collectives  54.3 us (35%)
  waiting for transfers between devices  45 us (29%)
  starting transfers between devices  32.3 us (21%)
  Pallas kernels  10.8 us (7%)
  local copies, waits for them, and re-layouts  9 us (6%)
  other arithmetic  1.73 us (1%)
    all_to_all x2, blocking collectives, exchange_wide(): return lax.all_to_all(blocks, 'wide', 0, 0, tiled=True)  54.3 us
    ppermute x4, waiting for transfers between devices, swap_chip(): return lax.ppermute(block, 'feat', CHIP_SWAP)  22.9 us
    all_to_all x2, waiting for transfers between devices, exchange_wide(): return lax.all_to_all(blocks, 'wide', 0, 0, tiled=True)  16.9 us
    ppermute x5, starting transfers between devices, swap_core(): return lax.ppermute(block, 'feat', CORE_SWAP)  11.4 us
    all_to_all x2, starting transfers between devices, exchange_wide(): return lax.all_to_all(blocks, 'wide', 0, 0, tiled=True)  10.5 us
    ppermute x4, starting transfers between devices, swap_chip(): return lax.ppermute(block, 'feat', CHIP_SWAP)  10.4 us
    pallas_call x5, Pallas kernels, local_call(): pl.pallas_call(body, in_specs=[IN_VMEM] * len(operands), out_specs=[IN_VM...  7.99 us
    unnamed x8, local copies, waits for them, and re-layouts  6.78 us
  transfers between devices with their start and end apart: 11, of which 10 were waited for; matrix products, arithmetic and copies ran while one was open for 1% of the time, Pallas kernels for 0%

profile of v2, /device:TPU:1, one launch (start us, length us, event | category | flops | bytes accessed | tf_op | source)
XLA Modules:
  0.0 153.4 jit_solution(8268363297555699855)
XLA Ops:
  0.0 2.9 %precond.1.block_ref = f32[32,128]{1,0:T(8,128)} custom-call(bf16[32,8192]{1,0:T(8,128)(2,1)} %bitcast.22, bf16[128,8192]{1,0:T(8,128)(2,1)} %queries_ref.1), custom_call_target="tpu_custom_call" | custom-call | tf_op jit(solution)/shard_map/precond/pallas_call | solution.py:63
  3.6 30.1 %all_to_all.33 = bf16[64,32,128]{2,1,0:T(8,128)(2,1)S(1)} all-to-all(bf16[64,32,128]{2,1,0:T(8,128)(2,1)S(1)} %tile.4), channel_id=1, replica_groups=mesh['wide'=64,'feat'=4] {'wide'}, dimensions={0} | all-to-all | bytes 1048576 | tf_op jit(solution)/shard_map/all_to_all | solution.py:24
  33.8 3.4 %copy-done = bf16[2048,2048]{1,0:T(8,128)(2,1)S(1)} copy-done((bf16[2048,2048]{1,0:T(8,128)(2,1)S(1)}, bf16[2048,2048]{1,0:T(8,128)(2,1)}, u32[]{:S(2)}) %copy-start) | copy-done | bytes 8388632
  37.1 2.3 %rows.1 = (bf16[1024,128]{1,0:T(8,128)(2,1)S(1)}, f32[1024,128]{1,0:T(8,128)S(1)}) custom-call(bf16[2048,2048]{1,0:T(8,128)(2,1)S(1)} %copy-done, bf16[2048,128]{1,0:T(8,128)(2,1)S(1)} %bitcast.18), custom_call_target="tpu_custom_call" | custom-call | tf_op jit(solution)/shard_map/rows/pallas_call | solution.py:28
  39.5 3.0 %collective-permute-start.2 = (bf16[1024,128]{1,0:T(8,128)(2,1)S(1)}, bf16[1024,128]{1,0:T(8,128)(2,1)S(1)}, u32[]{:S(2)}, u32[]{:S(2)}) collective-permute-start(bf16[1024,128]{1,0:T(8,128)(2,1)S(1)} %get-tuple-element.12), channel_id=1, source_target_pairs={{0,1},{1,0},{2,3},{3,2},{4,5},{5,4},{6,7},{7,6},{8,9},{9,8},{10,11... | collective-permute-start | bytes 786440 | tf_op jit(solution)/shard_map/ppermute | solution.py:16
  42.5 1.2 collective-permute-done.2
  43.7 2.7 %collective-permute-start.3 = (bf16[1024,128]{1,0:T(8,128)(2,1)S(1)}, bf16[1024,128]{1,0:T(8,128)(2,1)S(1)}, u32[]{:S(2)}, u32[]{:S(2)}) collective-permute-start(bf16[1024,128]{1,0:T(8,128)(2,1)S(1)} %add_convert_fusion.1), channel_id=1, source_target_pairs={{0,2},{2,0},{1,3},{3,1},{4,6},{6,4},{5,7},{7,5},{8,10},{10,8},{9,1... | collective-permute-start | bytes 786440 | tf_op jit(solution)/shard_map/ppermute | solution.py:20
  46.4 6.4 %collective-permute-done.3 = bf16[1024,128]{1,0:T(8,128)(2,1)S(1)} collective-permute-done((bf16[1024,128]{1,0:T(8,128)(2,1)S(1)}, bf16[1024,128]{1,0:T(8,128)(2,1)S(1)}, u32[]{:S(2)}, u32[]{:S(2)}) %collective-permute-start.3) | collective-permute-done | bytes 262176 | tf_op jit(solution)/shard_map/ppermute | solution.py:20
  52.9 1.3 collective-permute-start.4
  54.2 1.2 collective-permute-done.4.other_ref
  55.3 2.2 %gram.1 = bf16[2048,128]{1,0:T(8,128)(2,1)} custom-call(bf16[2048,2048]{1,0:T(8,128)(2,1)S(1)} %copy-done, bf16[1024,128]{1,0:T(8,128)(2,1)S(1)} %add_convert_fusion.mine_ref, bf16[1024,128]{1,0:T(8,128)(2,1)S(1)} %collective-permute-done.4.other_ref), custom_call_target="tpu_custom_call" | custom-call | tf_op jit(solution)/shard_map/gram/pallas_call | solution.py:28
  57.5 4.7 %all-to-all-start.1 = ((bf16[64,32,128]{2,1,0:T(8,128)(2,1)}), bf16[64,32,128]{2,1,0:T(8,128)(2,1)S(1)}, u32[]{:S(2)}, u32[]{:S(2)}) async-start(bf16[64,32,128]{2,1,0:T(8,128)(2,1)} %bitcast.9), calls=%async_computation.1 | async-start | bytes 1048576 | tf_op jit(solution)/shard_map/all_to_all | solution.py:24
  62.6 16.9 %all-to-all-done.1.parts_ref = bf16[64,32,128]{2,1,0:T(8,128)(2,1)S(1)} async-done(((bf16[64,32,128]{2,1,0:T(8,128)(2,1)}), bf16[64,32,128]{2,1,0:T(8,128)(2,1)S(1)}, u32[]{:S(2)}, u32[]{:S(2)}) %all-to-all-start.1) | async-done | bytes 524320 | tf_op jit(solution)/shard_map/all_to_all | solution.py:24
  79.5 0.9 residual.1
  80.5 5.8 %all-to-all-start.2 = ((bf16[64,32,128]{2,1,0:T(8,128)(2,1)}), bf16[64,32,128]{2,1,0:T(8,128)(2,1)S(1)}, u32[]{:S(2)}, u32[]{:S(2)}) async-start(bf16[64,32,128]{2,1,0:T(8,128)(2,1)} %residual.1), calls=%async_computation.2 | async-start | bytes 1048576 | tf_op jit(solution)/shard_map/all_to_all | solution.py:24
  86.2 1.1 constant_dynamic-slice_fusion
  87.7 1.7 %collective-permute-start = (bf16[32,2,2048]{2,0,1:T(8,128)(2,1)S(1)}, bf16[32,2,2048]{2,0,1:T(8,128)(2,1)S(1)}, u32[]{:S(2)}, u32[]{:S(2)}) collective-permute-start(bf16[32,2,2048]{2,0,1:T(8,128)(2,1)S(1)} %bitcast.25), channel_id=1, source_target_pairs={{0,1},{1,0},{2,3},{3,2},{4,5},{5,4},{6,7},{7,6},{8,9},{9,8},{10,11... | collective-permute-start | bytes 786440 | tf_op jit(solution)/shard_map/ppermute | solution.py:16
  89.6 0.9 collective-permute-done
  90.5 2.7 %collective-permute-start.1 = (bf16[2,32,2048]{2,1,0:T(8,128)(2,1)S(1)}, bf16[2,32,2048]{2,1,0:T(8,128)(2,1)S(1)}, u32[]{:S(2)}, u32[]{:S(2)}) collective-permute-start(bf16[2,32,2048]{2,1,0:T(8,128)(2,1)S(1)} %get-tuple-element.17), channel_id=1, source_target_pairs={{0,2},{2,0},{1,3},{3,1},{4,6},{6,4},{5,7},{7,5},{8,10},{10,8},{9,1... | collective-permute-start | bytes 786440 | tf_op jit(solution)/shard_map/ppermute | solution.py:20
  93.2 11.1 %collective-permute-done.1 = bf16[2,32,2048]{2,1,0:T(8,128)(2,1)S(1)} collective-permute-done((bf16[2,32,2048]{2,1,0:T(8,128)(2,1)S(1)}, bf16[2,32,2048]{2,1,0:T(8,128)(2,1)S(1)}, u32[]{:S(2)}, u32[]{:S(2)}) %collective-permute-start.1) | collective-permute-done | bytes 262176 | tf_op jit(solution)/shard_map/ppermute | solution.py:20
  104.6 1.9 %collective-permute-start.5 = (f32[64,128]{1,0:T(8,128)S(1)}, f32[64,128]{1,0:T(8,128)S(1)}, u32[]{:S(2)}, u32[]{:S(2)}) collective-permute-start(f32[64,128]{1,0:T(8,128)S(1)} %get-tuple-element.14), channel_id=1, source_target_pairs={{0,1},{1,0},{2,3},{3,2},{4,5},{5,4},{6,7},{7,6},{8,9},{9,8},{10,11... | collective-permute-start | bytes 98312 | tf_op jit(solution)/shard_map/ppermute | solution.py:16
  106.5 0.9 collective-permute-done.5
  107.4 2.7 %collective-permute-start.6 = (f32[32,128]{1,0:T(8,128)S(1)}, f32[32,128]{1,0:T(8,128)S(1)}, u32[]{:S(2)}, u32[]{:S(2)}) collective-permute-start(f32[32,128]{1,0:T(8,128)S(1)} %slice.18), channel_id=1, source_target_pairs={{0,2},{2,0},{1,3},{3,1},{4,6},{6,4},{5,7},{7,5},{8,10},{10,8},{9,1... | collective-permute-start | bytes 49160 | tf_op jit(solution)/shard_map/ppermute | solution.py:20
  110.1 1.5 collective-permute-done.6
  111.6 24.2 %all_to_all.34 = bf16[64,32,128]{2,1,0:T(8,128)(2,1)S(1)} all-to-all(bf16[64,32,128]{2,1,0:T(8,128)(2,1)S(1)} %tile.5), channel_id=1, replica_groups=mesh['wide'=64,'feat'=4] {'wide'}, dimensions={0} | all-to-all | bytes 1048576 | tf_op jit(solution)/shard_map/all_to_all | solution.py:24
  135.8 3.4 %copy-done.1 = bf16[2048,2048]{1,0:T(8,128)(2,1)S(1)} copy-done((bf16[2048,2048]{1,0:T(8,128)(2,1)S(1)}, bf16[2048,2048]{1,0:T(8,128)(2,1)}, u32[]{:S(2)}) %copy-start.1) | copy-done | bytes 8388632
  139.2 2.3 %scores.1 = (bf16[1024,128]{1,0:T(8,128)(2,1)S(1)}, f32[1024,128]{1,0:T(8,128)S(1)}) custom-call(bf16[2048,2048]{1,0:T(8,128)(2,1)S(1)} %copy-done.1, bf16[2048,128]{1,0:T(8,128)(2,1)S(1)} %bitcast.19), custom_call_target="tpu_custom_call" | custom-call | tf_op jit(solution)/shard_map/scores/pallas_call | solution.py:28
  141.5 3.6 %collective-permute-start.7 = (bf16[1024,128]{1,0:T(8,128)(2,1)S(1)}, bf16[1024,128]{1,0:T(8,128)(2,1)S(1)}, u32[]{:S(2)}, u32[]{:S(2)}) collective-permute-start(bf16[1024,128]{1,0:T(8,128)(2,1)S(1)} %get-tuple-element.16), channel_id=1, source_target_pairs={{0,1},{1,0},{2,3},{3,2},{4,5},{5,4},{6,7},{7,6},{8,9},{9,8},{10,11... | collective-permute-start | bytes 786440 | tf_op jit(solution)/shard_map/ppermute | solution.py:16
  145.1 1.2 collective-permute-done.7
  146.3 2.3 %collective-permute-start.8 = (bf16[512,128]{1,0:T(8,128)(2,1)S(1)}, bf16[512,128]{1,0:T(8,128)(2,1)S(1)}, u32[]{:S(2)}, u32[]{:S(2)}) collective-permute-start(bf16[512,128]{1,0:T(8,128)(2,1)S(1)} %slice.28), channel_id=1, source_target_pairs={{0,2},{2,0},{1,3},{3,1},{4,6},{6,4},{5,7},{7,5},{8,10},{10,8},{9,1... | collective-permute-start | bytes 393224 | tf_op jit(solution)/shard_map/ppermute | solution.py:20
  148.7 4.0 %collective-permute-done.8 = bf16[512,128]{1,0:T(8,128)(2,1)S(1)} collective-permute-done((bf16[512,128]{1,0:T(8,128)(2,1)S(1)}, bf16[512,128]{1,0:T(8,128)(2,1)S(1)}, u32[]{:S(2)}, u32[]{:S(2)}) %collective-permute-start.8) | collective-permute-done | bytes 131104 | tf_op jit(solution)/shard_map/ppermute | solution.py:20
  152.6 0.7 slice_add_fusion
  (23 shorter events, 2.4 us)
Async XLA Ops:
  33.8 3.4 %copy-start = (bf16[2048,2048]{1,0:T(8,128)(2,1)S(1)}, bf16[2048,2048]{1,0:T(8,128)(2,1)}, u32[]{:S(2)}) copy-start(bf16[2048,2048]{1,0:T(8,128)(2,1)} %features_ref.5) | copy-start | bytes 25165828
  39.5 22.7 %copy-start.3 = (bf16[1,32,8192]{2,1,0:T(8,128)(2,1)S(1)}, bf16[1,32,8192]{2,1,0:T(8,128)(2,1)}, u32[]{:S(2)}) copy-start(bf16[1,32,8192]{2,1,0:T(8,128)(2,1)} %param.5) | copy-start | bytes 1572868
  39.5 40.1 %copy-start.2 = (f32[32,128]{1,0:T(8,128)S(1)}, f32[32,128]{1,0:T(8,128)}, u32[]{:S(2)}) copy-start(f32[32,128]{1,0:T(8,128)} %precond.1.block_ref) | copy-start | bytes 49156
  39.5 4.1 %collective-permute-start.2 = (bf16[1024,128]{1,0:T(8,128)(2,1)S(1)}, bf16[1024,128]{1,0:T(8,128)(2,1)S(1)}, u32[]{:S(2)}, u32[]{:S(2)}) collective-permute-start(bf16[1024,128]{1,0:T(8,128)(2,1)S(1)} %get-tuple-element.12), channel_id=1, source_target_pairs={{0,1},{1,0},{2,3},{3,2},{4,5},{5,4},{6,7},{7,6},{8,9},{9,8},{10,11... | collective-permute-start | bytes 786440 | tf_op jit(solution)/shard_map/ppermute | solution.py:16
  43.7 9.1 %collective-permute-start.3 = (bf16[1024,128]{1,0:T(8,128)(2,1)S(1)}, bf16[1024,128]{1,0:T(8,128)(2,1)S(1)}, u32[]{:S(2)}, u32[]{:S(2)}) collective-permute-start(bf16[1024,128]{1,0:T(8,128)(2,1)S(1)} %add_convert_fusion.1), channel_id=1, source_target_pairs={{0,2},{2,0},{1,3},{3,1},{4,6},{6,4},{5,7},{7,5},{8,10},{10,8},{9,1... | collective-permute-start | bytes 786440 | tf_op jit(solution)/shard_map/ppermute | solution.py:20
  52.9 2.5 %collective-permute-start.4 = (bf16[1024,128]{1,0:T(8,128)(2,1)S(1)}, bf16[1024,128]{1,0:T(8,128)(2,1)S(1)}, u32[]{:S(2)}, u32[]{:S(2)}) collective-permute-start(bf16[1024,128]{1,0:T(8,128)(2,1)S(1)} %add_convert_fusion.mine_ref), channel_id=1, source_target_pairs={{0,1},{1,0},{2,3},{3,2},{4,5},{5,4},{6,7},{7,6},{8,9},{9,8},{10,11... | collective-permute-start | bytes 786440 | tf_op jit(solution)/shard_map/ppermute | solution.py:16
  57.5 22.0 %all-to-all-start.1 = ((bf16[64,32,128]{2,1,0:T(8,128)(2,1)}), bf16[64,32,128]{2,1,0:T(8,128)(2,1)S(1)}, u32[]{:S(2)}, u32[]{:S(2)}) async-start(bf16[64,32,128]{2,1,0:T(8,128)(2,1)} %bitcast.9), calls=%async_computation.1 | async-start | bytes 1048576 | tf_op jit(solution)/shard_map/all_to_all | solution.py:24
  80.5 23.9 %all-to-all-start.2 = ((bf16[64,32,128]{2,1,0:T(8,128)(2,1)}), bf16[64,32,128]{2,1,0:T(8,128)(2,1)S(1)}, u32[]{:S(2)}, u32[]{:S(2)}) async-start(bf16[64,32,128]{2,1,0:T(8,128)(2,1)} %residual.1), calls=%async_computation.2 | async-start | bytes 1048576 | tf_op jit(solution)/shard_map/all_to_all | solution.py:24
  87.7 2.8 %collective-permute-start = (bf16[32,2,2048]{2,0,1:T(8,128)(2,1)S(1)}, bf16[32,2,2048]{2,0,1:T(8,128)(2,1)S(1)}, u32[]{:S(2)}, u32[]{:S(2)}) collective-permute-start(bf16[32,2,2048]{2,0,1:T(8,128)(2,1)S(1)} %bitcast.25), channel_id=1, source_target_pairs={{0,1},{1,0},{2,3},{3,2},{4,5},{5,4},{6,7},{7,6},{8,9},{9,8},{10,11... | collective-permute-start | bytes 786440 | tf_op jit(solution)/shard_map/ppermute | solution.py:16
  90.5 13.8 %collective-permute-start.1 = (bf16[2,32,2048]{2,1,0:T(8,128)(2,1)S(1)}, bf16[2,32,2048]{2,1,0:T(8,128)(2,1)S(1)}, u32[]{:S(2)}, u32[]{:S(2)}) collective-permute-start(bf16[2,32,2048]{2,1,0:T(8,128)(2,1)S(1)} %get-tuple-element.17), channel_id=1, source_target_pairs={{0,2},{2,0},{1,3},{3,1},{4,6},{6,4},{5,7},{7,5},{8,10},{10,8},{9,1... | collective-permute-start | bytes 786440 | tf_op jit(solution)/shard_map/ppermute | solution.py:20
  104.6 2.7 %collective-permute-start.5 = (f32[64,128]{1,0:T(8,128)S(1)}, f32[64,128]{1,0:T(8,128)S(1)}, u32[]{:S(2)}, u32[]{:S(2)}) collective-permute-start(f32[64,128]{1,0:T(8,128)S(1)} %get-tuple-element.14), channel_id=1, source_target_pairs={{0,1},{1,0},{2,3},{3,2},{4,5},{5,4},{6,7},{7,6},{8,9},{9,8},{10,11... | collective-permute-start | bytes 98312 | tf_op jit(solution)/shard_map/ppermute | solution.py:16
  107.4 4.2 %collective-permute-start.6 = (f32[32,128]{1,0:T(8,128)S(1)}, f32[32,128]{1,0:T(8,128)S(1)}, u32[]{:S(2)}, u32[]{:S(2)}) collective-permute-start(f32[32,128]{1,0:T(8,128)S(1)} %slice.18), channel_id=1, source_target_pairs={{0,2},{2,0},{1,3},{3,1},{4,6},{6,4},{5,7},{7,5},{8,10},{10,8},{9,1... | collective-permute-start | bytes 49160 | tf_op jit(solution)/shard_map/ppermute | solution.py:20
  135.8 3.4 %copy-start.1 = (bf16[2048,2048]{1,0:T(8,128)(2,1)S(1)}, bf16[2048,2048]{1,0:T(8,128)(2,1)}, u32[]{:S(2)}) copy-start(bf16[2048,2048]{1,0:T(8,128)(2,1)} %features_ref.5) | copy-start | bytes 25165828
  141.5 4.7 %collective-permute-start.7 = (bf16[1024,128]{1,0:T(8,128)(2,1)S(1)}, bf16[1024,128]{1,0:T(8,128)(2,1)S(1)}, u32[]{:S(2)}, u32[]{:S(2)}) collective-permute-start(bf16[1024,128]{1,0:T(8,128)(2,1)S(1)} %get-tuple-element.16), channel_id=1, source_target_pairs={{0,1},{1,0},{2,3},{3,2},{4,5},{5,4},{6,7},{7,6},{8,9},{9,8},{10,11... | collective-permute-start | bytes 786440 | tf_op jit(solution)/shard_map/ppermute | solution.py:16
  146.3 6.3 %collective-permute-start.8 = (bf16[512,128]{1,0:T(8,128)(2,1)S(1)}, bf16[512,128]{1,0:T(8,128)(2,1)S(1)}, u32[]{:S(2)}, u32[]{:S(2)}) collective-permute-start(bf16[512,128]{1,0:T(8,128)(2,1)S(1)} %slice.28), channel_id=1, source_target_pairs={{0,2},{2,0},{1,3},{3,1},{4,6},{6,4},{5,7},{7,5},{8,10},{10,8},{9,1... | collective-permute-start | bytes 393224 | tf_op jit(solution)/shard_map/ppermute | solution.py:20

commit v3 on v2

v3 whole, which is shorter than its diff:
```python
import functools
import jax
import jax.numpy as jnp
from jax import lax
from jax.experimental import pallas as pl
from jax.experimental.pallas import tpu as pltpu
from jax.sharding import PartitionSpec as P

CORE_SWAP = [(0, 1), (1, 0), (2, 3), (3, 2)]
CHIP_SWAP = [(0, 2), (2, 0), (1, 3), (3, 1)]
F32, BF16 = jnp.float32, jnp.bfloat16
IN_VMEM = pl.BlockSpec(memory_space=pltpu.VMEM)


def swap_core(block):
    return lax.ppermute(block, "feat", CORE_SWAP)


def swap_chip(block):
    return lax.ppermute(block, "feat", CHIP_SWAP)


def exchange_wide(blocks):
    return lax.all_to_all(blocks, "wide", 0, 0, tiled=True)


def local_call(body, operands, shapes, name, scratch=(), outside=0, limit=8):
    anywhere = pl.BlockSpec(memory_space=pl.ANY)
    return pl.pallas_call(
        body,
        in_specs=[anywhere] * outside + [IN_VMEM] * (len(operands) - outside),
        out_specs=[IN_VMEM] * len(shapes),
        out_shape=[jax.ShapeDtypeStruct(shape, dtype) for shape, dtype in shapes],
        scratch_shapes=list(scratch),
        compiler_params=pltpu.CompilerParams(vmem_limit_bytes=limit << 20),
        name=name,
    )(*operands)


def span(start, size):
    return pl.ds(pl.multiple_of(start, size), size)


def precond_body(
    factor_hbm, queries_hbm, block_ref, tiled_ref, give_ref, keep_ref, factor_ref, queries_ref, sems
):
    place = lax.axis_index("feat")
    chip, core = place // 2, place % 2
    size = give_ref.shape[2]
    steps = 4
    size_q = factor_ref.shape[1] // steps
    factor_copies, query_copies = [], []
    for i in range(steps):
        cols = slice(i * size_q, (i + 1) * size_q)
        factor_copies.append(
            pltpu.make_async_copy(factor_hbm.at[:, cols], factor_ref.at[:, cols], sems.at[0, i])
        )
        query_copies.append(
            pltpu.make_async_copy(queries_hbm.at[:, cols], queries_ref.at[:, cols], sems.at[1, i])
        )
        factor_copies[i].start()
        query_copies[i].start()
    block = jnp.zeros_like(block_ref)
    for j in range(2):
        for i in range(j * steps // 2, (j + 1) * steps // 2):
            factor_copies[i].wait()
            query_copies[i].wait()
        piece = factor_ref.shape[1] // 2
        cols = slice(j * piece, (j + 1) * piece)
        block += lax.dot_general(
            factor_ref[:, cols],
            queries_ref[:, cols],
            (((1,), (1,)), ((), ())),
            preferred_element_type=F32,
        )
    for whose, out_ref in ((1 - core, give_ref), (core, keep_ref)):
        for i, where in enumerate((1 - chip, chip)):
            out_ref[i] = factor_ref[:, span((where * 2 + whose) * size, size)]
    block_ref[...] = block
    tiled_ref[...] = jnp.broadcast_to(block.astype(tiled_ref.dtype)[None], tiled_ref.shape)


def row_body(pieces, features_hbm, cols_ref, give_ref, keep_ref, features_ref, sems):
    core = lax.axis_index("feat") % 2
    half = give_ref.shape[0]
    steps = sems.shape[0]
    size = 2 * half // steps
    first = (1 - core) * half
    cols = cols_ref[...]
    copies = []
    for i in range(steps):
        rows = span(lax.rem(first + i * size, 2 * half), size)
        copies.append(
            pltpu.make_async_copy(features_hbm.at[rows], features_ref.at[rows], sems.at[i])
        )
    ahead = 6
    for copy in copies[:ahead]:
        copy.start()
    size = 2 * half // pieces
    for i in range(pieces):
        for j in range(i * steps // pieces, (i + 1) * steps // pieces):
            copies[j].wait()
            if j + ahead < steps:
                copies[j + ahead].start()
        rows = span(lax.rem(first + i * size, 2 * half), size)
        product = jnp.dot(features_ref[rows, :], cols, preferred_element_type=F32)
        out_ref, j = (give_ref, i) if i < pieces // 2 else (keep_ref, i - pieces // 2)
        out_ref[j * size : (j + 1) * size, :] = product.astype(out_ref.dtype)


def gram_body(features_ref, mine_ref, other_ref, out_ref, rows_ref):
    core = lax.axis_index("feat") % 2
    size = mine_ref.shape[0]
    piece = 512
    rows_ref[span(core * size, size), :] = mine_ref[...]
    rows_ref[span((1 - core) * size, size), :] = other_ref[...]
    rows = rows_ref[...].T
    for i in range(out_ref.shape[0] // piece):
        cols = slice(i * piece, (i + 1) * piece)
        total = jnp.dot(rows, features_ref[:, cols], preferred_element_type=F32)
        out_ref[cols, :] = total.T.astype(out_ref.dtype)


def residual_body(total_rows, block_ref, parts_ref, out_ref):
    gram = jnp.sum(parts_ref[...].astype(F32), axis=0)
    residual = (gram / total_rows + 0.1 * block_ref[...]).astype(out_ref.dtype)
    out_ref[...] = jnp.broadcast_to(residual[None], out_ref.shape)


def product_body(factor_ref, cols_ref, give_ref, keep_ref):
    size = give_ref.shape[0]
    product = jnp.dot(factor_ref[...], cols_ref[...], preferred_element_type=F32)
    give_ref[...] = product[:size]
    keep_ref[...] = product[size:]


def score_body(own, features_ref, cols_ref, give_ref, keep_ref):
    place = lax.axis_index("feat")
    chip, core = place // 2, place % 2
    where = chip if own else 1 - chip
    size = give_ref.shape[0]
    cols = cols_ref[...]
    for whose, out_ref in ((1 - core, give_ref), (core, keep_ref)):
        rows = features_ref[span((where * 2 + whose) * size, size), :]
        out_ref[...] = jnp.dot(rows, cols, preferred_element_type=F32).astype(out_ref.dtype)


def on_device(features, queries, inverse_factor):
    factor = inverse_factor[0]
    width = lax.axis_size("wide")
    row_count, cols = features.shape
    depth = factor.shape[0]
    count = queries.shape[0]
    total_rows = row_count * width

    query_block, tiled, give, keep = local_call(
        precond_body,
        (factor, queries),
        [((depth, count), F32), ((width, depth, count), BF16)] + [((2, depth, cols), BF16)] * 2,
        "precond",
        [
            pltpu.VMEM(factor.shape, BF16),
            pltpu.VMEM(queries.shape, BF16),
            pltpu.SemaphoreType.DMA((2, 4)),
        ],
        outside=2,
        limit=53,
        )
    query_cols = exchange_wide(tiled.reshape(cols, count))
    got = swap_core(give)
    far = swap_chip(jnp.stack([got[0], keep[0]]))
    factor_cols = jnp.stack([far[0], got[1], far[1], keep[1]]).reshape(4 * depth, cols)
    query_cols, factor_cols = lax.optimization_barrier((query_cols, factor_cols))

    half = (row_count // 2, count)
    give, keep, held = local_call(
        functools.partial(row_body, 8),
        (features, query_cols),
        [(half, BF16), (half, F32), (features.shape, BF16)],
        "rows",
        [pltpu.SemaphoreType.DMA((16,))],
        outside=1,
        limit=43,
    )
    chip_sum = (keep + swap_core(give).astype(F32)).astype(BF16)
    mine = (chip_sum.astype(F32) + swap_chip(chip_sum).astype(F32)).astype(BF16)
    other = swap_core(mine)

    (gram_part,) = local_call(
        gram_body,
        (held, mine, other),
        [((cols, count), BF16)],
        "gram",
        [pltpu.VMEM((row_count, count), BF16)],
    )
    gram_parts = exchange_wide(gram_part).reshape(width, depth, count)
    (residual,) = local_call(
        functools.partial(residual_body, total_rows),
        (query_block, gram_parts),
        [((width, depth, count), BF16)],
        "residual",
    )
    residual_cols = exchange_wide(residual.reshape(cols, count))

    part = (2 * depth, count)
    give, keep = local_call(
        product_body, (factor_cols, residual_cols), [(part, F32), (part, F32)], "product"
    )
    product = keep + swap_core(give)
    product = product[depth:] + swap_chip(product[:depth])
    corrected = (2.0 * query_block - product).astype(BF16)
    corrected_cols = exchange_wide(jnp.tile(corrected, (width, 1)))

    quarter = (row_count // 4, count)
    sums = []
    for own in (False, True):
        give, keep = local_call(
            functools.partial(score_body, own),
            (held, corrected_cols),
            [(quarter, BF16), (quarter, F32)],
            "own_scores" if own else "far_scores",
        )
        sums.append(keep + swap_core(give).astype(F32))
    return sums[1] + swap_chip(sums[0].astype(BF16)).astype(F32)


def solution(mesh):
    in_specs = (P("wide", "feat"), P(), P("feat", "wide", None))
    out_specs = P(("wide", "feat"), None)
    return jax.shard_map(
        on_device, mesh=mesh, in_specs=in_specs, out_specs=out_specs, check_vma=False
    )
```

time: 154 us -> 145 us (0.942)
  waiting for transfers between devices: 45 us -> 28.4 us
  blocking collectives: 54.3 us -> 66.8 us
  local copies, waits for them, and re-layouts: 9 us -> 0.13 us
  starting transfers between devices: 32.3 us -> 36 us
  Pallas kernels: 10.8 us -> 12.6 us
    all_to_all x2 -> x1, waiting for transfers between devices: 16.9 us -> 1.26 us  [exchange_wide(): return lax.all_to_all(blocks, 'wide', 0, 0, tiled=True)]
    all_to_all x2 -> x3, blocking collectives: 54.3 us -> 66.8 us  [exchange_wide(): return lax.all_to_all(blocks, 'wide', 0, 0, tiled=True)]
    unnamed x8 -> x0, local copies, waits for them, and re-layouts: 6.78 us -> none
    all_to_all x2 -> x1, starting transfers between devices: 10.5 us -> 13.5 us  [exchange_wide(): return lax.all_to_all(blocks, 'wide', 0, 0, tiled=True)]
    pallas_call x6 -> x7, Pallas kernels: 10.8 us -> 12.6 us  [local_call(): pl.pallas_call(body, in_specs=[anywhere] * outside + [IN_VMEM] * (len(ope...]
    dynamic_slice x3 -> x0, local copies, waits for them, and re-layouts: 1.69 us -> none  [the longest x2 1.4 us: own_columns(): keep = lax.dynamic_index_in_dim(by_core, core, 2, keepdims=False)]
    ppermute x5 -> x6, starting transfers between devices: 11.4 us -> 12.5 us  [swap_core(): return lax.ppermute(block, 'feat', CORE_SWAP)]
    ppermute x5 -> x6, waiting for transfers between devices: 5.2 us -> 4.33 us  [swap_core(): return lax.ppermute(block, 'feat', CORE_SWAP)]
  transfers between devices with their start and end apart: 11 -> 11, of which waited for: 10 -> 9; matrix products, arithmetic and copies ran while one was open for 1% -> 0% of each run, Pallas kernels for 0% -> 1%
where the time goes in v3:
time: 145 us
  blocking collectives  66.8 us (46%)
  starting transfers between devices  36 us (25%)
  waiting for transfers between devices  28.4 us (20%)
  Pallas kernels  12.6 us (9%)
    all_to_all x3, blocking collectives, exchange_wide(): return lax.all_to_all(blocks, 'wide', 0, 0, tiled=True)  66.8 us
    ppermute x4, waiting for transfers between devices, swap_chip(): return lax.ppermute(block, 'feat', CHIP_SWAP)  22.8 us
    all_to_all x1, starting transfers between devices, exchange_wide(): return lax.all_to_all(blocks, 'wide', 0, 0, tiled=True)  13.5 us
    pallas_call x7, Pallas kernels, local_call(): pl.pallas_call(body, in_specs=[anywhere] * outside + [IN_VMEM] * (len(ope...  12.6 us
    ppermute x6, starting transfers between devices, swap_core(): return lax.ppermute(block, 'feat', CORE_SWAP)  12.5 us
    ppermute x4, starting transfers between devices, swap_chip(): return lax.ppermute(block, 'feat', CHIP_SWAP)  10 us
    ppermute x6, waiting for transfers between devices, swap_core(): return lax.ppermute(block, 'feat', CORE_SWAP)  4.33 us
  transfers between devices with their start and end apart: 11, of which 9 were waited for; matrix products, arithmetic and copies ran while one was open for 0% of the time, Pallas kernels for 1%

profile of v3, /device:TPU:1, one launch (start us, length us, event | category | flops | bytes accessed | tf_op | source)
XLA Modules:
  0.0 145.1 jit_solution(11196397552008365277)
XLA Ops:
  0.0 3.4 %precond.1 = (f32[32,128]{1,0:T(8,128)S(1)}, bf16[64,32,128]{2,1,0:T(8,128)(2,1)}, bf16[2,32,2048]{2,1,0:T(8,128)(2,1)S(1)}, bf16[2,32,2048]{2,1,0:T(8,128)(2,1)S(1)}) custom-call(bf16[32,8192]{1,0:T(8,128)(2,1)} %bitcast.12, bf16[128,8192]{1,0:T(8,128)(2,1)} %queries_hbm.1), custom_call_target="tpu_custom_call" | custom-call | tf_op jit(solution)/shard_map/precond/pallas_call | solution.py:29
  3.4 13.5 %all-to-all-start = ((bf16[64,32,128]{2,1,0:T(8,128)(2,1)}), bf16[64,32,128]{2,1,0:T(8,128)(2,1)S(1)}, u32[]{:S(2)}, u32[]{:S(2)}) async-start(bf16[64,32,128]{2,1,0:T(8,128)(2,1)} %get-tuple-element.20), calls=%async_computation | async-start | bytes 1048576 | tf_op jit(solution)/shard_map/all_to_all | solution.py:24
  17.0 1.0 collective-permute-start
  18.0 1.1 collective-permute-done
  19.2 2.7 %collective-permute-start.1 = (bf16[2,32,2048]{2,1,0:T(8,128)(2,1)S(1)}, bf16[2,32,2048]{2,1,0:T(8,128)(2,1)S(1)}, u32[]{:S(2)}, u32[]{:S(2)}) collective-permute-start(bf16[2,32,2048]{2,1,0:T(8,128)(2,1)S(1)} %pad_maximum_fusion.1), channel_id=1, source_target_pairs={{0,2},{2,0},{1,3},{3,1},{4,6},{6,4},{5,7},{7,5},{8,10},{10,8},{9,1... | collective-permute-start | bytes 786440 | tf_op jit(solution)/shard_map/ppermute | solution.py:20
  21.9 10.5 %collective-permute-done.1 = bf16[2,32,2048]{2,1,0:T(8,128)(2,1)S(1)} collective-permute-done((bf16[2,32,2048]{2,1,0:T(8,128)(2,1)S(1)}, bf16[2,32,2048]{2,1,0:T(8,128)(2,1)S(1)}, u32[]{:S(2)}, u32[]{:S(2)}) %collective-permute-start.1) | collective-permute-done | bytes 262176 | tf_op jit(solution)/shard_map/ppermute | solution.py:20
  32.5 1.3 all-to-all-done
  33.8 4.9 %rows.1 = (bf16[1024,128]{1,0:T(8,128)(2,1)S(1)}, f32[1024,128]{1,0:T(8,128)S(1)}, bf16[2048,2048]{1,0:T(8,128)(2,1)S(1)}) custom-call(bf16[2048,2048]{1,0:T(8,128)(2,1)} %features_hbm.1, bf16[2048,128]{1,0:T(8,128)(2,1)S(1)} %bitcast.8), custom_call_target="tpu_custom_call" | custom-call | tf_op jit(solution)/shard_map/rows/pallas_call | solution.py:29
  38.7 3.0 %collective-permute-start.2 = (bf16[1024,128]{1,0:T(8,128)(2,1)S(1)}, bf16[1024,128]{1,0:T(8,128)(2,1)S(1)}, u32[]{:S(2)}, u32[]{:S(2)}) collective-permute-start(bf16[1024,128]{1,0:T(8,128)(2,1)S(1)} %get-tuple-element.28), channel_id=1, source_target_pairs={{0,1},{1,0},{2,3},{3,2},{4,5},{5,4},{6,7},{7,6},{8,9},{9,8},{10,11... | collective-permute-start | bytes 786440 | tf_op jit(solution)/shard_map/ppermute | solution.py:16
  41.6 1.2 collective-permute-done.2
  42.9 2.7 %collective-permute-start.3 = (bf16[1024,128]{1,0:T(8,128)(2,1)S(1)}, bf16[1024,128]{1,0:T(8,128)(2,1)S(1)}, u32[]{:S(2)}, u32[]{:S(2)}) collective-permute-start(bf16[1024,128]{1,0:T(8,128)(2,1)S(1)} %add_convert_fusion.1), channel_id=1, source_target_pairs={{0,2},{2,0},{1,3},{3,1},{4,6},{6,4},{5,7},{7,5},{8,10},{10,8},{9,1... | collective-permute-start | bytes 786440 | tf_op jit(solution)/shard_map/ppermute | solution.py:20
  45.6 6.4 %collective-permute-done.3 = bf16[1024,128]{1,0:T(8,128)(2,1)S(1)} collective-permute-done((bf16[1024,128]{1,0:T(8,128)(2,1)S(1)}, bf16[1024,128]{1,0:T(8,128)(2,1)S(1)}, u32[]{:S(2)}, u32[]{:S(2)}) %collective-permute-start.3) | collective-permute-done | bytes 262176 | tf_op jit(solution)/shard_map/ppermute | solution.py:20
  52.0 0.1 add_convert_fusion.mine_ref
  52.0 1.3 collective-permute-start.4
  53.3 1.2 collective-permute-done.4.other_ref
  54.5 1.4 gram.1
  55.9 24.3 %all_to_all.34.parts_ref = bf16[64,32,128]{2,1,0:T(8,128)(2,1)S(1)} all-to-all(bf16[64,32,128]{2,1,0:T(8,128)(2,1)S(1)} %bitcast.9), channel_id=1, replica_groups=mesh['wide'=64,'feat'=4] {'wide'}, dimensions={0} | all-to-all | bytes 1048576 | tf_op jit(solution)/shard_map/all_to_all | solution.py:24
  80.2 0.1 residual.1
  80.3 21.9 %all_to_all.35 = bf16[64,32,128]{2,1,0:T(8,128)(2,1)S(1)} all-to-all(bf16[64,32,128]{2,1,0:T(8,128)(2,1)S(1)} %residual.1), channel_id=1, replica_groups=mesh['wide'=64,'feat'=4] {'wide'}, dimensions={0} | all-to-all | bytes 1048576 | tf_op jit(solution)/shard_map/all_to_all | solution.py:24
  102.2 0.3 product.1
  102.5 3.5 %collective-permute-start.5 = (f32[64,128]{1,0:T(8,128)S(1)}, f32[64,128]{1,0:T(8,128)S(1)}, u32[]{:S(2)}, u32[]{:S(2)}) collective-permute-start(f32[64,128]{1,0:T(8,128)S(1)} %get-tuple-element.30), channel_id=1, source_target_pairs={{0,1},{1,0},{2,3},{3,2},{4,5},{5,4},{6,7},{7,6},{8,9},{9,8},{10,11... | collective-permute-start | bytes 98312 | tf_op jit(solution)/shard_map/ppermute | solution.py:16
  106.0 0.9 collective-permute-done.5
  106.8 2.4 %collective-permute-start.6 = (f32[32,128]{1,0:T(8,128)S(1)}, f32[32,128]{1,0:T(8,128)S(1)}, u32[]{:S(2)}, u32[]{:S(2)}) collective-permute-start(f32[32,128]{1,0:T(8,128)S(1)} %slice.37), channel_id=1, source_target_pairs={{0,2},{2,0},{1,3},{3,1},{4,6},{6,4},{5,7},{7,5},{8,10},{10,8},{9,1... | collective-permute-start | bytes 49160 | tf_op jit(solution)/shard_map/ppermute | solution.py:20
  109.2 2.0 %collective-permute-done.6 = f32[32,128]{1,0:T(8,128)S(1)} collective-permute-done((f32[32,128]{1,0:T(8,128)S(1)}, f32[32,128]{1,0:T(8,128)S(1)}, u32[]{:S(2)}, u32[]{:S(2)}) %collective-permute-start.6) | collective-permute-done | bytes 16416 | tf_op jit(solution)/shard_map/ppermute | solution.py:20
  111.3 20.7 %all_to_all.36 = bf16[64,32,128]{2,1,0:T(8,128)(2,1)S(1)} all-to-all(bf16[64,32,128]{2,1,0:T(8,128)(2,1)S(1)} %tile.2), channel_id=1, replica_groups=mesh['wide'=64,'feat'=4] {'wide'}, dimensions={0} | all-to-all | bytes 1048576 | tf_op jit(solution)/shard_map/all_to_all | solution.py:24
  132.0 1.2 far_scores.1
  133.2 3.6 %collective-permute-start.8 = (bf16[512,128]{1,0:T(8,128)(2,1)S(1)}, bf16[512,128]{1,0:T(8,128)(2,1)S(1)}, u32[]{:S(2)}, u32[]{:S(2)}) collective-permute-start(bf16[512,128]{1,0:T(8,128)(2,1)S(1)} %get-tuple-element.34), channel_id=1, source_target_pairs={{0,1},{1,0},{2,3},{3,2},{4,5},{5,4},{6,7},{7,6},{8,9},{9,8},{10,11... | collective-permute-start | bytes 393224 | tf_op jit(solution)/shard_map/ppermute | solution.py:16
  136.8 1.2 own_scores.1
  138.1 0.1 collective-permute-start.7
  138.2 2.2 %collective-permute-start.9 = (bf16[512,128]{1,0:T(8,128)(2,1)S(1)}, bf16[512,128]{1,0:T(8,128)(2,1)S(1)}, u32[]{:S(2)}, u32[]{:S(2)}) collective-permute-start(bf16[512,128]{1,0:T(8,128)(2,1)S(1)} %add_convert_fusion.2), channel_id=1, source_target_pairs={{0,2},{2,0},{1,3},{3,1},{4,6},{6,4},{5,7},{7,5},{8,10},{10,8},{9,1... | collective-permute-start | bytes 393224 | tf_op jit(solution)/shard_map/ppermute | solution.py:20
  140.4 3.9 %collective-permute-done.9 = bf16[512,128]{1,0:T(8,128)(2,1)S(1)} collective-permute-done((bf16[512,128]{1,0:T(8,128)(2,1)S(1)}, bf16[512,128]{1,0:T(8,128)(2,1)S(1)}, u32[]{:S(2)}, u32[]{:S(2)}) %collective-permute-start.9) | collective-permute-done | bytes 131104 | tf_op jit(solution)/shard_map/ppermute | solution.py:20
  144.4 0.7 convert_add_fusion
  (13 shorter events, 0.3 us)
Async XLA Ops:
  3.4 30.3 %all-to-all-start = ((bf16[64,32,128]{2,1,0:T(8,128)(2,1)}), bf16[64,32,128]{2,1,0:T(8,128)(2,1)S(1)}, u32[]{:S(2)}, u32[]{:S(2)}) async-start(bf16[64,32,128]{2,1,0:T(8,128)(2,1)} %get-tuple-element.20), calls=%async_computation | async-start | bytes 1048576 | tf_op jit(solution)/shard_map/all_to_all | solution.py:24
  17.0 2.2 %collective-permute-start = (bf16[2,32,2048]{2,1,0:T(8,128)(2,1)S(1)}, bf16[2,32,2048]{2,1,0:T(8,128)(2,1)S(1)}, u32[]{:S(2)}, u32[]{:S(2)}) collective-permute-start(bf16[2,32,2048]{2,1,0:T(8,128)(2,1)S(1)} %get-tuple-element.21), channel_id=1, source_target_pairs={{0,1},{1,0},{2,3},{3,2},{4,5},{5,4},{6,7},{7,6},{8,9},{9,8},{10,11... | collective-permute-start | bytes 786440 | tf_op jit(solution)/shard_map/ppermute | solution.py:16
  19.2 13.2 %collective-permute-start.1 = (bf16[2,32,2048]{2,1,0:T(8,128)(2,1)S(1)}, bf16[2,32,2048]{2,1,0:T(8,128)(2,1)S(1)}, u32[]{:S(2)}, u32[]{:S(2)}) collective-permute-start(bf16[2,32,2048]{2,1,0:T(8,128)(2,1)S(1)} %pad_maximum_fusion.1), channel_id=1, source_target_pairs={{0,2},{2,0},{1,3},{3,1},{4,6},{6,4},{5,7},{7,5},{8,10},{10,8},{9,1... | collective-permute-start | bytes 786440 | tf_op jit(solution)/shard_map/ppermute | solution.py:20
  38.7 4.1 %collective-permute-start.2 = (bf16[1024,128]{1,0:T(8,128)(2,1)S(1)}, bf16[1024,128]{1,0:T(8,128)(2,1)S(1)}, u32[]{:S(2)}, u32[]{:S(2)}) collective-permute-start(bf16[1024,128]{1,0:T(8,128)(2,1)S(1)} %get-tuple-element.28), channel_id=1, source_target_pairs={{0,1},{1,0},{2,3},{3,2},{4,5},{5,4},{6,7},{7,6},{8,9},{9,8},{10,11... | collective-permute-start | bytes 786440 | tf_op jit(solution)/shard_map/ppermute | solution.py:16
  42.9 9.1 %collective-permute-start.3 = (bf16[1024,128]{1,0:T(8,128)(2,1)S(1)}, bf16[1024,128]{1,0:T(8,128)(2,1)S(1)}, u32[]{:S(2)}, u32[]{:S(2)}) collective-permute-start(bf16[1024,128]{1,0:T(8,128)(2,1)S(1)} %add_convert_fusion.1), channel_id=1, source_target_pairs={{0,2},{2,0},{1,3},{3,1},{4,6},{6,4},{5,7},{7,5},{8,10},{10,8},{9,1... | collective-permute-start | bytes 786440 | tf_op jit(solution)/shard_map/ppermute | solution.py:20
  52.0 2.5 %collective-permute-start.4 = (bf16[1024,128]{1,0:T(8,128)(2,1)S(1)}, bf16[1024,128]{1,0:T(8,128)(2,1)S(1)}, u32[]{:S(2)}, u32[]{:S(2)}) collective-permute-start(bf16[1024,128]{1,0:T(8,128)(2,1)S(1)} %add_convert_fusion.mine_ref), channel_id=1, source_target_pairs={{0,1},{1,0},{2,3},{3,2},{4,5},{5,4},{6,7},{7,6},{8,9},{9,8},{10,11... | collective-permute-start | bytes 786440 | tf_op jit(solution)/shard_map/ppermute | solution.py:16
  102.5 4.4 %collective-permute-start.5 = (f32[64,128]{1,0:T(8,128)S(1)}, f32[64,128]{1,0:T(8,128)S(1)}, u32[]{:S(2)}, u32[]{:S(2)}) collective-permute-start(f32[64,128]{1,0:T(8,128)S(1)} %get-tuple-element.30), channel_id=1, source_target_pairs={{0,1},{1,0},{2,3},{3,2},{4,5},{5,4},{6,7},{7,6},{8,9},{9,8},{10,11... | collective-permute-start | bytes 98312 | tf_op jit(solution)/shard_map/ppermute | solution.py:16
  106.8 4.4 %collective-permute-start.6 = (f32[32,128]{1,0:T(8,128)S(1)}, f32[32,128]{1,0:T(8,128)S(1)}, u32[]{:S(2)}, u32[]{:S(2)}) collective-permute-start(f32[32,128]{1,0:T(8,128)S(1)} %slice.37), channel_id=1, source_target_pairs={{0,2},{2,0},{1,3},{3,1},{4,6},{6,4},{5,7},{7,5},{8,10},{10,8},{9,1... | collective-permute-start | bytes 49160 | tf_op jit(solution)/shard_map/ppermute | solution.py:20
  133.2 4.9 %collective-permute-start.8 = (bf16[512,128]{1,0:T(8,128)(2,1)S(1)}, bf16[512,128]{1,0:T(8,128)(2,1)S(1)}, u32[]{:S(2)}, u32[]{:S(2)}) collective-permute-start(bf16[512,128]{1,0:T(8,128)(2,1)S(1)} %get-tuple-element.34), channel_id=1, source_target_pairs={{0,1},{1,0},{2,3},{3,2},{4,5},{5,4},{6,7},{7,6},{8,9},{9,8},{10,11... | collective-permute-start | bytes 393224 | tf_op jit(solution)/shard_map/ppermute | solution.py:16
  138.1 2.4 %collective-permute-start.7 = (bf16[512,128]{1,0:T(8,128)(2,1)S(1)}, bf16[512,128]{1,0:T(8,128)(2,1)S(1)}, u32[]{:S(2)}, u32[]{:S(2)}) collective-permute-start(bf16[512,128]{1,0:T(8,128)(2,1)S(1)} %get-tuple-element.32), channel_id=1, source_target_pairs={{0,1},{1,0},{2,3},{3,2},{4,5},{5,4},{6,7},{7,6},{8,9},{9,8},{10,11... | collective-permute-start | bytes 393224 | tf_op jit(solution)/shard_map/ppermute | solution.py:16
  138.2 6.2 %collective-permute-start.9 = (bf16[512,128]{1,0:T(8,128)(2,1)S(1)}, bf16[512,128]{1,0:T(8,128)(2,1)S(1)}, u32[]{:S(2)}, u32[]{:S(2)}) collective-permute-start(bf16[512,128]{1,0:T(8,128)(2,1)S(1)} %add_convert_fusion.2), channel_id=1, source_target_pairs={{0,2},{2,0},{1,3},{3,1},{4,6},{6,4},{5,7},{7,5},{8,10},{10,8},{9,1... | collective-permute-start | bytes 393224 | tf_op jit(solution)/shard_map/ppermute | solution.py:20

commit v4 on v3

--- a/solution.py
+++ b/solution.py
@@ -20,8 +20,27 @@
     return lax.ppermute(block, "feat", CHIP_SWAP)
 
 
-def exchange_wide(blocks):
-    return lax.all_to_all(blocks, "wide", 0, 0, tiled=True)
+def swap_side(block):
+    width = lax.axis_size("wide")
+    return lax.ppermute(block, "wide", [(i, (i + width // 2) % width) for i in range(width)])
+
+
+def swap_chip_and_side(block):
+    width = lax.axis_size("wide")
+    pairs = [
+        (i * 4 + j, (i + width // 2) % width * 4 + k) for i in range(width) for j, k in CHIP_SWAP
+    ]
+    return lax.ppermute(block, ("wide", "feat"), pairs)
+
+
+def exchange_side(blocks):
+    half = lax.axis_size("wide") // 2
+    sides = [list(range(half)), list(range(half, 2 * half))]
+    return lax.all_to_all(blocks, "wide", 0, 0, tiled=True, axis_index_groups=sides)
+
+
+def my_side():
+    return lax.axis_index("wide") // (lax.axis_size("wide") // 2)
 
 
 def local_call(body, operands, shapes, name, scratch=(), outside=0, limit=8):
@@ -45,8 +64,8 @@
     factor_hbm, queries_hbm, block_ref, tiled_ref, give_ref, keep_ref, factor_ref, queries_ref, sems
 ):
     place = lax.axis_index("feat")
-    chip, core = place // 2, place % 2
-    size = give_ref.shape[2]
+    chip, core, side = place // 2, place % 2, my_side()
+    size = give_ref.shape[3]
     steps = 4
     size_q = factor_ref.shape[1] // steps
     factor_copies, query_copies = [], []
@@ -74,15 +93,19 @@
             preferred_element_type=F32,
         )
     for whose, out_ref in ((1 - core, give_ref), (core, keep_ref)):
-        for i, where in enumerate((1 - chip, chip)):
-            out_ref[i] = factor_ref[:, span((where * 2 + whose) * size, size)]
+        for i, where in enumerate((chip, 1 - chip)):
+            for j, part in enumerate((side, 1 - side)):
+                start = ((where * 2 + whose) * 2 + part) * size
+                out_ref[i, j] = factor_ref[:, span(start, size)]
     block_ref[...] = block
     tiled_ref[...] = jnp.broadcast_to(block.astype(tiled_ref.dtype)[None], tiled_ref.shape)
 
 
-def row_body(pieces, features_hbm, cols_ref, give_ref, keep_ref, features_ref, sems):
-    core = lax.axis_index("feat") % 2
-    half = give_ref.shape[0]
+def near_row_body(
+    pieces, features_hbm, cols_ref, give_ref, keep_ref, features_ref, sems
+):
+    core, side = lax.axis_index("feat") % 2, my_side()
+    half, depth = give_ref.shape[0], cols_ref.shape[0]
     steps = sems.shape[0]
     size = 2 * half // steps
     first = (1 - core) * half
@@ -103,22 +126,37 @@
             if j + ahead < steps:
                 copies[j + ahead].start()
         rows = span(lax.rem(first + i * size, 2 * half), size)
-        product = jnp.dot(features_ref[rows, :], cols, preferred_element_type=F32)
+        block = features_ref[rows, span(side * depth, depth)]
         out_ref, j = (give_ref, i) if i < pieces // 2 else (keep_ref, i - pieces // 2)
-        out_ref[j * size : (j + 1) * size, :] = product.astype(out_ref.dtype)
-
-
-def gram_body(features_ref, mine_ref, other_ref, out_ref, rows_ref):
+        out_ref[j * size : (j + 1) * size, :] = jnp.dot(block, cols, preferred_element_type=F32)
+
+
+def far_row_body(features_ref, cols_ref, near_give_ref, near_keep_ref, give_ref, keep_ref):
+    core, side = lax.axis_index("feat") % 2, my_side()
+    half, depth = give_ref.shape[0], cols_ref.shape[0]
+    cols = cols_ref[...]
+    for part, near_ref, out_ref in (
+        (1 - core, near_give_ref, give_ref),
+        (core, near_keep_ref, keep_ref),
+    ):
+        block = features_ref[span(part * half, half), span((1 - side) * depth, depth)]
+        product = near_ref[...] + jnp.dot(block, cols, preferred_element_type=F32)
+        out_ref[...] = product.astype(out_ref.dtype)
+
+
+def gram_body(other, features_ref, mine_ref, other_ref, out_ref, rows_ref):
     core = lax.axis_index("feat") % 2
+    side = 1 - my_side() if other else my_side()
     size = mine_ref.shape[0]
     piece = 512
     rows_ref[span(core * size, size), :] = mine_ref[...]
     rows_ref[span((1 - core) * size, size), :] = other_ref[...]
     rows = rows_ref[...].T
-    for i in range(out_ref.shape[0] // piece):
-        cols = slice(i * piece, (i + 1) * piece)
+    depth = out_ref.shape[0]
+    for i in range(depth // piece):
+        cols = span(side * depth + i * piece, piece)
         total = jnp.dot(rows, features_ref[:, cols], preferred_element_type=F32)
-        out_ref[cols, :] = total.T.astype(out_ref.dtype)
+        out_ref[i * piece : (i + 1) * piece, :] = total.T.astype(out_ref.dtype)
 
 
 def residual_body(total_rows, block_ref, parts_ref, out_ref):
@@ -134,14 +172,50 @@
     keep_ref[...] = product[size:]
 
 
-def score_body(own, features_ref, cols_ref, give_ref, keep_ref):
-    place = lax.axis_index("feat")
-    chip, core = place // 2, place % 2
-    where = chip if own else 1 - chip
+def load_body(own, features_hbm, out_ref, sems):
+    chip = lax.axis_index("feat") // 2
+    rows, steps = out_ref.shape[0], sems.shape[0]
+    first, size = (chip if own else 1 - chip) * rows, rows // steps
+    copies = [
+        pltpu.make_async_copy(
+            features_hbm.at[span(first + i * size, size)],
+            out_ref.at[pl.ds(i * size, size)],
+            sems.at[i],
+        )
+        for i in range(steps)
+    ]
+    for copy in copies:
+        copy.start()
+    for copy in copies:
+        copy.wait()
+
+
+def load_rows(features, own):
+    shape = (features.shape[0] // 2, features.shape[1])
+    (rows,) = local_call(
+        functools.partial(load_body, own),
+        (features,),
+        [(shape, BF16)],
+        "load_own" if own else "load_far",
+        [pltpu.SemaphoreType.DMA((8,))],
+        outside=1,
+        limit=46,
+    )
+    return rows
+
+
+def score_body(own, features_ref, cols_ref, give_ref, keep_ref, *ordered_ref):
+    core = lax.axis_index("feat") % 2
     size = give_ref.shape[0]
-    cols = cols_ref[...]
+    if own:
+        cols = cols_ref[...]
+    else:
+        half, side = features_ref.shape[1] // 2, my_side()
+        for i, part in enumerate((side, 1 - side)):
+            ordered_ref[0][span(part * half, half), :] = cols_ref[:, i].reshape(half, -1)
+        cols = ordered_ref[0][...]
     for whose, out_ref in ((1 - core, give_ref), (core, keep_ref)):
-        rows = features_ref[span((where * 2 + whose) * size, size), :]
+        rows = features_ref[span(whose * size, size), :]
         out_ref[...] = jnp.dot(rows, cols, preferred_element_type=F32).astype(out_ref.dtype)
 
 
@@ -156,7 +230,7 @@
     query_block, tiled, give, keep = local_call(
         precond_body,
         (factor, queries),
-        [((depth, count), F32), ((width, depth, count), BF16)] + [((2, depth, cols), BF16)] * 2,
+        [((depth, count), F32), ((width // 2, depth, count), BF16)] + [((2, 2, depth, cols // 2), BF16)] * 2,
         "precond",
         [
             pltpu.VMEM(factor.shape, BF16),
@@ -166,62 +240,85 @@
         outside=2,
         limit=53,
         )
-    query_cols = exchange_wide(tiled.reshape(cols, count))
+    query_cols = exchange_side(tiled.reshape(cols // 2, count))
     got = swap_core(give)
-    far = swap_chip(jnp.stack([got[0], keep[0]]))
-    factor_cols = jnp.stack([far[0], got[1], far[1], keep[1]]).reshape(4 * depth, cols)
-    query_cols, factor_cols = lax.optimization_barrier((query_cols, factor_cols))
+    piece = [[jnp.stack([got[i, j], keep[i, j]]) for j in range(2)] for i in range(2)]
+    piece[0][1] = swap_side(piece[0][1])
+    piece[1][0] = swap_chip(piece[1][0])
+    piece[1][1] = swap_chip_and_side(piece[1][1])
+    factor_cols = jnp.stack([jnp.stack(row, 1) for row in piece], 1)
+    factor_cols = factor_cols.reshape(8 * depth, cols // 2)
 
     half = (row_count // 2, count)
+    far_cols = swap_side(query_cols)
     give, keep, held = local_call(
-        functools.partial(row_body, 8),
+        functools.partial(near_row_body, 8),
         (features, query_cols),
-        [(half, BF16), (half, F32), (features.shape, BF16)],
-        "rows",
+        [(half, F32), (half, F32), (features.shape, BF16)],
+        "near_rows",
         [pltpu.SemaphoreType.DMA((16,))],
         outside=1,
         limit=43,
     )
+    give, keep = local_call(
+        far_row_body, (held, far_cols, give, keep), [(half, BF16), (half, F32)], "far_rows"
+    )
     chip_sum = (keep + swap_core(give).astype(F32)).astype(BF16)
     mine = (chip_sum.astype(F32) + swap_chip(chip_sum).astype(F32)).astype(BF16)
     other = swap_core(mine)
 
-    (gram_part,) = local_call(
-        gram_body,
-        (held, mine, other),
-        [((cols, count), BF16)],
-        "gram",
-        [pltpu.VMEM((row_count, count), BF16)],
-    )
-    gram_parts = exchange_wide(gram_part).reshape(width, depth, count)
+    parts = []
+    for far in (True, False):
+        (part,) = local_call(
+            functools.partial(gram_body, far),
+            (held, mine, other),
+            [((cols // 2, count), BF16 if far else F32)],
+            "far_gram" if far else "own_gram",
+            [pltpu.VMEM((row_count, count), BF16)],
+        )
+        parts.append(part)
+    gram_part = (parts[1] + swap_side(parts[0]).astype(F32)).astype(BF16)
+    gram_parts = exchange_side(gram_part).reshape(width // 2, depth, count)
     (residual,) = local_call(
         functools.partial(residual_body, total_rows),
         (query_block, gram_parts),
-        [((width, depth, count), BF16)],
+        [((width // 2, depth, count), BF16)],
         "residual",
     )
-    residual_cols = exchange_wide(residual.reshape(cols, count))
-
-    part = (2 * depth, count)
+    residual_cols = exchange_side(residual.reshape(cols // 2, count))
+
+    part = (4 * depth, count)
     give, keep = local_call(
         product_body, (factor_cols, residual_cols), [(part, F32), (part, F32)], "product"
     )
     product = keep + swap_core(give)
-    product = product[depth:] + swap_chip(product[:depth])
-    corrected = (2.0 * query_block - product).astype(BF16)
-    corrected_cols = exchange_wide(jnp.tile(corrected, (width, 1)))
+    product, source = lax.optimization_barrier((product, features))
+    far_features = load_rows(source, False)
+    product = product[: 2 * depth] + swap_chip(product[2 * depth :])
+    start = jnp.concatenate([2.0 * query_block - product[:depth], -product[depth:]])
+    start, far_features, source = lax.optimization_barrier((start, far_features, features))
+    own_features = load_rows(source, True)
+    corrected = (start + jnp.roll(swap_side(start), depth, 0)).astype(BF16)
+    corrected, own_features = lax.optimization_barrier((corrected, own_features))
+    corrected_cols = exchange_side(jnp.tile(corrected, (width // 2, 1)))
+    corrected_cols = corrected_cols.reshape(width // 2, 2, depth, count)
 
     quarter = (row_count // 4, count)
-    sums = []
-    for own in (False, True):
-        give, keep = local_call(
-            functools.partial(score_body, own),
-            (held, corrected_cols),
-            [(quarter, BF16), (quarter, F32)],
-            "own_scores" if own else "far_scores",
-        )
-        sums.append(keep + swap_core(give).astype(F32))
-    return sums[1] + swap_chip(sums[0].astype(BF16)).astype(F32)
+    give, keep, corrected_cols = local_call(
+        functools.partial(score_body, False),
+        (far_features, corrected_cols),
+        [(quarter, BF16), (quarter, F32), ((cols, count), BF16)],
+        "far_scores",
+    )
+    far = keep + swap_core(give).astype(F32)
+    give, keep = local_call(
+        functools.partial(score_body, True),
+        (own_features, corrected_cols),
+        [(quarter, BF16), (quarter, F32)],
+        "own_scores",
+    )
+    own = keep + swap_core(give).astype(F32)
+    return own + swap_chip(far.astype(BF16)).astype(F32)
 
 
 def solution(mesh):

time: 145 us -> 135 us (0.931)
  blocking collectives: 66.8 us -> 38.5 us
  starting transfers between devices: 36 us -> 45.6 us
  Pallas kernels: 12.6 us -> 18 us
    all_to_all x3 -> x2, blocking collectives: 66.8 us -> 38.5 us  [exchange_side(): lax.all_to_all(blocks, 'wide', 0, 0, tiled=True, axis_index_groups=sides)]
    ppermute x4, waiting for transfers between devices: 22.8 us -> 9.47 us  [swap_chip(): return lax.ppermute(block, 'feat', CHIP_SWAP)]
    all_to_all x1 -> x2, waiting for transfers between devices: 1.26 us -> 9.78 us  [exchange_side(): lax.all_to_all(blocks, 'wide', 0, 0, tiled=True, axis_index_groups=sides)]
    ppermute x0 -> x5, starting transfers between devices: none -> 7.37 us  [the longest x4 4.55 us: swap_side(): lax.ppermute(block, 'wide', [(i, (i + width // 2) % width) for i in range...]
    ppermute x0 -> x5, waiting for transfers between devices: none -> 7.05 us  [the longest x4 4.77 us: swap_side(): lax.ppermute(block, 'wide', [(i, (i + width // 2) % width) for i in range...]
    pallas_call x7 -> x11, Pallas kernels: 12.6 us -> 18 us  [local_call(): pl.pallas_call(body, in_specs=[anywhere] * outside + [IN_VMEM] * (len(ope...]
    ppermute x6, starting transfers between devices: 12.5 us -> 15.6 us  [swap_core(): return lax.ppermute(block, 'feat', CORE_SWAP)]
    all_to_all x1 -> x2, starting transfers between devices: 13.5 us -> 11.1 us  [exchange_side(): lax.all_to_all(blocks, 'wide', 0, 0, tiled=True, axis_index_groups=sides)]
  transfers between devices with their start and end apart: 11 -> 17, of which waited for: 9 -> 10; matrix products, arithmetic and copies ran while one was open for 0% -> 1% of each run, Pallas kernels for 1% -> 9%
where the time goes in v4:
time: 135 us; the launch traced here: 134 us
  starting transfers between devices  45.6 us (34%)
  blocking collectives  38.5 us (29%)
  waiting for transfers between devices  29.5 us (22%)
  Pallas kernels  18 us (13%)
  other arithmetic  1.89 us (1%)
    all_to_all x2, blocking collectives, exchange_side(): lax.all_to_all(blocks, 'wide', 0, 0, tiled=True, axis_index_groups=sides)  38.5 us
    pallas_call x11, Pallas kernels, local_call(): pl.pallas_call(body, in_specs=[anywhere] * outside + [IN_VMEM] * (len(ope...  18 us
    ppermute x6, starting transfers between devices, swap_core(): return lax.ppermute(block, 'feat', CORE_SWAP)  15.6 us
    ppermute x4, starting transfers between devices, swap_chip(): return lax.ppermute(block, 'feat', CHIP_SWAP)  11.5 us
    all_to_all x2, starting transfers between devices, exchange_side(): lax.all_to_all(blocks, 'wide', 0, 0, tiled=True, axis_index_groups=sides)  11.1 us
    all_to_all x2, waiting for transfers between devices, exchange_side(): lax.all_to_all(blocks, 'wide', 0, 0, tiled=True, axis_index_groups=sides)  9.78 us
    ppermute x4, waiting for transfers between devices, swap_chip(): return lax.ppermute(block, 'feat', CHIP_SWAP)  9.47 us
    ppermute x4, waiting for transfers between devices, swap_side(): lax.ppermute(block, 'wide', [(i, (i + width // 2) % width) for i in range...  4.77 us
  transfers between devices with their start and end apart: 17, of which 10 were waited for; matrix products, arithmetic and copies ran while one was open for 1% of the time, Pallas kernels for 9%

profile of v4, /device:TPU:1, one launch (start us, length us, event | category | flops | bytes accessed | tf_op | source)
XLA Modules:
  0.0 134.0 jit_solution(12614820461404377742)
XLA Ops:
  0.0 2.5 %precond.1 = (f32[32,128]{1,0:T(8,128)S(1)}, bf16[32,32,128]{2,1,0:T(8,128)(2,1)S(1)}, bf16[2,2,32,1024]{3,2,1,0:T(8,128)(2,1)S(1)}, bf16[2,2,32,1024]{3,2,1,0:T(8,128)(2,1)S(1)}) custom-call(bf16[32,8192]{1,0:T(8,128)(2,1)} %bitcast.36, bf16[128,8192]{1,0:T(8,128)(2,1)} %queries_hbm.1), custom_call_target="tpu_custom_call" | custom-call | tf_op jit(solution)/shard_map/precond/pallas_call | solution.py:48
  2.5 21.4 %all_to_all.31 = bf16[32,32,128]{2,1,0:T(8,128)(2,1)S(1)} all-to-all(bf16[32,32,128]{2,1,0:T(8,128)(2,1)S(1)} %get-tuple-element.31), channel_id=1, replica_groups={{0,4,8,12,16,20,24,28,32,36,40,44,48,52,56,60,64,68,72,76,80,84,88,92,9..., dimensions={0} | all-to-all | bytes 524288 | tf_op jit(solution)/shard_map/all_to_all | solution.py:39
  23.8 1.3 collective-permute-start.4
  25.1 4.5 %near_rows.1 = (f32[1024,128]{1,0:T(8,128)S(1)}, f32[1024,128]{1,0:T(8,128)S(1)}, bf16[2048,2048]{1,0:T(8,128)(2,1)S(1)}) custom-call(bf16[2048,2048]{1,0:T(8,128)(2,1)} %features_hbm.3, bf16[1024,128]{1,0:T(8,128)(2,1)S(1)} %bitcast.35), custom_call_target="tpu_custom_call" | custom-call | tf_op jit(solution)/shard_map/near_rows/pallas_call | solution.py:48
  29.7 1.3 far_rows.1
  30.9 4.4 %collective-permute-start.5 = (bf16[1024,128]{1,0:T(8,128)(2,1)S(1)}, bf16[1024,128]{1,0:T(8,128)(2,1)S(1)}, u32[]{:S(2)}, u32[]{:S(2)}) collective-permute-start(bf16[1024,128]{1,0:T(8,128)(2,1)S(1)} %get-tuple-element.36), channel_id=1, source_target_pairs={{0,1},{1,0},{2,3},{3,2},{4,5},{5,4},{6,7},{7,6},{8,9},{9,8},{10,11... | collective-permute-start | bytes 786440 | tf_op jit(solution)/shard_map/ppermute | solution.py:16
  35.3 1.2 collective-permute-done.5
  36.5 3.0 %collective-permute-start.6 = (bf16[1024,128]{1,0:T(8,128)(2,1)S(1)}, bf16[1024,128]{1,0:T(8,128)(2,1)S(1)}, u32[]{:S(2)}, u32[]{:S(2)}) collective-permute-start(bf16[1024,128]{1,0:T(8,128)(2,1)S(1)} %add_convert_fusion.2), channel_id=1, source_target_pairs={{0,2},{2,0},{1,3},{3,1},{4,6},{6,4},{5,7},{7,5},{8,10},{10,8},{9,1... | collective-permute-start | bytes 786440 | tf_op jit(solution)/shard_map/ppermute | solution.py:20
  39.5 6.1 %collective-permute-done.6 = bf16[1024,128]{1,0:T(8,128)(2,1)S(1)} collective-permute-done((bf16[1024,128]{1,0:T(8,128)(2,1)S(1)}, bf16[1024,128]{1,0:T(8,128)(2,1)S(1)}, u32[]{:S(2)}, u32[]{:S(2)}) %collective-permute-start.6) | collective-permute-done | bytes 262176 | tf_op jit(solution)/shard_map/ppermute | solution.py:20
  45.7 1.3 collective-permute-start.7
  47.0 1.2 collective-permute-done.7.other_ref
  49.0 1.4 %collective-permute-start.8 = (bf16[1024,128]{1,0:T(8,128)(2,1)S(1)}, bf16[1024,128]{1,0:T(8,128)(2,1)S(1)}, u32[]{:S(2)}, u32[]{:S(2)}) collective-permute-start(bf16[1024,128]{1,0:T(8,128)(2,1)S(1)} %far_gram.1), channel_id=1, source_target_pairs={{0,128},{4,132},{8,136},{12,140},{16,144},{20,148},{24,152},{28,15... | collective-permute-start | bytes 786440 | tf_op jit(solution)/shard_map/ppermute | solution.py:25
  51.1 0.9 own_gram.1
  52.0 4.6 %collective-permute-done.8 = bf16[1024,128]{1,0:T(8,128)(2,1)S(1)} collective-permute-done((bf16[1024,128]{1,0:T(8,128)(2,1)S(1)}, bf16[1024,128]{1,0:T(8,128)(2,1)S(1)}, u32[]{:S(2)}, u32[]{:S(2)}) %collective-permute-start.8) | collective-permute-done | bytes 262176 | tf_op jit(solution)/shard_map/ppermute | solution.py:25
  57.4 4.9 %all-to-all-start.1 = ((bf16[32,32,128]{2,1,0:T(8,128)(2,1)}), bf16[32,32,128]{2,1,0:T(8,128)(2,1)S(1)}, u32[]{:S(2)}, u32[]{:S(2)}) async-start(bf16[32,32,128]{2,1,0:T(8,128)(2,1)} %bitcast.17), calls=%async_computation.1 | async-start | bytes 524288 | tf_op jit(solution)/shard_map/all_to_all | solution.py:39
  62.4 1.4 %collective-permute-start.1 = (bf16[2,32,1024]{2,1,0:T(8,128)(2,1)S(1)}, bf16[2,32,1024]{2,1,0:T(8,128)(2,1)S(1)}, u32[]{:S(2)}, u32[]{:S(2)}) collective-permute-start(bf16[2,32,1024]{2,1,0:T(8,128)(2,1)S(1)} %pad_maximum_fusion.1), channel_id=1, source_target_pairs={{0,128},{4,132},{8,136},{12,140},{16,144},{20,148},{24,152},{28,15... | collective-permute-start | bytes 393224 | tf_op jit(solution)/shard_map/ppermute | solution.py:25
  63.8 2.7 %collective-permute-start.2 = (bf16[2,32,1024]{2,1,0:T(8,128)(2,1)S(1)}, bf16[2,32,1024]{2,1,0:T(8,128)(2,1)S(1)}, u32[]{:S(2)}, u32[]{:S(2)}) collective-permute-start(bf16[2,32,1024]{2,1,0:T(8,128)(2,1)S(1)} %pad_maximum_fusion.2), channel_id=1, source_target_pairs={{0,2},{2,0},{1,3},{3,1},{4,6},{6,4},{5,7},{7,5},{8,10},{10,8},{9,1... | collective-permute-start | bytes 393224 | tf_op jit(solution)/shard_map/ppermute | solution.py:20
  66.5 5.5 %all-to-all-done.1.parts_ref = bf16[32,32,128]{2,1,0:T(8,128)(2,1)S(1)} async-done(((bf16[32,32,128]{2,1,0:T(8,128)(2,1)}), bf16[32,32,128]{2,1,0:T(8,128)(2,1)S(1)}, u32[]{:S(2)}, u32[]{:S(2)}) %all-to-all-start.1) | async-done | bytes 262176 | tf_op jit(solution)/shard_map/all_to_all | solution.py:39
  72.8 6.2 %all-to-all-start.2 = ((bf16[32,32,128]{2,1,0:T(8,128)(2,1)}), bf16[32,32,128]{2,1,0:T(8,128)(2,1)S(1)}, u32[]{:S(2)}, u32[]{:S(2)}) async-start(bf16[32,32,128]{2,1,0:T(8,128)(2,1)} %residual.1), calls=%async_computation.2 | async-start | bytes 524288 | tf_op jit(solution)/shard_map/all_to_all | solution.py:39
  78.9 2.8 %collective-permute-start.3 = (bf16[2,32,1024]{2,1,0:T(8,128)(2,1)S(1)}, bf16[2,32,1024]{2,1,0:T(8,128)(2,1)S(1)}, u32[]{:S(2)}, u32[]{:S(2)}) collective-permute-start(bf16[2,32,1024]{2,1,0:T(8,128)(2,1)S(1)} %pad_maximum_fusion.3), channel_id=1, source_target_pairs={{0,130},{2,128},{1,131},{3,129},{4,134},{6,132},{5,135},{7,133},{8... | collective-permute-start | bytes 393224 | tf_op jit(solution)/shard_map/ppermute | solution.py:33
  81.8 2.3 %collective-permute-done.3 = bf16[2,32,1024]{2,1,0:T(8,128)(2,1)S(1)} collective-permute-done((bf16[2,32,1024]{2,1,0:T(8,128)(2,1)S(1)}, bf16[2,32,1024]{2,1,0:T(8,128)(2,1)S(1)}, u32[]{:S(2)}, u32[]{:S(2)}) %collective-permute-start.3) | collective-permute-done | bytes 131104 | tf_op jit(solution)/shard_map/ppermute | solution.py:33
  84.3 4.3 %all-to-all-done.2 = bf16[32,32,128]{2,1,0:T(8,128)(2,1)S(1)} async-done(((bf16[32,32,128]{2,1,0:T(8,128)(2,1)}), bf16[32,32,128]{2,1,0:T(8,128)(2,1)S(1)}, u32[]{:S(2)}, u32[]{:S(2)}) %all-to-all-start.2) | async-done | bytes 262176 | tf_op jit(solution)/shard_map/all_to_all | solution.py:39
  88.9 3.9 %collective-permute-start.9 = (f32[128,128]{1,0:T(8,128)S(1)}, f32[128,128]{1,0:T(8,128)S(1)}, u32[]{:S(2)}, u32[]{:S(2)}) collective-permute-start(f32[128,128]{1,0:T(8,128)S(1)} %get-tuple-element.38), channel_id=1, source_target_pairs={{0,1},{1,0},{2,3},{3,2},{4,5},{5,4},{6,7},{7,6},{8,9},{9,8},{10,11... | collective-permute-start | bytes 196616 | tf_op jit(solution)/shard_map/ppermute | solution.py:16
  93.7 3.0 %collective-permute-start.10 = (f32[64,128]{1,0:T(8,128)S(1)}, f32[64,128]{1,0:T(8,128)S(1)}, u32[]{:S(2)}, u32[]{:S(2)}) collective-permute-start(f32[64,128]{1,0:T(8,128)S(1)} %slice.53), channel_id=1, source_target_pairs={{0,2},{2,0},{1,3},{3,1},{4,6},{6,4},{5,7},{7,5},{8,10},{10,8},{9,1... | collective-permute-start | bytes 98312 | tf_op jit(solution)/shard_map/ppermute | solution.py:20
  96.7 2.2 %load_far.1.features_ref = bf16[1024,2048]{1,0:T(8,128)(2,1)S(1)} custom-call(bf16[2048,2048]{1,0:T(8,128)(2,1)} %features_hbm.3), custom_call_target="tpu_custom_call" | custom-call | tf_op jit(solution)/shard_map/load_far/pallas_call | solution.py:48
  99.5 2.2 %load_own.1.features_ref = bf16[1024,2048]{1,0:T(8,128)(2,1)S(1)} custom-call(bf16[2048,2048]{1,0:T(8,128)(2,1)} %features_hbm.3), custom_call_target="tpu_custom_call" | custom-call | tf_op jit(solution)/shard_map/load_own/pallas_call | solution.py:48
  102.0 17.2 %all_to_all.32 = bf16[32,64,128]{2,1,0:T(8,128)(2,1)S(1)} all-to-all(bf16[32,64,128]{2,1,0:T(8,128)(2,1)S(1)} %tile.2), channel_id=1, replica_groups={{0,4,8,12,16,20,24,28,32,36,40,44,48,52,56,60,64,68,72,76,80,84,88,92,9..., dimensions={0} | all-to-all | bytes 1048576 | tf_op jit(solution)/shard_map/all_to_all | solution.py:39
  119.2 1.3 far_scores.1
  120.5 5.2 %collective-permute-start.13 = (bf16[512,128]{1,0:T(8,128)(2,1)S(1)}, bf16[512,128]{1,0:T(8,128)(2,1)S(1)}, u32[]{:S(2)}, u32[]{:S(2)}) collective-permute-start(bf16[512,128]{1,0:T(8,128)(2,1)S(1)} %get-tuple-element.50), channel_id=1, source_target_pairs={{0,1},{1,0},{2,3},{3,2},{4,5},{5,4},{6,7},{7,6},{8,9},{9,8},{10,11... | collective-permute-start | bytes 393224 | tf_op jit(solution)/shard_map/ppermute | solution.py:16
  125.7 1.2 own_scores.1
  127.1 2.8 %collective-permute-start.14 = (bf16[512,128]{1,0:T(8,128)(2,1)S(1)}, bf16[512,128]{1,0:T(8,128)(2,1)S(1)}, u32[]{:S(2)}, u32[]{:S(2)}) collective-permute-start(bf16[512,128]{1,0:T(8,128)(2,1)S(1)} %add_convert_fusion.3), channel_id=1, source_target_pairs={{0,2},{2,0},{1,3},{3,1},{4,6},{6,4},{5,7},{7,5},{8,10},{10,8},{9,1... | collective-permute-start | bytes 393224 | tf_op jit(solution)/shard_map/ppermute | solution.py:20
  129.9 3.4 %collective-permute-done.14 = bf16[512,128]{1,0:T(8,128)(2,1)S(1)} collective-permute-done((bf16[512,128]{1,0:T(8,128)(2,1)S(1)}, bf16[512,128]{1,0:T(8,128)(2,1)S(1)}, u32[]{:S(2)}, u32[]{:S(2)}) %collective-permute-start.14) | collective-permute-done | bytes 131104 | tf_op jit(solution)/shard_map/ppermute | solution.py:20
  (38 shorter events, 6.3 us)
Async XLA Ops:
  23.8 5.8 %collective-permute-start.4 = (bf16[1024,128]{1,0:T(8,128)(2,1)S(1)}, bf16[1024,128]{1,0:T(8,128)(2,1)S(1)}, u32[]{:S(2)}, u32[]{:S(2)}) collective-permute-start(bf16[1024,128]{1,0:T(8,128)(2,1)S(1)} %bitcast.34), channel_id=1, source_target_pairs={{0,128},{4,132},{8,136},{12,140},{16,144},{20,148},{24,152},{28,15... | collective-permute-start | bytes 786440 | tf_op jit(solution)/shard_map/ppermute | solution.py:25
  30.9 5.5 %collective-permute-start.5 = (bf16[1024,128]{1,0:T(8,128)(2,1)S(1)}, bf16[1024,128]{1,0:T(8,128)(2,1)S(1)}, u32[]{:S(2)}, u32[]{:S(2)}) collective-permute-start(bf16[1024,128]{1,0:T(8,128)(2,1)S(1)} %get-tuple-element.36), channel_id=1, source_target_pairs={{0,1},{1,0},{2,3},{3,2},{4,5},{5,4},{6,7},{7,6},{8,9},{9,8},{10,11... | collective-permute-start | bytes 786440 | tf_op jit(solution)/shard_map/ppermute | solution.py:16
  36.5 9.1 %collective-permute-start.6 = (bf16[1024,128]{1,0:T(8,128)(2,1)S(1)}, bf16[1024,128]{1,0:T(8,128)(2,1)S(1)}, u32[]{:S(2)}, u32[]{:S(2)}) collective-permute-start(bf16[1024,128]{1,0:T(8,128)(2,1)S(1)} %add_convert_fusion.2), channel_id=1, source_target_pairs={{0,2},{2,0},{1,3},{3,1},{4,6},{6,4},{5,7},{7,5},{8,10},{10,8},{9,1... | collective-permute-start | bytes 786440 | tf_op jit(solution)/shard_map/ppermute | solution.py:20
  45.7 2.5 %collective-permute-start.7 = (bf16[1024,128]{1,0:T(8,128)(2,1)S(1)}, bf16[1024,128]{1,0:T(8,128)(2,1)S(1)}, u32[]{:S(2)}, u32[]{:S(2)}) collective-permute-start(bf16[1024,128]{1,0:T(8,128)(2,1)S(1)} %add_convert_fusion.1.mine_ref), channel_id=1, source_target_pairs={{0,1},{1,0},{2,3},{3,2},{4,5},{5,4},{6,7},{7,6},{8,9},{9,8},{10,11... | collective-permute-start | bytes 786440 | tf_op jit(solution)/shard_map/ppermute | solution.py:16
  49.0 7.6 %collective-permute-start.8 = (bf16[1024,128]{1,0:T(8,128)(2,1)S(1)}, bf16[1024,128]{1,0:T(8,128)(2,1)S(1)}, u32[]{:S(2)}, u32[]{:S(2)}) collective-permute-start(bf16[1024,128]{1,0:T(8,128)(2,1)S(1)} %far_gram.1), channel_id=1, source_target_pairs={{0,128},{4,132},{8,136},{12,140},{16,144},{20,148},{24,152},{28,15... | collective-permute-start | bytes 786440 | tf_op jit(solution)/shard_map/ppermute | solution.py:25
  50.4 12.0 %collective-permute-start = (bf16[2,2,32,1024]{3,2,1,0:T(8,128)(2,1)S(1)}, bf16[2,2,32,1024]{3,2,1,0:T(8,128)(2,1)S(1)}, u32[]{:S(2)}, u32[]{:S(2)}) collective-permute-start(bf16[2,2,32,1024]{3,2,1,0:T(8,128)(2,1)S(1)} %get-tuple-element.29), channel_id=1, source_target_pairs={{0,1},{1,0},{2,3},{3,2},{4,5},{5,4},{6,7},{7,6},{8,9},{9,8},{10,11... | collective-permute-start | bytes 786440 | tf_op jit(solution)/shard_map/ppermute | solution.py:16
  57.4 14.6 %all-to-all-start.1 = ((bf16[32,32,128]{2,1,0:T(8,128)(2,1)}), bf16[32,32,128]{2,1,0:T(8,128)(2,1)S(1)}, u32[]{:S(2)}, u32[]{:S(2)}) async-start(bf16[32,32,128]{2,1,0:T(8,128)(2,1)} %bitcast.17), calls=%async_computation.1 | async-start | bytes 524288 | tf_op jit(solution)/shard_map/all_to_all | solution.py:39
  62.4 19.4 %collective-permute-start.1 = (bf16[2,32,1024]{2,1,0:T(8,128)(2,1)S(1)}, bf16[2,32,1024]{2,1,0:T(8,128)(2,1)S(1)}, u32[]{:S(2)}, u32[]{:S(2)}) collective-permute-start(bf16[2,32,1024]{2,1,0:T(8,128)(2,1)S(1)} %pad_maximum_fusion.1), channel_id=1, source_target_pairs={{0,128},{4,132},{8,136},{12,140},{16,144},{20,148},{24,152},{28,15... | collective-permute-start | bytes 393224 | tf_op jit(solution)/shard_map/ppermute | solution.py:25
  63.8 18.0 %collective-permute-start.2 = (bf16[2,32,1024]{2,1,0:T(8,128)(2,1)S(1)}, bf16[2,32,1024]{2,1,0:T(8,128)(2,1)S(1)}, u32[]{:S(2)}, u32[]{:S(2)}) collective-permute-start(bf16[2,32,1024]{2,1,0:T(8,128)(2,1)S(1)} %pad_maximum_fusion.2), channel_id=1, source_target_pairs={{0,2},{2,0},{1,3},{3,1},{4,6},{6,4},{5,7},{7,5},{8,10},{10,8},{9,1... | collective-permute-start | bytes 393224 | tf_op jit(solution)/shard_map/ppermute | solution.py:20
  72.8 15.8 %all-to-all-start.2 = ((bf16[32,32,128]{2,1,0:T(8,128)(2,1)}), bf16[32,32,128]{2,1,0:T(8,128)(2,1)S(1)}, u32[]{:S(2)}, u32[]{:S(2)}) async-start(bf16[32,32,128]{2,1,0:T(8,128)(2,1)} %residual.1), calls=%async_computation.2 | async-start | bytes 524288 | tf_op jit(solution)/shard_map/all_to_all | solution.py:39
  78.9 5.2 %collective-permute-start.3 = (bf16[2,32,1024]{2,1,0:T(8,128)(2,1)S(1)}, bf16[2,32,1024]{2,1,0:T(8,128)(2,1)S(1)}, u32[]{:S(2)}, u32[]{:S(2)}) collective-permute-start(bf16[2,32,1024]{2,1,0:T(8,128)(2,1)S(1)} %pad_maximum_fusion.3), channel_id=1, source_target_pairs={{0,130},{2,128},{1,131},{3,129},{4,134},{6,132},{5,135},{7,133},{8... | collective-permute-start | bytes 393224 | tf_op jit(solution)/shard_map/ppermute | solution.py:33
  88.9 4.8 %collective-permute-start.9 = (f32[128,128]{1,0:T(8,128)S(1)}, f32[128,128]{1,0:T(8,128)S(1)}, u32[]{:S(2)}, u32[]{:S(2)}) collective-permute-start(f32[128,128]{1,0:T(8,128)S(1)} %get-tuple-element.38), channel_id=1, source_target_pairs={{0,1},{1,0},{2,3},{3,2},{4,5},{5,4},{6,7},{7,6},{8,9},{9,8},{10,11... | collective-permute-start | bytes 196616 | tf_op jit(solution)/shard_map/ppermute | solution.py:16
  93.7 5.2 %collective-permute-start.10 = (f32[64,128]{1,0:T(8,128)S(1)}, f32[64,128]{1,0:T(8,128)S(1)}, u32[]{:S(2)}, u32[]{:S(2)}) collective-permute-start(f32[64,128]{1,0:T(8,128)S(1)} %slice.53), channel_id=1, source_target_pairs={{0,2},{2,0},{1,3},{3,1},{4,6},{6,4},{5,7},{7,5},{8,10},{10,8},{9,1... | collective-permute-start | bytes 98312 | tf_op jit(solution)/shard_map/ppermute | solution.py:20
  99.0 2.9 %collective-permute-start.11 = (f32[64,128]{1,0:T(8,128)S(1)}, f32[64,128]{1,0:T(8,128)S(1)}, u32[]{:S(2)}, u32[]{:S(2)}) collective-permute-start(f32[64,128]{1,0:T(8,128)S(1)} %pad_maximum_fusion.4), channel_id=1, source_target_pairs={{0,128},{4,132},{8,136},{12,140},{16,144},{20,148},{24,152},{28,15... | collective-permute-start | bytes 98312 | tf_op jit(solution)/shard_map/ppermute | solution.py:25
  120.5 6.6 %collective-permute-start.13 = (bf16[512,128]{1,0:T(8,128)(2,1)S(1)}, bf16[512,128]{1,0:T(8,128)(2,1)S(1)}, u32[]{:S(2)}, u32[]{:S(2)}) collective-permute-start(bf16[512,128]{1,0:T(8,128)(2,1)S(1)} %get-tuple-element.50), channel_id=1, source_target_pairs={{0,1},{1,0},{2,3},{3,2},{4,5},{5,4},{6,7},{7,6},{8,9},{9,8},{10,11... | collective-permute-start | bytes 393224 | tf_op jit(solution)/shard_map/ppermute | solution.py:16
  127.0 3.0 %collective-permute-start.12 = (bf16[512,128]{1,0:T(8,128)(2,1)S(1)}, bf16[512,128]{1,0:T(8,128)(2,1)S(1)}, u32[]{:S(2)}, u32[]{:S(2)}) collective-permute-start(bf16[512,128]{1,0:T(8,128)(2,1)S(1)} %get-tuple-element.48), channel_id=1, source_target_pairs={{0,1},{1,0},{2,3},{3,2},{4,5},{5,4},{6,7},{7,6},{8,9},{9,8},{10,11... | collective-permute-start | bytes 393224 | tf_op jit(solution)/shard_map/ppermute | solution.py:16
  127.1 6.2 %collective-permute-start.14 = (bf16[512,128]{1,0:T(8,128)(2,1)S(1)}, bf16[512,128]{1,0:T(8,128)(2,1)S(1)}, u32[]{:S(2)}, u32[]{:S(2)}) collective-permute-start(bf16[512,128]{1,0:T(8,128)(2,1)S(1)} %add_convert_fusion.3), channel_id=1, source_target_pairs={{0,2},{2,0},{1,3},{3,1},{4,6},{6,4},{5,7},{7,5},{8,10},{10,8},{9,1... | collective-permute-start | bytes 393224 | tf_op jit(solution)/shard_map/ppermute | solution.py:20

commit v5 on v4

--- a/solution.py
+++ b/solution.py
@@ -131,27 +131,34 @@
         out_ref[j * size : (j + 1) * size, :] = jnp.dot(block, cols, preferred_element_type=F32)
 
 
-def far_row_body(features_ref, cols_ref, near_give_ref, near_keep_ref, give_ref, keep_ref):
+def far_row_body(
+    piece, features_ref, cols_ref, near_give_ref, near_keep_ref, give_ref, keep_ref
+):
     core, side = lax.axis_index("feat") % 2, my_side()
-    half, depth = give_ref.shape[0], cols_ref.shape[0]
+    size, depth, half = give_ref.shape[0], cols_ref.shape[0], near_give_ref.shape[0]
     cols = cols_ref[...]
+    near = slice(piece * size, (piece + 1) * size)
     for part, near_ref, out_ref in (
         (1 - core, near_give_ref, give_ref),
         (core, near_keep_ref, keep_ref),
     ):
-        block = features_ref[span(part * half, half), span((1 - side) * depth, depth)]
-        product = near_ref[...] + jnp.dot(block, cols, preferred_element_type=F32)
+        rows = span(part * half + piece * size, size)
+        block = features_ref[rows, span((1 - side) * depth, depth)]
+        product = near_ref[near, :] + jnp.dot(block, cols, preferred_element_type=F32)
         out_ref[...] = product.astype(out_ref.dtype)
 
 
-def gram_body(other, features_ref, mine_ref, other_ref, out_ref, rows_ref):
+def gram_body(other, features_ref, *refs):
+    *parts, out_ref, rows_ref = refs
     core = lax.axis_index("feat") % 2
     side = 1 - my_side() if other else my_side()
-    size = mine_ref.shape[0]
+    size = parts[0].shape[0]
+    half = size * len(parts) // 2
+    for i, part_ref in enumerate(parts):
+        whose = core if i % 2 == 0 else 1 - core
+        rows_ref[span(whose * half + i // 2 * size, size), :] = part_ref[...]
+    rows = rows_ref[...].T
     piece = 512
-    rows_ref[span(core * size, size), :] = mine_ref[...]
-    rows_ref[span((1 - core) * size, size), :] = other_ref[...]
-    rows = rows_ref[...].T
     depth = out_ref.shape[0]
     for i in range(depth // piece):
         cols = span(side * depth + i * piece, piece)
@@ -172,13 +179,13 @@
     keep_ref[...] = product[size:]
 
 
-def load_body(own, features_hbm, out_ref, sems):
+def load_body(features_hbm, out_ref, sems):
     chip = lax.axis_index("feat") // 2
     rows, steps = out_ref.shape[0], sems.shape[0]
-    first, size = (chip if own else 1 - chip) * rows, rows // steps
+    size = rows // steps
     copies = [
         pltpu.make_async_copy(
-            features_hbm.at[span(first + i * size, size)],
+            features_hbm.at[span((1 - chip) * rows + i * size, size)],
             out_ref.at[pl.ds(i * size, size)],
             sems.at[i],
         )
@@ -190,13 +197,13 @@
         copy.wait()
 
 
-def load_rows(features, own):
+def load_far_rows(features):
     shape = (features.shape[0] // 2, features.shape[1])
     (rows,) = local_call(
-        functools.partial(load_body, own),
+        load_body,
         (features,),
         [(shape, BF16)],
-        "load_own" if own else "load_far",
+        "load_far",
         [pltpu.SemaphoreType.DMA((8,))],
         outside=1,
         limit=46,
@@ -204,19 +211,54 @@
     return rows
 
 
-def score_body(own, features_ref, cols_ref, give_ref, keep_ref, *ordered_ref):
-    core = lax.axis_index("feat") % 2
-    size = give_ref.shape[0]
-    if own:
-        cols = cols_ref[...]
-    else:
-        half, side = features_ref.shape[1] // 2, my_side()
-        for i, part in enumerate((side, 1 - side)):
-            ordered_ref[0][span(part * half, half), :] = cols_ref[:, i].reshape(half, -1)
-        cols = ordered_ref[0][...]
+def far_score_body(features_ref, cols_ref, give_ref, keep_ref, ordered_ref):
+    core, side = lax.axis_index("feat") % 2, my_side()
+    size, half = give_ref.shape[0], features_ref.shape[1] // 2
+    for i, part in enumerate((side, 1 - side)):
+        ordered_ref[span(part * half, half), :] = cols_ref[:, i].reshape(half, -1)
+    cols = ordered_ref[...]
     for whose, out_ref in ((1 - core, give_ref), (core, keep_ref)):
         rows = features_ref[span(whose * size, size), :]
         out_ref[...] = jnp.dot(rows, cols, preferred_element_type=F32).astype(out_ref.dtype)
+
+
+def own_score_body(features_hbm, cols_ref, give_ref, keep_ref, features_ref, sems):
+    place = lax.axis_index("feat")
+    chip, core = place // 2, place % 2
+    half, steps = give_ref.shape[0], sems.shape[0]
+    size = 2 * half // steps
+    copies = []
+    for i in range(steps):
+        whose = 1 - core if i < steps // 2 else core
+        start = (chip * 2 + whose) * half + i % (steps // 2) * size
+        copies.append(
+            pltpu.make_async_copy(
+                features_hbm.at[span(start, size)],
+                features_ref.at[pl.ds(i * size, size)],
+                sems.at[i],
+            )
+        )
+        copies[i].start()
+    cols = cols_ref[...]
+    size = half // 2
+    for i in range(4):
+        for copy in copies[i * steps // 4 : (i + 1) * steps // 4]:
+            copy.wait()
+        rows = features_ref[i * size : (i + 1) * size, :]
+        out_ref = give_ref if i < 2 else keep_ref
+        product = jnp.dot(rows, cols, preferred_element_type=F32)
+        out_ref[i % 2 * size : (i % 2 + 1) * size, :] = product.astype(out_ref.dtype)
+
+
+def own_columns(other_factor, near_factor):
+    _, _, depth, cols = near_factor.shape
+    pairs = [
+        [jnp.stack([other_factor[i, j], near_factor[i, j]]) for j in range(2)] for i in range(2)
+    ]
+    pairs[0][1] = swap_side(pairs[0][1])
+    pairs[1][0] = swap_chip(pairs[1][0])
+    pairs[1][1] = swap_chip_and_side(pairs[1][1])
+    return jnp.stack([jnp.stack(pair, 1) for pair in pairs], 1).reshape(8 * depth, cols)
 
 
 def on_device(features, queries, inverse_factor):
@@ -227,7 +269,7 @@
     count = queries.shape[0]
     total_rows = row_count * width
 
-    query_block, tiled, give, keep = local_call(
+    query_block, tiled, far_factor, near_factor = local_call(
         precond_body,
         (factor, queries),
         [((depth, count), F32), ((width // 2, depth, count), BF16)] + [((2, 2, depth, cols // 2), BF16)] * 2,
@@ -241,14 +283,6 @@
         limit=53,
         )
     query_cols = exchange_side(tiled.reshape(cols // 2, count))
-    got = swap_core(give)
-    piece = [[jnp.stack([got[i, j], keep[i, j]]) for j in range(2)] for i in range(2)]
-    piece[0][1] = swap_side(piece[0][1])
-    piece[1][0] = swap_chip(piece[1][0])
-    piece[1][1] = swap_chip_and_side(piece[1][1])
-    factor_cols = jnp.stack([jnp.stack(row, 1) for row in piece], 1)
-    factor_cols = factor_cols.reshape(8 * depth, cols // 2)
-
     half = (row_count // 2, count)
     far_cols = swap_side(query_cols)
     give, keep, held = local_call(
@@ -260,24 +294,35 @@
         outside=1,
         limit=43,
     )
-    give, keep = local_call(
-        far_row_body, (held, far_cols, give, keep), [(half, BF16), (half, F32)], "far_rows"
-    )
-    chip_sum = (keep + swap_core(give).astype(F32)).astype(BF16)
-    mine = (chip_sum.astype(F32) + swap_chip(chip_sum).astype(F32)).astype(BF16)
-    other = swap_core(mine)
+    quarter = (row_count // 4, count)
+    sums = []
+    for i in range(2):
+        part, kept = local_call(
+            functools.partial(far_row_body, i),
+            (held, far_cols, give, keep),
+            [(quarter, BF16), (quarter, F32)],
+            f"far_rows_{i}",
+        )
+        sums.append((kept, swap_core(part)))
+    row_weights = []
+    for kept, got in sums:
+        chip_sum = (kept + got.astype(F32)).astype(BF16)
+        mine = (chip_sum.astype(F32) + swap_chip(chip_sum).astype(F32)).astype(BF16)
+        row_weights += [mine, swap_core(mine)]
 
     parts = []
     for far in (True, False):
         (part,) = local_call(
             functools.partial(gram_body, far),
-            (held, mine, other),
+            (held, *row_weights),
             [((cols // 2, count), BF16 if far else F32)],
             "far_gram" if far else "own_gram",
             [pltpu.VMEM((row_count, count), BF16)],
         )
         parts.append(part)
     gram_part = (parts[1] + swap_side(parts[0]).astype(F32)).astype(BF16)
+    other_factor = swap_core(far_factor)
+    gram_part, other_factor = lax.optimization_barrier((gram_part, other_factor))
     gram_parts = exchange_side(gram_part).reshape(width // 2, depth, count)
     (residual,) = local_call(
         functools.partial(residual_body, total_rows),
@@ -285,6 +330,7 @@
         [((width // 2, depth, count), BF16)],
         "residual",
     )
+    factor_cols = own_columns(other_factor, near_factor)
     residual_cols = exchange_side(residual.reshape(cols // 2, count))
 
     part = (4 * depth, count)
@@ -293,32 +339,36 @@
     )
     product = keep + swap_core(give)
     product, source = lax.optimization_barrier((product, features))
-    far_features = load_rows(source, False)
-    product = product[: 2 * depth] + swap_chip(product[2 * depth :])
-    start = jnp.concatenate([2.0 * query_block - product[:depth], -product[depth:]])
-    start, far_features, source = lax.optimization_barrier((start, far_features, features))
-    own_features = load_rows(source, True)
-    corrected = (start + jnp.roll(swap_side(start), depth, 0)).astype(BF16)
-    corrected, own_features = lax.optimization_barrier((corrected, own_features))
+    own, far = product[: 2 * depth], -product[2 * depth :]
+    own = jnp.concatenate([2.0 * query_block - own[:depth], -own[depth:]])
+    crossed = swap_side(own) + swap_chip_and_side(far)
+    corrected = own + swap_chip(far) + jnp.roll(crossed, depth, 0)
+    far_features = load_far_rows(source)
+    corrected, far_features = lax.optimization_barrier((corrected.astype(BF16), far_features))
     corrected_cols = exchange_side(jnp.tile(corrected, (width // 2, 1)))
     corrected_cols = corrected_cols.reshape(width // 2, 2, depth, count)
 
     quarter = (row_count // 4, count)
     give, keep, corrected_cols = local_call(
-        functools.partial(score_body, False),
+        far_score_body,
         (far_features, corrected_cols),
         [(quarter, BF16), (quarter, F32), ((cols, count), BF16)],
         "far_scores",
     )
-    far = keep + swap_core(give).astype(F32)
+    far = (keep + swap_core(give).astype(F32)).astype(BF16)
+    far, corrected_cols, source = lax.optimization_barrier((far, corrected_cols, features))
     give, keep = local_call(
-        functools.partial(score_body, True),
-        (own_features, corrected_cols),
+        own_score_body,
+        (source, corrected_cols),
         [(quarter, BF16), (quarter, F32)],
         "own_scores",
-    )
-    own = keep + swap_core(give).astype(F32)
-    return own + swap_chip(far.astype(BF16)).astype(F32)
+        [pltpu.VMEM((row_count // 2, cols), BF16), pltpu.SemaphoreType.DMA((8,))],
+        outside=1,
+        limit=46,
+    )
+    size = row_count // 8
+    got = jnp.concatenate([swap_core(give[:size]), swap_core(give[size:])])
+    return keep + got.astype(F32) + swap_chip(far).astype(F32)
 
 
 def solution(mesh):

time: 135 us -> 132 us (0.978)
  waiting for transfers between devices: 29.5 us -> 26.3 us
  starting transfers between devices: 45.6 us -> 47.2 us
    ppermute x4 -> x5, waiting for transfers between devices: 9.47 us -> 4.84 us  [swap_chip(): return lax.ppermute(block, 'feat', CHIP_SWAP)]
    ppermute x4 -> x5, starting transfers between devices: 11.5 us -> 9.18 us  [swap_chip(): return lax.ppermute(block, 'feat', CHIP_SWAP)]
    ppermute x6 -> x9, starting transfers between devices: 15.6 us -> 17.8 us  [swap_core(): return lax.ppermute(block, 'feat', CORE_SWAP)]
    ppermute x1 -> x2, starting transfers between devices: 2.82 us -> 4.49 us  [swap_chip_and_side(): return lax.ppermute(block, ('wide', 'feat'), pairs)]
    ppermute x6 -> x9, waiting for transfers between devices: 3.23 us -> 4.2 us  [swap_core(): return lax.ppermute(block, 'feat', CORE_SWAP)]
  transfers between devices with their start and end apart: 17 -> 22, of which waited for: 10 -> 13; matrix products, arithmetic and copies ran while one was open for 1% -> 1% of each run, Pallas kernels for 9% -> 9%
where the time goes in v5:
time: 132 us
  starting transfers between devices  47.2 us (36%)
  blocking collectives  38.1 us (29%)
  waiting for transfers between devices  26.3 us (20%)
  Pallas kernels  17.7 us (13%)
  other arithmetic  1.9 us (1%)
    all_to_all x2, blocking collectives, exchange_side(): lax.all_to_all(blocks, 'wide', 0, 0, tiled=True, axis_index_groups=sides)  38.1 us
    ppermute x9, starting transfers between devices, swap_core(): return lax.ppermute(block, 'feat', CORE_SWAP)  17.8 us
    pallas_call x11, Pallas kernels, local_call(): pl.pallas_call(body, in_specs=[anywhere] * outside + [IN_VMEM] * (len(ope...  17.7 us
    all_to_all x2, starting transfers between devices, exchange_side(): lax.all_to_all(blocks, 'wide', 0, 0, tiled=True, axis_index_groups=sides)  11.1 us
    all_to_all x2, waiting for transfers between devices, exchange_side(): lax.all_to_all(blocks, 'wide', 0, 0, tiled=True, axis_index_groups=sides)  9.89 us
    ppermute x5, starting transfers between devices, swap_chip(): return lax.ppermute(block, 'feat', CHIP_SWAP)  9.18 us
    ppermute x4, waiting for transfers between devices, swap_side(): lax.ppermute(block, 'wide', [(i, (i + width // 2) % width) for i in range...  4.9 us
    ppermute x5, waiting for transfers between devices, swap_chip(): return lax.ppermute(block, 'feat', CHIP_SWAP)  4.84 us
  transfers between devices with their start and end apart: 22, of which 13 were waited for; matrix products, arithmetic and copies ran while one was open for 1% of the time, Pallas kernels for 9%

profile of v5, /device:TPU:1, one launch (start us, length us, event | category | flops | bytes accessed | tf_op | source)
XLA Modules:
  0.0 131.8 jit_solution(11668619053990975575)
XLA Ops:
  0.0 2.5 %precond.1 = (f32[32,128]{1,0:T(8,128)S(1)}, bf16[32,32,128]{2,1,0:T(8,128)(2,1)S(1)}, bf16[2,2,32,1024]{3,2,1,0:T(8,128)(2,1)S(1)}, bf16[2,2,32,1024]{3,2,1,0:T(8,128)(2,1)S(1)}) custom-call(bf16[32,8192]{1,0:T(8,128)(2,1)} %bitcast.36, bf16[128,8192]{1,0:T(8,128)(2,1)} %queries_hbm.1), custom_call_target="tpu_custom_call" | custom-call | tf_op jit(solution)/shard_map/precond/pallas_call | solution.py:48
  2.5 21.4 %all_to_all.31 = bf16[32,32,128]{2,1,0:T(8,128)(2,1)S(1)} all-to-all(bf16[32,32,128]{2,1,0:T(8,128)(2,1)S(1)} %get-tuple-element.33), channel_id=1, replica_groups={{0,4,8,12,16,20,24,28,32,36,40,44,48,52,56,60,64,68,72,76,80,84,88,92,9..., dimensions={0} | all-to-all | bytes 524288 | tf_op jit(solution)/shard_map/all_to_all | solution.py:39
  23.8 1.3 collective-permute-start
  25.1 4.5 %near_rows.1 = (f32[1024,128]{1,0:T(8,128)S(1)}, f32[1024,128]{1,0:T(8,128)S(1)}, bf16[2048,2048]{1,0:T(8,128)(2,1)S(1)}) custom-call(bf16[2048,2048]{1,0:T(8,128)(2,1)} %features_hbm.3, bf16[1024,128]{1,0:T(8,128)(2,1)S(1)} %bitcast.35), custom_call_target="tpu_custom_call" | custom-call | tf_op jit(solution)/shard_map/near_rows/pallas_call | solution.py:48
  30.4 4.4 %collective-permute-start.4 = (bf16[512,128]{1,0:T(8,128)(2,1)S(1)}, bf16[512,128]{1,0:T(8,128)(2,1)S(1)}, u32[]{:S(2)}, u32[]{:S(2)}) collective-permute-start(bf16[512,128]{1,0:T(8,128)(2,1)S(1)} %get-tuple-element.40), channel_id=1, source_target_pairs={{0,1},{1,0},{2,3},{3,2},{4,5},{5,4},{6,7},{7,6},{8,9},{9,8},{10,11... | collective-permute-start | bytes 393224 | tf_op jit(solution)/shard_map/ppermute | solution.py:16
  35.8 3.0 %collective-permute-start.5 = (bf16[512,128]{1,0:T(8,128)(2,1)S(1)}, bf16[512,128]{1,0:T(8,128)(2,1)S(1)}, u32[]{:S(2)}, u32[]{:S(2)}) collective-permute-start(bf16[512,128]{1,0:T(8,128)(2,1)S(1)} %add_convert_fusion.3), channel_id=1, source_target_pairs={{0,2},{2,0},{1,3},{3,1},{4,6},{6,4},{5,7},{7,5},{8,10},{10,8},{9,1... | collective-permute-start | bytes 393224 | tf_op jit(solution)/shard_map/ppermute | solution.py:20
  38.8 1.1 collective-permute-start.2
  39.9 2.1 %collective-permute-done.5 = bf16[512,128]{1,0:T(8,128)(2,1)S(1)} collective-permute-done((bf16[512,128]{1,0:T(8,128)(2,1)S(1)}, bf16[512,128]{1,0:T(8,128)(2,1)S(1)}, u32[]{:S(2)}, u32[]{:S(2)}) %collective-permute-start.5) | collective-permute-done | bytes 131104 | tf_op jit(solution)/shard_map/ppermute | solution.py:20
  42.1 1.3 collective-permute-start.6
  43.4 1.4 %collective-permute-done.2 = bf16[512,128]{1,0:T(8,128)(2,1)S(1)} collective-permute-done((bf16[512,128]{1,0:T(8,128)(2,1)S(1)}, bf16[512,128]{1,0:T(8,128)(2,1)S(1)}, u32[]{:S(2)}, u32[]{:S(2)}) %collective-permute-start.2) | collective-permute-done | bytes 131104 | tf_op jit(solution)/shard_map/ppermute | solution.py:20
  44.9 1.6 %collective-permute-start.3 = (bf16[512,128]{1,0:T(8,128)(2,1)S(1)}, bf16[512,128]{1,0:T(8,128)(2,1)S(1)}, u32[]{:S(2)}, u32[]{:S(2)}) collective-permute-start(bf16[512,128]{1,0:T(8,128)(2,1)S(1)} %add_convert_fusion.4.refs_0_), channel_id=1, source_target_pairs={{0,1},{1,0},{2,3},{3,2},{4,5},{5,4},{6,7},{7,6},{8,9},{9,8},{10,11... | collective-permute-start | bytes 393224 | tf_op jit(solution)/shard_map/ppermute | solution.py:16
  48.3 1.1 collective-permute-start.7
  51.0 4.9 %collective-permute-done.7 = bf16[1024,128]{1,0:T(8,128)(2,1)S(1)} collective-permute-done((bf16[1024,128]{1,0:T(8,128)(2,1)S(1)}, bf16[1024,128]{1,0:T(8,128)(2,1)S(1)}, u32[]{:S(2)}, u32[]{:S(2)}) %collective-permute-start.7) | collective-permute-done | bytes 262176 | tf_op jit(solution)/shard_map/ppermute | solution.py:25
  56.7 4.9 %all-to-all-start.1 = ((bf16[32,32,128]{2,1,0:T(8,128)(2,1)}), bf16[32,32,128]{2,1,0:T(8,128)(2,1)S(1)}, u32[]{:S(2)}, u32[]{:S(2)}) async-start(bf16[32,32,128]{2,1,0:T(8,128)(2,1)} %bitcast.17), calls=%async_computation.1 | async-start | bytes 524288 | tf_op jit(solution)/shard_map/all_to_all | solution.py:39
  61.6 1.2 collective-permute-start.9
  62.8 2.9 %collective-permute-start.10 = (bf16[2,32,1024]{2,1,0:T(8,128)(2,1)S(1)}, bf16[2,32,1024]{2,1,0:T(8,128)(2,1)S(1)}, u32[]{:S(2)}, u32[]{:S(2)}) collective-permute-start(bf16[2,32,1024]{2,1,0:T(8,128)(2,1)S(1)} %pad_maximum_fusion.2), channel_id=1, source_target_pairs={{0,2},{2,0},{1,3},{3,1},{4,6},{6,4},{5,7},{7,5},{8,10},{10,8},{9,1... | collective-permute-start | bytes 393224 | tf_op jit(solution)/shard_map/ppermute | solution.py:20
  65.7 5.5 %all-to-all-done.1.parts_ref = bf16[32,32,128]{2,1,0:T(8,128)(2,1)S(1)} async-done(((bf16[32,32,128]{2,1,0:T(8,128)(2,1)}), bf16[32,32,128]{2,1,0:T(8,128)(2,1)S(1)}, u32[]{:S(2)}, u32[]{:S(2)}) %all-to-all-start.1) | async-done | bytes 262176 | tf_op jit(solution)/shard_map/all_to_all | solution.py:39
  72.0 6.2 %all-to-all-start.2 = ((bf16[32,32,128]{2,1,0:T(8,128)(2,1)}), bf16[32,32,128]{2,1,0:T(8,128)(2,1)S(1)}, u32[]{:S(2)}, u32[]{:S(2)}) async-start(bf16[32,32,128]{2,1,0:T(8,128)(2,1)} %residual.1), calls=%async_computation.2 | async-start | bytes 524288 | tf_op jit(solution)/shard_map/all_to_all | solution.py:39
  78.2 2.6 %collective-permute-start.11 = (bf16[2,32,1024]{2,1,0:T(8,128)(2,1)S(1)}, bf16[2,32,1024]{2,1,0:T(8,128)(2,1)S(1)}, u32[]{:S(2)}, u32[]{:S(2)}) collective-permute-start(bf16[2,32,1024]{2,1,0:T(8,128)(2,1)S(1)} %pad_maximum_fusion.3), channel_id=1, source_target_pairs={{0,130},{2,128},{1,131},{3,129},{4,134},{6,132},{5,135},{7,133},{8... | collective-permute-start | bytes 393224 | tf_op jit(solution)/shard_map/ppermute | solution.py:33
  80.9 2.5 %collective-permute-done.11 = bf16[2,32,1024]{2,1,0:T(8,128)(2,1)S(1)} collective-permute-done((bf16[2,32,1024]{2,1,0:T(8,128)(2,1)S(1)}, bf16[2,32,1024]{2,1,0:T(8,128)(2,1)S(1)}, u32[]{:S(2)}, u32[]{:S(2)}) %collective-permute-start.11) | collective-permute-done | bytes 131104 | tf_op jit(solution)/shard_map/ppermute | solution.py:33
  83.4 4.4 %all-to-all-done.2 = bf16[32,32,128]{2,1,0:T(8,128)(2,1)S(1)} async-done(((bf16[32,32,128]{2,1,0:T(8,128)(2,1)}), bf16[32,32,128]{2,1,0:T(8,128)(2,1)S(1)}, u32[]{:S(2)}, u32[]{:S(2)}) %all-to-all-start.2) | async-done | bytes 262176 | tf_op jit(solution)/shard_map/all_to_all | solution.py:39
  88.1 3.8 %collective-permute-start.12 = (f32[128,128]{1,0:T(8,128)S(1)}, f32[128,128]{1,0:T(8,128)S(1)}, u32[]{:S(2)}, u32[]{:S(2)}) collective-permute-start(f32[128,128]{1,0:T(8,128)S(1)} %get-tuple-element.46), channel_id=1, source_target_pairs={{0,1},{1,0},{2,3},{3,2},{4,5},{5,4},{6,7},{7,6},{8,9},{9,8},{10,11... | collective-permute-start | bytes 196616 | tf_op jit(solution)/shard_map/ppermute | solution.py:16
  92.8 1.1 collective-permute-start.14
  94.0 1.9 %collective-permute-start.15 = (f32[64,128]{1,0:T(8,128)S(1)}, f32[64,128]{1,0:T(8,128)S(1)}, u32[]{:S(2)}, u32[]{:S(2)}) collective-permute-start(f32[64,128]{1,0:T(8,128)S(1)} %slice_negate_fusion), channel_id=1, source_target_pairs={{0,130},{2,128},{1,131},{3,129},{4,134},{6,132},{5,135},{7,133},{8... | collective-permute-start | bytes 98312 | tf_op jit(solution)/shard_map/ppermute | solution.py:33
  96.6 2.2 %load_far.1.features_ref = bf16[1024,2048]{1,0:T(8,128)(2,1)S(1)} custom-call(bf16[2048,2048]{1,0:T(8,128)(2,1)} %features_hbm.3), custom_call_target="tpu_custom_call" | custom-call | tf_op jit(solution)/shard_map/load_far/pallas_call | solution.py:48
  98.9 1.3 collective-permute-done.13
  100.3 16.8 %all_to_all.32 = bf16[32,64,128]{2,1,0:T(8,128)(2,1)S(1)} all-to-all(bf16[32,64,128]{2,1,0:T(8,128)(2,1)S(1)} %tile.2), channel_id=1, replica_groups={{0,4,8,12,16,20,24,28,32,36,40,44,48,52,56,60,64,68,72,76,80,84,88,92,9..., dimensions={0} | all-to-all | bytes 1048576 | tf_op jit(solution)/shard_map/all_to_all | solution.py:39
  117.1 1.3 far_scores.1
  118.4 5.2 %collective-permute-start.16 = (bf16[512,128]{1,0:T(8,128)(2,1)S(1)}, bf16[512,128]{1,0:T(8,128)(2,1)S(1)}, u32[]{:S(2)}, u32[]{:S(2)}) collective-permute-start(bf16[512,128]{1,0:T(8,128)(2,1)S(1)} %get-tuple-element.52), channel_id=1, source_target_pairs={{0,1},{1,0},{2,3},{3,2},{4,5},{5,4},{6,7},{7,6},{8,9},{9,8},{10,11... | collective-permute-start | bytes 393224 | tf_op jit(solution)/shard_map/ppermute | solution.py:16
  123.6 1.0 collective-permute-done.16
  124.6 1.4 %collective-permute-start.19 = (bf16[512,128]{1,0:T(8,128)(2,1)S(1)}, bf16[512,128]{1,0:T(8,128)(2,1)S(1)}, u32[]{:S(2)}, u32[]{:S(2)}) collective-permute-start(bf16[512,128]{1,0:T(8,128)(2,1)S(1)} %add_convert_fusion.1), channel_id=1, source_target_pairs={{0,2},{2,0},{1,3},{3,1},{4,6},{6,4},{5,7},{7,5},{8,10},{10,8},{9,1... | collective-permute-start | bytes 393224 | tf_op jit(solution)/shard_map/ppermute | solution.py:20
  126.1 3.0 %own_scores.1 = (bf16[512,128]{1,0:T(8,128)(2,1)S(1)}, f32[512,128]{1,0:T(8,128)S(1)}) custom-call(bf16[2048,2048]{1,0:T(8,128)(2,1)} %features_hbm.3, bf16[2048,128]{1,0:T(8,128)(2,1)S(1)} %get-tuple-element.55.cols_ref), custom_call_target="tpu_custom_call" | custom-call | tf_op jit(solution)/shard_map/own_scores/pallas_call | solution.py:48
  (51 shorter events, 11.9 us)
Async XLA Ops:
  23.8 5.8 %collective-permute-start = (bf16[1024,128]{1,0:T(8,128)(2,1)S(1)}, bf16[1024,128]{1,0:T(8,128)(2,1)S(1)}, u32[]{:S(2)}, u32[]{:S(2)}) collective-permute-start(bf16[1024,128]{1,0:T(8,128)(2,1)S(1)} %bitcast.34), channel_id=1, source_target_pairs={{0,128},{4,132},{8,136},{12,140},{16,144},{20,148},{24,152},{28,15... | collective-permute-start | bytes 786440 | tf_op jit(solution)/shard_map/ppermute | solution.py:25
  30.4 5.3 %collective-permute-start.4 = (bf16[512,128]{1,0:T(8,128)(2,1)S(1)}, bf16[512,128]{1,0:T(8,128)(2,1)S(1)}, u32[]{:S(2)}, u32[]{:S(2)}) collective-permute-start(bf16[512,128]{1,0:T(8,128)(2,1)S(1)} %get-tuple-element.40), channel_id=1, source_target_pairs={{0,1},{1,0},{2,3},{3,2},{4,5},{5,4},{6,7},{7,6},{8,9},{9,8},{10,11... | collective-permute-start | bytes 393224 | tf_op jit(solution)/shard_map/ppermute | solution.py:16
  35.5 3.3 %collective-permute-start.1 = (bf16[512,128]{1,0:T(8,128)(2,1)S(1)}, bf16[512,128]{1,0:T(8,128)(2,1)S(1)}, u32[]{:S(2)}, u32[]{:S(2)}) collective-permute-start(bf16[512,128]{1,0:T(8,128)(2,1)S(1)} %get-tuple-element.38), channel_id=1, source_target_pairs={{0,1},{1,0},{2,3},{3,2},{4,5},{5,4},{6,7},{7,6},{8,9},{9,8},{10,11... | collective-permute-start | bytes 393224 | tf_op jit(solution)/shard_map/ppermute | solution.py:16
  35.8 6.3 %collective-permute-start.5 = (bf16[512,128]{1,0:T(8,128)(2,1)S(1)}, bf16[512,128]{1,0:T(8,128)(2,1)S(1)}, u32[]{:S(2)}, u32[]{:S(2)}) collective-permute-start(bf16[512,128]{1,0:T(8,128)(2,1)S(1)} %add_convert_fusion.3), channel_id=1, source_target_pairs={{0,2},{2,0},{1,3},{3,1},{4,6},{6,4},{5,7},{7,5},{8,10},{10,8},{9,1... | collective-permute-start | bytes 393224 | tf_op jit(solution)/shard_map/ppermute | solution.py:20
  38.8 6.0 %collective-permute-start.2 = (bf16[512,128]{1,0:T(8,128)(2,1)S(1)}, bf16[512,128]{1,0:T(8,128)(2,1)S(1)}, u32[]{:S(2)}, u32[]{:S(2)}) collective-permute-start(bf16[512,128]{1,0:T(8,128)(2,1)S(1)} %add_convert_fusion.5), channel_id=1, source_target_pairs={{0,2},{2,0},{1,3},{3,1},{4,6},{6,4},{5,7},{7,5},{8,10},{10,8},{9,1... | collective-permute-start | bytes 393224 | tf_op jit(solution)/shard_map/ppermute | solution.py:20
  42.1 4.3 %collective-permute-start.6 = (bf16[512,128]{1,0:T(8,128)(2,1)S(1)}, bf16[512,128]{1,0:T(8,128)(2,1)S(1)}, u32[]{:S(2)}, u32[]{:S(2)}) collective-permute-start(bf16[512,128]{1,0:T(8,128)(2,1)S(1)} %add_convert_fusion.2.refs_2_), channel_id=1, source_target_pairs={{0,1},{1,0},{2,3},{3,2},{4,5},{5,4},{6,7},{7,6},{8,9},{9,8},{10,11... | collective-permute-start | bytes 393224 | tf_op jit(solution)/shard_map/ppermute | solution.py:16
  44.9 2.6 %collective-permute-start.3 = (bf16[512,128]{1,0:T(8,128)(2,1)S(1)}, bf16[512,128]{1,0:T(8,128)(2,1)S(1)}, u32[]{:S(2)}, u32[]{:S(2)}) collective-permute-start(bf16[512,128]{1,0:T(8,128)(2,1)S(1)} %add_convert_fusion.4.refs_0_), channel_id=1, source_target_pairs={{0,1},{1,0},{2,3},{3,2},{4,5},{5,4},{6,7},{7,6},{8,9},{9,8},{10,11... | collective-permute-start | bytes 393224 | tf_op jit(solution)/shard_map/ppermute | solution.py:16
  48.3 7.6 %collective-permute-start.7 = (bf16[1024,128]{1,0:T(8,128)(2,1)S(1)}, bf16[1024,128]{1,0:T(8,128)(2,1)S(1)}, u32[]{:S(2)}, u32[]{:S(2)}) collective-permute-start(bf16[1024,128]{1,0:T(8,128)(2,1)S(1)} %far_gram.1), channel_id=1, source_target_pairs={{0,128},{4,132},{8,136},{12,140},{16,144},{20,148},{24,152},{28,15... | collective-permute-start | bytes 786440 | tf_op jit(solution)/shard_map/ppermute | solution.py:25
  49.4 7.2 %collective-permute-start.8 = (bf16[2,2,32,1024]{3,2,1,0:T(8,128)(2,1)S(1)}, bf16[2,2,32,1024]{3,2,1,0:T(8,128)(2,1)S(1)}, u32[]{:S(2)}, u32[]{:S(2)}) collective-permute-start(bf16[2,2,32,1024]{3,2,1,0:T(8,128)(2,1)S(1)} %get-tuple-element.41), channel_id=1, source_target_pairs={{0,1},{1,0},{2,3},{3,2},{4,5},{5,4},{6,7},{7,6},{8,9},{9,8},{10,11... | collective-permute-start | bytes 786440 | tf_op jit(solution)/shard_map/ppermute | solution.py:16
  56.7 14.5 %all-to-all-start.1 = ((bf16[32,32,128]{2,1,0:T(8,128)(2,1)}), bf16[32,32,128]{2,1,0:T(8,128)(2,1)S(1)}, u32[]{:S(2)}, u32[]{:S(2)}) async-start(bf16[32,32,128]{2,1,0:T(8,128)(2,1)} %bitcast.17), calls=%async_computation.1 | async-start | bytes 524288 | tf_op jit(solution)/shard_map/all_to_all | solution.py:39
  61.6 19.2 %collective-permute-start.9 = (bf16[2,32,1024]{2,1,0:T(8,128)(2,1)S(1)}, bf16[2,32,1024]{2,1,0:T(8,128)(2,1)S(1)}, u32[]{:S(2)}, u32[]{:S(2)}) collective-permute-start(bf16[2,32,1024]{2,1,0:T(8,128)(2,1)S(1)} %pad_maximum_fusion.1), channel_id=1, source_target_pairs={{0,128},{4,132},{8,136},{12,140},{16,144},{20,148},{24,152},{28,15... | collective-permute-start | bytes 393224 | tf_op jit(solution)/shard_map/ppermute | solution.py:25
  62.8 18.0 %collective-permute-start.10 = (bf16[2,32,1024]{2,1,0:T(8,128)(2,1)S(1)}, bf16[2,32,1024]{2,1,0:T(8,128)(2,1)S(1)}, u32[]{:S(2)}, u32[]{:S(2)}) collective-permute-start(bf16[2,32,1024]{2,1,0:T(8,128)(2,1)S(1)} %pad_maximum_fusion.2), channel_id=1, source_target_pairs={{0,2},{2,0},{1,3},{3,1},{4,6},{6,4},{5,7},{7,5},{8,10},{10,8},{9,1... | collective-permute-start | bytes 393224 | tf_op jit(solution)/shard_map/ppermute | solution.py:20
  72.0 15.8 %all-to-all-start.2 = ((bf16[32,32,128]{2,1,0:T(8,128)(2,1)}), bf16[32,32,128]{2,1,0:T(8,128)(2,1)S(1)}, u32[]{:S(2)}, u32[]{:S(2)}) async-start(bf16[32,32,128]{2,1,0:T(8,128)(2,1)} %residual.1), calls=%async_computation.2 | async-start | bytes 524288 | tf_op jit(solution)/shard_map/all_to_all | solution.py:39
  78.2 5.1 %collective-permute-start.11 = (bf16[2,32,1024]{2,1,0:T(8,128)(2,1)S(1)}, bf16[2,32,1024]{2,1,0:T(8,128)(2,1)S(1)}, u32[]{:S(2)}, u32[]{:S(2)}) collective-permute-start(bf16[2,32,1024]{2,1,0:T(8,128)(2,1)S(1)} %pad_maximum_fusion.3), channel_id=1, source_target_pairs={{0,130},{2,128},{1,131},{3,129},{4,134},{6,132},{5,135},{7,133},{8... | collective-permute-start | bytes 393224 | tf_op jit(solution)/shard_map/ppermute | solution.py:33
  88.1 4.7 %collective-permute-start.12 = (f32[128,128]{1,0:T(8,128)S(1)}, f32[128,128]{1,0:T(8,128)S(1)}, u32[]{:S(2)}, u32[]{:S(2)}) collective-permute-start(f32[128,128]{1,0:T(8,128)S(1)} %get-tuple-element.46), channel_id=1, source_target_pairs={{0,1},{1,0},{2,3},{3,2},{4,5},{5,4},{6,7},{7,6},{8,9},{9,8},{10,11... | collective-permute-start | bytes 196616 | tf_op jit(solution)/shard_map/ppermute | solution.py:16
  92.8 6.0 %collective-permute-start.14 = (f32[64,128]{1,0:T(8,128)S(1)}, f32[64,128]{1,0:T(8,128)S(1)}, u32[]{:S(2)}, u32[]{:S(2)}) collective-permute-start(f32[64,128]{1,0:T(8,128)S(1)} %pad_maximum_fusion.4), channel_id=1, source_target_pairs={{0,128},{4,132},{8,136},{12,140},{16,144},{20,148},{24,152},{28,15... | collective-permute-start | bytes 98312 | tf_op jit(solution)/shard_map/ppermute | solution.py:25
  94.0 4.9 %collective-permute-start.15 = (f32[64,128]{1,0:T(8,128)S(1)}, f32[64,128]{1,0:T(8,128)S(1)}, u32[]{:S(2)}, u32[]{:S(2)}) collective-permute-start(f32[64,128]{1,0:T(8,128)S(1)} %slice_negate_fusion), channel_id=1, source_target_pairs={{0,130},{2,128},{1,131},{3,129},{4,134},{6,132},{5,135},{7,133},{8... | collective-permute-start | bytes 98312 | tf_op jit(solution)/shard_map/ppermute | solution.py:33
  95.9 4.3 %collective-permute-start.13 = (f32[64,128]{1,0:T(8,128)S(1)}, f32[64,128]{1,0:T(8,128)S(1)}, u32[]{:S(2)}, u32[]{:S(2)}) collective-permute-start(f32[64,128]{1,0:T(8,128)S(1)} %slice_negate_fusion), channel_id=1, source_target_pairs={{0,2},{2,0},{1,3},{3,1},{4,6},{6,4},{5,7},{7,5},{8,10},{10,8},{9,1... | collective-permute-start | bytes 98312 | tf_op jit(solution)/shard_map/ppermute | solution.py:20
  118.4 6.2 %collective-permute-start.16 = (bf16[512,128]{1,0:T(8,128)(2,1)S(1)}, bf16[512,128]{1,0:T(8,128)(2,1)S(1)}, u32[]{:S(2)}, u32[]{:S(2)}) collective-permute-start(bf16[512,128]{1,0:T(8,128)(2,1)S(1)} %get-tuple-element.52), channel_id=1, source_target_pairs={{0,1},{1,0},{2,3},{3,2},{4,5},{5,4},{6,7},{7,6},{8,9},{9,8},{10,11... | collective-permute-start | bytes 393224 | tf_op jit(solution)/shard_map/ppermute | solution.py:16
  124.6 6.4 %collective-permute-start.19 = (bf16[512,128]{1,0:T(8,128)(2,1)S(1)}, bf16[512,128]{1,0:T(8,128)(2,1)S(1)}, u32[]{:S(2)}, u32[]{:S(2)}) collective-permute-start(bf16[512,128]{1,0:T(8,128)(2,1)S(1)} %add_convert_fusion.1), channel_id=1, source_target_pairs={{0,2},{2,0},{1,3},{3,1},{4,6},{6,4},{5,7},{7,5},{8,10},{10,8},{9,1... | collective-permute-start | bytes 393224 | tf_op jit(solution)/shard_map/ppermute | solution.py:20
  129.0 1.6 %collective-permute-start.17 = (bf16[256,128]{1,0:T(8,128)(2,1)S(1)}, bf16[256,128]{1,0:T(8,128)(2,1)S(1)}, u32[]{:S(2)}, u32[]{:S(2)}) collective-permute-start(bf16[256,128]{1,0:T(8,128)(2,1)S(1)} %get-tuple-element.67), channel_id=1, source_target_pairs={{0,1},{1,0},{2,3},{3,2},{4,5},{5,4},{6,7},{7,6},{8,9},{9,8},{10,11... | collective-permute-start | bytes 196616 | tf_op jit(solution)/shard_map/ppermute | solution.py:16
  129.8 1.3 collective-permute-start.18

commit v6 on v5

--- a/solution.py
+++ b/solution.py
@@ -148,22 +148,32 @@
         out_ref[...] = product.astype(out_ref.dtype)
 
 
-def gram_body(other, features_ref, *refs):
-    *parts, out_ref, rows_ref = refs
+def gram_body(chunk, other, features_ref, mine_ref, other_ref, *refs):
+    *before, out_ref, rows_ref = refs
     core = lax.axis_index("feat") % 2
     side = 1 - my_side() if other else my_side()
-    size = parts[0].shape[0]
-    half = size * len(parts) // 2
-    for i, part_ref in enumerate(parts):
-        whose = core if i % 2 == 0 else 1 - core
-        rows_ref[span(whose * half + i // 2 * size, size), :] = part_ref[...]
+    size = mine_ref.shape[0]
+    half = features_ref.shape[0] // 2
+    rows_ref[span(core * size, size), :] = mine_ref[...]
+    rows_ref[span((1 - core) * size, size), :] = other_ref[...]
     rows = rows_ref[...].T
     piece = 512
     depth = out_ref.shape[0]
     for i in range(depth // piece):
         cols = span(side * depth + i * piece, piece)
-        total = jnp.dot(rows, features_ref[:, cols], preferred_element_type=F32)
-        out_ref[i * piece : (i + 1) * piece, :] = total.T.astype(out_ref.dtype)
+        total = sum(
+            jnp.dot(
+                rows[:, j * size : (j + 1) * size],
+                features_ref[j * half + chunk * size : j * half + (chunk + 1) * size, cols],
+                preferred_element_type=F32,
+            )
+            for j in range(2)
+        )
+        where = slice(i * piece, (i + 1) * piece)
+        total = total.T
+        if before:
+            total += before[0][where, :]
+        out_ref[where, :] = total.astype(out_ref.dtype)
 
 
 def residual_body(total_rows, block_ref, parts_ref, out_ref):
@@ -180,33 +190,36 @@
 
 
 def load_body(features_hbm, out_ref, sems):
-    chip = lax.axis_index("feat") // 2
-    rows, steps = out_ref.shape[0], sems.shape[0]
-    size = rows // steps
-    copies = [
-        pltpu.make_async_copy(
-            features_hbm.at[span((1 - chip) * rows + i * size, size)],
-            out_ref.at[pl.ds(i * size, size)],
-            sems.at[i],
-        )
-        for i in range(steps)
-    ]
+    place = lax.axis_index("feat")
+    chip, core = place // 2, place % 2
+    quarter = features_hbm.shape[0] // 4
+    steps = sems.shape[0] // 3
+    size = quarter // steps
+    copies = []
+    for i, part in enumerate((2 - 2 * chip, 3 - 2 * chip, 2 * chip + 1 - core)):
+        for j in range(steps):
+            copies.append(
+                pltpu.make_async_copy(
+                    features_hbm.at[span(part * quarter + j * size, size)],
+                    out_ref.at[pl.ds(i * quarter + j * size, size)],
+                    sems.at[i * steps + j],
+                )
+            )
     for copy in copies:
         copy.start()
     for copy in copies:
         copy.wait()
 
 
-def load_far_rows(features):
-    shape = (features.shape[0] // 2, features.shape[1])
+def load_rows(features):
     (rows,) = local_call(
         load_body,
         (features,),
-        [(shape, BF16)],
-        "load_far",
-        [pltpu.SemaphoreType.DMA((8,))],
+        [((features.shape[0] // 4 * 3, features.shape[1]), BF16)],
+        "load",
+        [pltpu.SemaphoreType.DMA((12,))],
         outside=1,
-        limit=46,
+        limit=44,
     )
     return rows
 
@@ -222,32 +235,33 @@
         out_ref[...] = jnp.dot(rows, cols, preferred_element_type=F32).astype(out_ref.dtype)
 
 
-def own_score_body(features_hbm, cols_ref, give_ref, keep_ref, features_ref, sems):
+def give_score_body(features_ref, cols_ref, out_ref):
+    rows = out_ref.shape[0]
+    product = jnp.dot(features_ref[2 * rows :, :], cols_ref[...], preferred_element_type=F32)
+    out_ref[...] = product.astype(out_ref.dtype)
+
+
+def keep_score_body(features_hbm, cols_ref, out_ref, features_ref, sems):
     place = lax.axis_index("feat")
-    chip, core = place // 2, place % 2
-    half, steps = give_ref.shape[0], sems.shape[0]
-    size = 2 * half // steps
+    rows, steps = out_ref.shape[0], sems.shape[0]
+    size = rows // steps
     copies = []
     for i in range(steps):
-        whose = 1 - core if i < steps // 2 else core
-        start = (chip * 2 + whose) * half + i % (steps // 2) * size
         copies.append(
             pltpu.make_async_copy(
-                features_hbm.at[span(start, size)],
+                features_hbm.at[span(place * rows + i * size, size)],
                 features_ref.at[pl.ds(i * size, size)],
                 sems.at[i],
             )
         )
         copies[i].start()
     cols = cols_ref[...]
-    size = half // 2
-    for i in range(4):
-        for copy in copies[i * steps // 4 : (i + 1) * steps // 4]:
+    size = rows // 2
+    for i in range(2):
+        for copy in copies[i * steps // 2 : (i + 1) * steps // 2]:
             copy.wait()
-        rows = features_ref[i * size : (i + 1) * size, :]
-        out_ref = give_ref if i < 2 else keep_ref
-        product = jnp.dot(rows, cols, preferred_element_type=F32)
-        out_ref[i % 2 * size : (i % 2 + 1) * size, :] = product.astype(out_ref.dtype)
+        piece = slice(i * size, (i + 1) * size)
+        out_ref[piece, :] = jnp.dot(features_ref[piece, :], cols, preferred_element_type=F32)
 
 
 def own_columns(other_factor, near_factor):
@@ -310,16 +324,18 @@
         mine = (chip_sum.astype(F32) + swap_chip(chip_sum).astype(F32)).astype(BF16)
         row_weights += [mine, swap_core(mine)]
 
-    parts = []
-    for far in (True, False):
-        (part,) = local_call(
-            functools.partial(gram_body, far),
-            (held, *row_weights),
-            [((cols // 2, count), BF16 if far else F32)],
-            "far_gram" if far else "own_gram",
-            [pltpu.VMEM((row_count, count), BF16)],
-        )
-        parts.append(part)
+    parts = [None, None]
+    for i in (1, 1 - 1):
+        for j, far in enumerate((True, False)):
+            last = i != 1
+            before = () if not last else (parts[j],)
+            (parts[j],) = local_call(
+                functools.partial(gram_body, i, far),
+                (held, *row_weights[2 * i : 2 * i + 2], *before),
+                [((cols // 2, count), BF16 if far and last else F32)],
+                f"far_gram_{i}" if far else f"own_gram_{i}",
+                [pltpu.VMEM((row_count // 2, count), BF16)],
+            )
     gram_part = (parts[1] + swap_side(parts[0]).astype(F32)).astype(BF16)
     other_factor = swap_core(far_factor)
     gram_part, other_factor = lax.optimization_barrier((gram_part, other_factor))
@@ -343,26 +359,29 @@
     own = jnp.concatenate([2.0 * query_block - own[:depth], -own[depth:]])
     crossed = swap_side(own) + swap_chip_and_side(far)
     corrected = own + swap_chip(far) + jnp.roll(crossed, depth, 0)
-    far_features = load_far_rows(source)
-    corrected, far_features = lax.optimization_barrier((corrected.astype(BF16), far_features))
+    loaded = load_rows(source)
+    corrected, loaded = lax.optimization_barrier((corrected.astype(BF16), loaded))
     corrected_cols = exchange_side(jnp.tile(corrected, (width // 2, 1)))
     corrected_cols = corrected_cols.reshape(width // 2, 2, depth, count)
 
     quarter = (row_count // 4, count)
     give, keep, corrected_cols = local_call(
         far_score_body,
-        (far_features, corrected_cols),
+        (loaded, corrected_cols),
         [(quarter, BF16), (quarter, F32), ((cols, count), BF16)],
         "far_scores",
     )
     far = (keep + swap_core(give).astype(F32)).astype(BF16)
+    (give,) = local_call(
+        give_score_body, (loaded, corrected_cols), [(quarter, BF16)], "give_scores"
+    )
     far, corrected_cols, source = lax.optimization_barrier((far, corrected_cols, features))
-    give, keep = local_call(
-        own_score_body,
+    (keep,) = local_call(
+        keep_score_body,
         (source, corrected_cols),
-        [(quarter, BF16), (quarter, F32)],
-        "own_scores",
-        [pltpu.VMEM((row_count // 2, cols), BF16), pltpu.SemaphoreType.DMA((8,))],
+        [(quarter, F32)],
+        "keep_scores",
+        [pltpu.VMEM((row_count // 4, cols), BF16), pltpu.SemaphoreType.DMA((4,))],
         outside=1,
         limit=46,
     )

time: 132 us -> 132 us (level)
  starting transfers between devices: 47.2 us -> 45.8 us
    ppermute x9, waiting for transfers between devices: 4.2 us -> 1.73 us  [swap_core(): return lax.ppermute(block, 'feat', CORE_SWAP)]
    ppermute x2, waiting for transfers between devices: 2.45 us -> 0.01 us  [swap_chip_and_side(): return lax.ppermute(block, ('wide', 'feat'), pairs)]
    ppermute x4, waiting for transfers between devices: 4.9 us -> 7.3 us  [swap_side(): lax.ppermute(block, 'wide', [(i, (i + width // 2) % width) for i in range...]
    all_to_all x2, waiting for transfers between devices: 9.89 us -> 12 us  [exchange_side(): lax.all_to_all(blocks, 'wide', 0, 0, tiled=True, axis_index_groups=sides)]
    ppermute x5, starting transfers between devices: 9.18 us -> 7.46 us  [swap_chip(): return lax.ppermute(block, 'feat', CHIP_SWAP)]
    pallas_call x11 -> x14, Pallas kernels: 17.7 us -> 18.8 us  [local_call(): pl.pallas_call(body, in_specs=[anywhere] * outside + [IN_VMEM] * (len(ope...]
  transfers between devices with their start and end apart: 22 -> 22, of which waited for: 13 -> 12; matrix products, arithmetic and copies ran while one was open for 1% -> 1% of each run, Pallas kernels for 9% -> 10%
where the time goes in v6:
time: 132 us; the launch traced here: 131 us
  starting transfers between devices  45.8 us (35%)
  blocking collectives  38 us (29%)
  waiting for transfers between devices  26.3 us (20%)
  Pallas kernels  18.8 us (14%)
  other arithmetic  1.91 us (1%)
    all_to_all x2, blocking collectives, exchange_side(): lax.all_to_all(blocks, 'wide', 0, 0, tiled=True, axis_index_groups=sides)  38 us
    pallas_call x14, Pallas kernels, local_call(): pl.pallas_call(body, in_specs=[anywhere] * outside + [IN_VMEM] * (len(ope...  18.8 us
    ppermute x9, starting transfers between devices, swap_core(): return lax.ppermute(block, 'feat', CORE_SWAP)  17.8 us
    all_to_all x2, waiting for transfers between devices, exchange_side(): lax.all_to_all(blocks, 'wide', 0, 0, tiled=True, axis_index_groups=sides)  12 us
    all_to_all x2, starting transfers between devices, exchange_side(): lax.all_to_all(blocks, 'wide', 0, 0, tiled=True, axis_index_groups=sides)  11.1 us
    ppermute x5, starting transfers between devices, swap_chip(): return lax.ppermute(block, 'feat', CHIP_SWAP)  7.46 us
    ppermute x4, waiting for transfers between devices, swap_side(): lax.ppermute(block, 'wide', [(i, (i + width // 2) % width) for i in range...  7.3 us
    ppermute x5, waiting for transfers between devices, swap_chip(): return lax.ppermute(block, 'feat', CHIP_SWAP)  5.34 us
  transfers between devices with their start and end apart: 22, of which 12 were waited for; matrix products, arithmetic and copies ran while one was open for 1% of the time, Pallas kernels for 10%

profile of v6, /device:TPU:1, one launch (start us, length us, event | category | flops | bytes accessed | tf_op | source)
XLA Modules:
  0.0 131.3 jit_solution(4967362189758969417)
XLA Ops:
  0.0 2.5 %precond.1 = (f32[32,128]{1,0:T(8,128)S(1)}, bf16[32,32,128]{2,1,0:T(8,128)(2,1)S(1)}, bf16[2,2,32,1024]{3,2,1,0:T(8,128)(2,1)S(1)}, bf16[2,2,32,1024]{3,2,1,0:T(8,128)(2,1)S(1)}) custom-call(bf16[32,8192]{1,0:T(8,128)(2,1)} %bitcast.36, bf16[128,8192]{1,0:T(8,128)(2,1)} %queries_hbm.1), custom_call_target="tpu_custom_call" | custom-call | tf_op jit(solution)/shard_map/precond/pallas_call | solution.py:48
  2.5 21.4 %all_to_all.31 = bf16[32,32,128]{2,1,0:T(8,128)(2,1)S(1)} all-to-all(bf16[32,32,128]{2,1,0:T(8,128)(2,1)S(1)} %get-tuple-element.31), channel_id=1, replica_groups={{0,4,8,12,16,20,24,28,32,36,40,44,48,52,56,60,64,68,72,76,80,84,88,92,9..., dimensions={0} | all-to-all | bytes 524288 | tf_op jit(solution)/shard_map/all_to_all | solution.py:39
  23.8 1.3 collective-permute-start
  25.1 4.5 %near_rows.1 = (f32[1024,128]{1,0:T(8,128)S(1)}, f32[1024,128]{1,0:T(8,128)S(1)}, bf16[2048,2048]{1,0:T(8,128)(2,1)S(1)}) custom-call(bf16[2048,2048]{1,0:T(8,128)(2,1)} %features_hbm.3, bf16[1024,128]{1,0:T(8,128)(2,1)S(1)} %bitcast.35), custom_call_target="tpu_custom_call" | custom-call | tf_op jit(solution)/shard_map/near_rows/pallas_call | solution.py:48
  30.4 4.4 %collective-permute-start.4 = (bf16[512,128]{1,0:T(8,128)(2,1)S(1)}, bf16[512,128]{1,0:T(8,128)(2,1)S(1)}, u32[]{:S(2)}, u32[]{:S(2)}) collective-permute-start(bf16[512,128]{1,0:T(8,128)(2,1)S(1)} %get-tuple-element.38), channel_id=1, source_target_pairs={{0,1},{1,0},{2,3},{3,2},{4,5},{5,4},{6,7},{7,6},{8,9},{9,8},{10,11... | collective-permute-start | bytes 393224 | tf_op jit(solution)/shard_map/ppermute | solution.py:16
  35.8 3.0 %collective-permute-start.5 = (bf16[512,128]{1,0:T(8,128)(2,1)S(1)}, bf16[512,128]{1,0:T(8,128)(2,1)S(1)}, u32[]{:S(2)}, u32[]{:S(2)}) collective-permute-start(bf16[512,128]{1,0:T(8,128)(2,1)S(1)} %add_convert_fusion.3), channel_id=1, source_target_pairs={{0,2},{2,0},{1,3},{3,1},{4,6},{6,4},{5,7},{7,5},{8,10},{10,8},{9,1... | collective-permute-start | bytes 393224 | tf_op jit(solution)/shard_map/ppermute | solution.py:20
  38.8 1.1 collective-permute-start.2
  39.9 2.1 %collective-permute-done.5 = bf16[512,128]{1,0:T(8,128)(2,1)S(1)} collective-permute-done((bf16[512,128]{1,0:T(8,128)(2,1)S(1)}, bf16[512,128]{1,0:T(8,128)(2,1)S(1)}, u32[]{:S(2)}, u32[]{:S(2)}) %collective-permute-start.5) | collective-permute-done | bytes 131104 | tf_op jit(solution)/shard_map/ppermute | solution.py:20
  42.1 1.3 collective-permute-start.6
  43.4 1.4 %collective-permute-done.2 = bf16[512,128]{1,0:T(8,128)(2,1)S(1)} collective-permute-done((bf16[512,128]{1,0:T(8,128)(2,1)S(1)}, bf16[512,128]{1,0:T(8,128)(2,1)S(1)}, u32[]{:S(2)}, u32[]{:S(2)}) %collective-permute-start.2) | collective-permute-done | bytes 131104 | tf_op jit(solution)/shard_map/ppermute | solution.py:20
  44.9 1.6 %collective-permute-start.3 = (bf16[512,128]{1,0:T(8,128)(2,1)S(1)}, bf16[512,128]{1,0:T(8,128)(2,1)S(1)}, u32[]{:S(2)}, u32[]{:S(2)}) collective-permute-start(bf16[512,128]{1,0:T(8,128)(2,1)S(1)} %add_convert_fusion.4.mine_ref), channel_id=1, source_target_pairs={{0,1},{1,0},{2,3},{3,2},{4,5},{5,4},{6,7},{7,6},{8,9},{9,8},{10,11... | collective-permute-start | bytes 393224 | tf_op jit(solution)/shard_map/ppermute | solution.py:16
  48.0 1.1 collective-permute-start.7
  51.1 4.6 %collective-permute-done.7 = bf16[1024,128]{1,0:T(8,128)(2,1)S(1)} collective-permute-done((bf16[1024,128]{1,0:T(8,128)(2,1)S(1)}, bf16[1024,128]{1,0:T(8,128)(2,1)S(1)}, u32[]{:S(2)}, u32[]{:S(2)}) %collective-permute-start.7) | collective-permute-done | bytes 262176 | tf_op jit(solution)/shard_map/ppermute | solution.py:25
  55.7 0.8 add_convert_fusion
  56.4 4.9 %all-to-all-start.1 = ((bf16[32,32,128]{2,1,0:T(8,128)(2,1)}), bf16[32,32,128]{2,1,0:T(8,128)(2,1)S(1)}, u32[]{:S(2)}, u32[]{:S(2)}) async-start(bf16[32,32,128]{2,1,0:T(8,128)(2,1)} %bitcast.17), calls=%async_computation.1 | async-start | bytes 524288 | tf_op jit(solution)/shard_map/all_to_all | solution.py:39
  61.4 2.8 %collective-permute-start.11 = (bf16[2,32,1024]{2,1,0:T(8,128)(2,1)S(1)}, bf16[2,32,1024]{2,1,0:T(8,128)(2,1)S(1)}, u32[]{:S(2)}, u32[]{:S(2)}) collective-permute-start(bf16[2,32,1024]{2,1,0:T(8,128)(2,1)S(1)} %pad_maximum_fusion.3), channel_id=1, source_target_pairs={{0,130},{2,128},{1,131},{3,129},{4,134},{6,132},{5,135},{7,133},{8... | collective-permute-start | bytes 393224 | tf_op jit(solution)/shard_map/ppermute | solution.py:33
  64.7 6.4 %all-to-all-done.1.parts_ref = bf16[32,32,128]{2,1,0:T(8,128)(2,1)S(1)} async-done(((bf16[32,32,128]{2,1,0:T(8,128)(2,1)}), bf16[32,32,128]{2,1,0:T(8,128)(2,1)S(1)}, u32[]{:S(2)}, u32[]{:S(2)}) %all-to-all-start.1) | async-done | bytes 262176 | tf_op jit(solution)/shard_map/all_to_all | solution.py:39
  71.8 6.1 %all-to-all-start.2 = ((bf16[32,32,128]{2,1,0:T(8,128)(2,1)}), bf16[32,32,128]{2,1,0:T(8,128)(2,1)S(1)}, u32[]{:S(2)}, u32[]{:S(2)}) async-start(bf16[32,32,128]{2,1,0:T(8,128)(2,1)} %residual.1), calls=%async_computation.2 | async-start | bytes 524288 | tf_op jit(solution)/shard_map/all_to_all | solution.py:39
  78.0 1.1 collective-permute-start.9
  79.2 2.7 %collective-permute-done.9 = bf16[2,32,1024]{2,1,0:T(8,128)(2,1)S(1)} collective-permute-done((bf16[2,32,1024]{2,1,0:T(8,128)(2,1)S(1)}, bf16[2,32,1024]{2,1,0:T(8,128)(2,1)S(1)}, u32[]{:S(2)}, u32[]{:S(2)}) %collective-permute-start.9) | collective-permute-done | bytes 131104 | tf_op jit(solution)/shard_map/ppermute | solution.py:25
  82.0 5.6 %all-to-all-done.2 = bf16[32,32,128]{2,1,0:T(8,128)(2,1)S(1)} async-done(((bf16[32,32,128]{2,1,0:T(8,128)(2,1)}), bf16[32,32,128]{2,1,0:T(8,128)(2,1)S(1)}, u32[]{:S(2)}, u32[]{:S(2)}) %all-to-all-start.2) | async-done | bytes 262176 | tf_op jit(solution)/shard_map/all_to_all | solution.py:39
  87.9 3.8 %collective-permute-start.12 = (f32[128,128]{1,0:T(8,128)S(1)}, f32[128,128]{1,0:T(8,128)S(1)}, u32[]{:S(2)}, u32[]{:S(2)}) collective-permute-start(f32[128,128]{1,0:T(8,128)S(1)} %get-tuple-element.44), channel_id=1, source_target_pairs={{0,1},{1,0},{2,3},{3,2},{4,5},{5,4},{6,7},{7,6},{8,9},{9,8},{10,11... | collective-permute-start | bytes 196616 | tf_op jit(solution)/shard_map/ppermute | solution.py:16
  91.6 0.9 collective-permute-done.12
  92.6 1.1 collective-permute-start.14
  93.7 1.9 %collective-permute-start.15 = (f32[64,128]{1,0:T(8,128)S(1)}, f32[64,128]{1,0:T(8,128)S(1)}, u32[]{:S(2)}, u32[]{:S(2)}) collective-permute-start(f32[64,128]{1,0:T(8,128)S(1)} %slice_negate_fusion), channel_id=1, source_target_pairs={{0,130},{2,128},{1,131},{3,129},{4,134},{6,132},{5,135},{7,133},{8... | collective-permute-start | bytes 98312 | tf_op jit(solution)/shard_map/ppermute | solution.py:33
  96.4 2.9 %load.1.features_ref = bf16[1536,2048]{1,0:T(8,128)(2,1)S(1)} custom-call(bf16[2048,2048]{1,0:T(8,128)(2,1)} %features_hbm.3), custom_call_target="tpu_custom_call" | custom-call | tf_op jit(solution)/shard_map/load/pallas_call | solution.py:48
  100.0 16.6 %all_to_all.32 = bf16[32,64,128]{2,1,0:T(8,128)(2,1)S(1)} all-to-all(bf16[32,64,128]{2,1,0:T(8,128)(2,1)S(1)} %tile.2), channel_id=1, replica_groups={{0,4,8,12,16,20,24,28,32,36,40,44,48,52,56,60,64,68,72,76,80,84,88,92,9..., dimensions={0} | all-to-all | bytes 1048576 | tf_op jit(solution)/shard_map/all_to_all | solution.py:39
  116.7 1.3 far_scores.1
  118.0 5.3 %collective-permute-start.16 = (bf16[512,128]{1,0:T(8,128)(2,1)S(1)}, bf16[512,128]{1,0:T(8,128)(2,1)S(1)}, u32[]{:S(2)}, u32[]{:S(2)}) collective-permute-start(bf16[512,128]{1,0:T(8,128)(2,1)S(1)} %get-tuple-element.50), channel_id=1, source_target_pairs={{0,1},{1,0},{2,3},{3,2},{4,5},{5,4},{6,7},{7,6},{8,9},{9,8},{10,11... | collective-permute-start | bytes 393224 | tf_op jit(solution)/shard_map/ppermute | solution.py:16
  124.3 2.2 %collective-permute-start.19 = (bf16[512,128]{1,0:T(8,128)(2,1)S(1)}, bf16[512,128]{1,0:T(8,128)(2,1)S(1)}, u32[]{:S(2)}, u32[]{:S(2)}) collective-permute-start(bf16[512,128]{1,0:T(8,128)(2,1)S(1)} %add_convert_fusion.1), channel_id=1, source_target_pairs={{0,2},{2,0},{1,3},{3,1},{4,6},{6,4},{5,7},{7,5},{8,10},{10,8},{9,1... | collective-permute-start | bytes 393224 | tf_op jit(solution)/shard_map/ppermute | solution.py:20
  127.3 2.1 %keep_scores.1 = f32[512,128]{1,0:T(8,128)S(1)} custom-call(bf16[2048,2048]{1,0:T(8,128)(2,1)} %features_hbm.3, bf16[2048,128]{1,0:T(8,128)(2,1)S(1)} %get-tuple-element.53.cols_ref), custom_call_target="tpu_custom_call" | custom-call | tf_op jit(solution)/shard_map/keep_scores/pallas_call | solution.py:48
  129.4 1.2 collective-permute-done.19
  (54 shorter events, 11.1 us)
Async XLA Ops:
  23.8 5.8 %collective-permute-start = (bf16[1024,128]{1,0:T(8,128)(2,1)S(1)}, bf16[1024,128]{1,0:T(8,128)(2,1)S(1)}, u32[]{:S(2)}, u32[]{:S(2)}) collective-permute-start(bf16[1024,128]{1,0:T(8,128)(2,1)S(1)} %bitcast.34), channel_id=1, source_target_pairs={{0,128},{4,132},{8,136},{12,140},{16,144},{20,148},{24,152},{28,15... | collective-permute-start | bytes 786440 | tf_op jit(solution)/shard_map/ppermute | solution.py:25
  30.4 5.3 %collective-permute-start.4 = (bf16[512,128]{1,0:T(8,128)(2,1)S(1)}, bf16[512,128]{1,0:T(8,128)(2,1)S(1)}, u32[]{:S(2)}, u32[]{:S(2)}) collective-permute-start(bf16[512,128]{1,0:T(8,128)(2,1)S(1)} %get-tuple-element.38), channel_id=1, source_target_pairs={{0,1},{1,0},{2,3},{3,2},{4,5},{5,4},{6,7},{7,6},{8,9},{9,8},{10,11... | collective-permute-start | bytes 393224 | tf_op jit(solution)/shard_map/ppermute | solution.py:16
  35.5 3.3 %collective-permute-start.1 = (bf16[512,128]{1,0:T(8,128)(2,1)S(1)}, bf16[512,128]{1,0:T(8,128)(2,1)S(1)}, u32[]{:S(2)}, u32[]{:S(2)}) collective-permute-start(bf16[512,128]{1,0:T(8,128)(2,1)S(1)} %get-tuple-element.36), channel_id=1, source_target_pairs={{0,1},{1,0},{2,3},{3,2},{4,5},{5,4},{6,7},{7,6},{8,9},{9,8},{10,11... | collective-permute-start | bytes 393224 | tf_op jit(solution)/shard_map/ppermute | solution.py:16
  35.8 6.3 %collective-permute-start.5 = (bf16[512,128]{1,0:T(8,128)(2,1)S(1)}, bf16[512,128]{1,0:T(8,128)(2,1)S(1)}, u32[]{:S(2)}, u32[]{:S(2)}) collective-permute-start(bf16[512,128]{1,0:T(8,128)(2,1)S(1)} %add_convert_fusion.3), channel_id=1, source_target_pairs={{0,2},{2,0},{1,3},{3,1},{4,6},{6,4},{5,7},{7,5},{8,10},{10,8},{9,1... | collective-permute-start | bytes 393224 | tf_op jit(solution)/shard_map/ppermute | solution.py:20
  38.8 6.0 %collective-permute-start.2 = (bf16[512,128]{1,0:T(8,128)(2,1)S(1)}, bf16[512,128]{1,0:T(8,128)(2,1)S(1)}, u32[]{:S(2)}, u32[]{:S(2)}) collective-permute-start(bf16[512,128]{1,0:T(8,128)(2,1)S(1)} %add_convert_fusion.5), channel_id=1, source_target_pairs={{0,2},{2,0},{1,3},{3,1},{4,6},{6,4},{5,7},{7,5},{8,10},{10,8},{9,1... | collective-permute-start | bytes 393224 | tf_op jit(solution)/shard_map/ppermute | solution.py:20
  42.1 4.3 %collective-permute-start.6 = (bf16[512,128]{1,0:T(8,128)(2,1)S(1)}, bf16[512,128]{1,0:T(8,128)(2,1)S(1)}, u32[]{:S(2)}, u32[]{:S(2)}) collective-permute-start(bf16[512,128]{1,0:T(8,128)(2,1)S(1)} %add_convert_fusion.2.mine_ref), channel_id=1, source_target_pairs={{0,1},{1,0},{2,3},{3,2},{4,5},{5,4},{6,7},{7,6},{8,9},{9,8},{10,11... | collective-permute-start | bytes 393224 | tf_op jit(solution)/shard_map/ppermute | solution.py:16
  44.9 2.6 %collective-permute-start.3 = (bf16[512,128]{1,0:T(8,128)(2,1)S(1)}, bf16[512,128]{1,0:T(8,128)(2,1)S(1)}, u32[]{:S(2)}, u32[]{:S(2)}) collective-permute-start(bf16[512,128]{1,0:T(8,128)(2,1)S(1)} %add_convert_fusion.4.mine_ref), channel_id=1, source_target_pairs={{0,1},{1,0},{2,3},{3,2},{4,5},{5,4},{6,7},{7,6},{8,9},{9,8},{10,11... | collective-permute-start | bytes 393224 | tf_op jit(solution)/shard_map/ppermute | solution.py:16
  48.0 7.6 %collective-permute-start.7 = (bf16[1024,128]{1,0:T(8,128)(2,1)S(1)}, bf16[1024,128]{1,0:T(8,128)(2,1)S(1)}, u32[]{:S(2)}, u32[]{:S(2)}) collective-permute-start(bf16[1024,128]{1,0:T(8,128)(2,1)S(1)} %far_gram_0.1), channel_id=1, source_target_pairs={{0,128},{4,132},{8,136},{12,140},{16,144},{20,148},{24,152},{28,15... | collective-permute-start | bytes 786440 | tf_op jit(solution)/shard_map/ppermute | solution.py:25
  49.2 7.2 %collective-permute-start.8 = (bf16[2,2,32,1024]{3,2,1,0:T(8,128)(2,1)S(1)}, bf16[2,2,32,1024]{3,2,1,0:T(8,128)(2,1)S(1)}, u32[]{:S(2)}, u32[]{:S(2)}) collective-permute-start(bf16[2,2,32,1024]{3,2,1,0:T(8,128)(2,1)S(1)} %get-tuple-element.39), channel_id=1, source_target_pairs={{0,1},{1,0},{2,3},{3,2},{4,5},{5,4},{6,7},{7,6},{8,9},{9,8},{10,11... | collective-permute-start | bytes 786440 | tf_op jit(solution)/shard_map/ppermute | solution.py:16
  56.4 14.6 %all-to-all-start.1 = ((bf16[32,32,128]{2,1,0:T(8,128)(2,1)}), bf16[32,32,128]{2,1,0:T(8,128)(2,1)S(1)}, u32[]{:S(2)}, u32[]{:S(2)}) async-start(bf16[32,32,128]{2,1,0:T(8,128)(2,1)} %bitcast.17), calls=%async_computation.1 | async-start | bytes 524288 | tf_op jit(solution)/shard_map/all_to_all | solution.py:39
  61.4 17.7 %collective-permute-start.11 = (bf16[2,32,1024]{2,1,0:T(8,128)(2,1)S(1)}, bf16[2,32,1024]{2,1,0:T(8,128)(2,1)S(1)}, u32[]{:S(2)}, u32[]{:S(2)}) collective-permute-start(bf16[2,32,1024]{2,1,0:T(8,128)(2,1)S(1)} %pad_maximum_fusion.3), channel_id=1, source_target_pairs={{0,130},{2,128},{1,131},{3,129},{4,134},{6,132},{5,135},{7,133},{8... | collective-permute-start | bytes 393224 | tf_op jit(solution)/shard_map/ppermute | solution.py:33
  64.2 14.9 %collective-permute-start.10 = (bf16[2,32,1024]{2,1,0:T(8,128)(2,1)S(1)}, bf16[2,32,1024]{2,1,0:T(8,128)(2,1)S(1)}, u32[]{:S(2)}, u32[]{:S(2)}) collective-permute-start(bf16[2,32,1024]{2,1,0:T(8,128)(2,1)S(1)} %pad_maximum_fusion.2), channel_id=1, source_target_pairs={{0,2},{2,0},{1,3},{3,1},{4,6},{6,4},{5,7},{7,5},{8,10},{10,8},{9,1... | collective-permute-start | bytes 393224 | tf_op jit(solution)/shard_map/ppermute | solution.py:20
  71.8 15.8 %all-to-all-start.2 = ((bf16[32,32,128]{2,1,0:T(8,128)(2,1)}), bf16[32,32,128]{2,1,0:T(8,128)(2,1)S(1)}, u32[]{:S(2)}, u32[]{:S(2)}) async-start(bf16[32,32,128]{2,1,0:T(8,128)(2,1)} %residual.1), calls=%async_computation.2 | async-start | bytes 524288 | tf_op jit(solution)/shard_map/all_to_all | solution.py:39
  78.0 3.9 %collective-permute-start.9 = (bf16[2,32,1024]{2,1,0:T(8,128)(2,1)S(1)}, bf16[2,32,1024]{2,1,0:T(8,128)(2,1)S(1)}, u32[]{:S(2)}, u32[]{:S(2)}) collective-permute-start(bf16[2,32,1024]{2,1,0:T(8,128)(2,1)S(1)} %pad_maximum_fusion.1), channel_id=1, source_target_pairs={{0,128},{4,132},{8,136},{12,140},{16,144},{20,148},{24,152},{28,15... | collective-permute-start | bytes 393224 | tf_op jit(solution)/shard_map/ppermute | solution.py:25
  87.9 4.7 %collective-permute-start.12 = (f32[128,128]{1,0:T(8,128)S(1)}, f32[128,128]{1,0:T(8,128)S(1)}, u32[]{:S(2)}, u32[]{:S(2)}) collective-permute-start(f32[128,128]{1,0:T(8,128)S(1)} %get-tuple-element.44), channel_id=1, source_target_pairs={{0,1},{1,0},{2,3},{3,2},{4,5},{5,4},{6,7},{7,6},{8,9},{9,8},{10,11... | collective-permute-start | bytes 196616 | tf_op jit(solution)/shard_map/ppermute | solution.py:16
  92.6 6.7 %collective-permute-start.14 = (f32[64,128]{1,0:T(8,128)S(1)}, f32[64,128]{1,0:T(8,128)S(1)}, u32[]{:S(2)}, u32[]{:S(2)}) collective-permute-start(f32[64,128]{1,0:T(8,128)S(1)} %pad_maximum_fusion.4), channel_id=1, source_target_pairs={{0,128},{4,132},{8,136},{12,140},{16,144},{20,148},{24,152},{28,15... | collective-permute-start | bytes 98312 | tf_op jit(solution)/shard_map/ppermute | solution.py:25
  93.7 5.5 %collective-permute-start.15 = (f32[64,128]{1,0:T(8,128)S(1)}, f32[64,128]{1,0:T(8,128)S(1)}, u32[]{:S(2)}, u32[]{:S(2)}) collective-permute-start(f32[64,128]{1,0:T(8,128)S(1)} %slice_negate_fusion), channel_id=1, source_target_pairs={{0,130},{2,128},{1,131},{3,129},{4,134},{6,132},{5,135},{7,133},{8... | collective-permute-start | bytes 98312 | tf_op jit(solution)/shard_map/ppermute | solution.py:33
  95.6 4.3 %collective-permute-start.13 = (f32[64,128]{1,0:T(8,128)S(1)}, f32[64,128]{1,0:T(8,128)S(1)}, u32[]{:S(2)}, u32[]{:S(2)}) collective-permute-start(f32[64,128]{1,0:T(8,128)S(1)} %slice_negate_fusion), channel_id=1, source_target_pairs={{0,2},{2,0},{1,3},{3,1},{4,6},{6,4},{5,7},{7,5},{8,10},{10,8},{9,1... | collective-permute-start | bytes 98312 | tf_op jit(solution)/shard_map/ppermute | solution.py:20
  118.0 6.3 %collective-permute-start.16 = (bf16[512,128]{1,0:T(8,128)(2,1)S(1)}, bf16[512,128]{1,0:T(8,128)(2,1)S(1)}, u32[]{:S(2)}, u32[]{:S(2)}) collective-permute-start(bf16[512,128]{1,0:T(8,128)(2,1)S(1)} %get-tuple-element.50), channel_id=1, source_target_pairs={{0,1},{1,0},{2,3},{3,2},{4,5},{5,4},{6,7},{7,6},{8,9},{9,8},{10,11... | collective-permute-start | bytes 393224 | tf_op jit(solution)/shard_map/ppermute | solution.py:16
  124.3 6.3 %collective-permute-start.19 = (bf16[512,128]{1,0:T(8,128)(2,1)S(1)}, bf16[512,128]{1,0:T(8,128)(2,1)S(1)}, u32[]{:S(2)}, u32[]{:S(2)}) collective-permute-start(bf16[512,128]{1,0:T(8,128)(2,1)S(1)} %add_convert_fusion.1), channel_id=1, source_target_pairs={{0,2},{2,0},{1,3},{3,1},{4,6},{6,4},{5,7},{7,5},{8,10},{10,8},{9,1... | collective-permute-start | bytes 393224 | tf_op jit(solution)/shard_map/ppermute | solution.py:20
  126.5 2.9 %collective-permute-start.18 = (bf16[256,128]{1,0:T(8,128)(2,1)S(1)}, bf16[256,128]{1,0:T(8,128)(2,1)S(1)}, u32[]{:S(2)}, u32[]{:S(2)}) collective-permute-start(bf16[256,128]{1,0:T(8,128)(2,1)S(1)} %get-tuple-element.64), channel_id=1, source_target_pairs={{0,1},{1,0},{2,3},{3,2},{4,5},{5,4},{6,7},{7,6},{8,9},{9,8},{10,11... | collective-permute-start | bytes 196616 | tf_op jit(solution)/shard_map/ppermute | solution.py:16
  127.2 2.2 %collective-permute-start.17 = (bf16[256,128]{1,0:T(8,128)(2,1)S(1)}, bf16[256,128]{1,0:T(8,128)(2,1)S(1)}, u32[]{:S(2)}, u32[]{:S(2)}) collective-permute-start(bf16[256,128]{1,0:T(8,128)(2,1)S(1)} %get-tuple-element.63), channel_id=1, source_target_pairs={{0,1},{1,0},{2,3},{3,2},{4,5},{5,4},{6,7},{7,6},{8,9},{9,8},{10,11... | collective-permute-start | bytes 196616 | tf_op jit(solution)/shard_map/ppermute | solution.py:16

commit v7 on v6

--- a/solution.py
+++ b/solution.py
@@ -357,8 +357,9 @@
     product, source = lax.optimization_barrier((product, features))
     own, far = product[: 2 * depth], -product[2 * depth :]
     own = jnp.concatenate([2.0 * query_block - own[:depth], -own[depth:]])
-    crossed = swap_side(own) + swap_chip_and_side(far)
-    corrected = own + swap_chip(far) + jnp.roll(crossed, depth, 0)
+    near, far = own.astype(BF16), far.astype(BF16)
+    crossed = swap_side(near).astype(F32) + swap_chip_and_side(far).astype(F32)
+    corrected = own + swap_chip(far).astype(F32) + jnp.roll(crossed, depth, 0)
     loaded = load_rows(source)
     corrected, loaded = lax.optimization_barrier((corrected.astype(BF16), loaded))
     corrected_cols = exchange_side(jnp.tile(corrected, (width // 2, 1)))

time: 132 us -> 132 us (level)
  transfers between devices with their start and end apart: 22 -> 22, of which waited for: 12 -> 11; matrix products, arithmetic and copies ran while one was open for 1% -> 1% of each run, Pallas kernels for 10% -> 10%
where the time goes in v7:
time: 132 us; the launch traced here: 131 us
  starting transfers between devices  45.5 us (34%)
  blocking collectives  38.4 us (29%)
  waiting for transfers between devices  26.1 us (20%)
  Pallas kernels  18.8 us (14%)
  other arithmetic  1.91 us (1%)
    all_to_all x2, blocking collectives, exchange_side(): lax.all_to_all(blocks, 'wide', 0, 0, tiled=True, axis_index_groups=sides)  38.4 us
    pallas_call x14, Pallas kernels, local_call(): pl.pallas_call(body, in_specs=[anywhere] * outside + [IN_VMEM] * (len(ope...  18.8 us
    ppermute x9, starting transfers between devices, swap_core(): return lax.ppermute(block, 'feat', CORE_SWAP)  17.8 us
    all_to_all x2, waiting for transfers between devices, exchange_side(): lax.all_to_all(blocks, 'wide', 0, 0, tiled=True, axis_index_groups=sides)  12 us
    all_to_all x2, starting transfers between devices, exchange_side(): lax.all_to_all(blocks, 'wide', 0, 0, tiled=True, axis_index_groups=sides)  11.1 us
    ppermute x5, starting transfers between devices, swap_chip(): return lax.ppermute(block, 'feat', CHIP_SWAP)  7.72 us
    ppermute x4, waiting for transfers between devices, swap_side(): lax.ppermute(block, 'wide', [(i, (i + width // 2) % width) for i in range...  7.3 us
    ppermute x2, starting transfers between devices, swap_chip_and_side(): return lax.ppermute(block, ('wide', 'feat'), pairs)  5.35 us
  transfers between devices with their start and end apart: 22, of which 11 were waited for; matrix products, arithmetic and copies ran while one was open for 1% of the time, Pallas kernels for 10%

profile of v7, /device:TPU:1, one launch (start us, length us, event | category | flops | bytes accessed | tf_op | source)
XLA Modules:
  0.0 131.2 jit_solution(11457839027927772078)
XLA Ops:
  0.0 2.5 %precond.1 = (f32[32,128]{1,0:T(8,128)S(1)}, bf16[32,32,128]{2,1,0:T(8,128)(2,1)S(1)}, bf16[2,2,32,1024]{3,2,1,0:T(8,128)(2,1)S(1)}, bf16[2,2,32,1024]{3,2,1,0:T(8,128)(2,1)S(1)}) custom-call(bf16[32,8192]{1,0:T(8,128)(2,1)} %bitcast.36, bf16[128,8192]{1,0:T(8,128)(2,1)} %queries_hbm.1), custom_call_target="tpu_custom_call" | custom-call | tf_op jit(solution)/shard_map/precond/pallas_call | solution.py:48
  2.5 21.4 %all_to_all.31 = bf16[32,32,128]{2,1,0:T(8,128)(2,1)S(1)} all-to-all(bf16[32,32,128]{2,1,0:T(8,128)(2,1)S(1)} %get-tuple-element.31), channel_id=1, replica_groups={{0,4,8,12,16,20,24,28,32,36,40,44,48,52,56,60,64,68,72,76,80,84,88,92,9..., dimensions={0} | all-to-all | bytes 524288 | tf_op jit(solution)/shard_map/all_to_all | solution.py:39
  23.8 1.3 collective-permute-start
  25.1 4.5 %near_rows.1 = (f32[1024,128]{1,0:T(8,128)S(1)}, f32[1024,128]{1,0:T(8,128)S(1)}, bf16[2048,2048]{1,0:T(8,128)(2,1)S(1)}) custom-call(bf16[2048,2048]{1,0:T(8,128)(2,1)} %features_hbm.3, bf16[1024,128]{1,0:T(8,128)(2,1)S(1)} %bitcast.35), custom_call_target="tpu_custom_call" | custom-call | tf_op jit(solution)/shard_map/near_rows/pallas_call | solution.py:48
  30.4 4.4 %collective-permute-start.4 = (bf16[512,128]{1,0:T(8,128)(2,1)S(1)}, bf16[512,128]{1,0:T(8,128)(2,1)S(1)}, u32[]{:S(2)}, u32[]{:S(2)}) collective-permute-start(bf16[512,128]{1,0:T(8,128)(2,1)S(1)} %get-tuple-element.38), channel_id=1, source_target_pairs={{0,1},{1,0},{2,3},{3,2},{4,5},{5,4},{6,7},{7,6},{8,9},{9,8},{10,11... | collective-permute-start | bytes 393224 | tf_op jit(solution)/shard_map/ppermute | solution.py:16
  35.8 3.0 %collective-permute-start.5 = (bf16[512,128]{1,0:T(8,128)(2,1)S(1)}, bf16[512,128]{1,0:T(8,128)(2,1)S(1)}, u32[]{:S(2)}, u32[]{:S(2)}) collective-permute-start(bf16[512,128]{1,0:T(8,128)(2,1)S(1)} %add_convert_fusion.3), channel_id=1, source_target_pairs={{0,2},{2,0},{1,3},{3,1},{4,6},{6,4},{5,7},{7,5},{8,10},{10,8},{9,1... | collective-permute-start | bytes 393224 | tf_op jit(solution)/shard_map/ppermute | solution.py:20
  38.8 1.1 collective-permute-start.2
  39.9 2.1 %collective-permute-done.5 = bf16[512,128]{1,0:T(8,128)(2,1)S(1)} collective-permute-done((bf16[512,128]{1,0:T(8,128)(2,1)S(1)}, bf16[512,128]{1,0:T(8,128)(2,1)S(1)}, u32[]{:S(2)}, u32[]{:S(2)}) %collective-permute-start.5) | collective-permute-done | bytes 131104 | tf_op jit(solution)/shard_map/ppermute | solution.py:20
  42.1 1.3 collective-permute-start.6
  43.4 1.4 %collective-permute-done.2 = bf16[512,128]{1,0:T(8,128)(2,1)S(1)} collective-permute-done((bf16[512,128]{1,0:T(8,128)(2,1)S(1)}, bf16[512,128]{1,0:T(8,128)(2,1)S(1)}, u32[]{:S(2)}, u32[]{:S(2)}) %collective-permute-start.2) | collective-permute-done | bytes 131104 | tf_op jit(solution)/shard_map/ppermute | solution.py:20
  44.9 1.6 %collective-permute-start.3 = (bf16[512,128]{1,0:T(8,128)(2,1)S(1)}, bf16[512,128]{1,0:T(8,128)(2,1)S(1)}, u32[]{:S(2)}, u32[]{:S(2)}) collective-permute-start(bf16[512,128]{1,0:T(8,128)(2,1)S(1)} %add_convert_fusion.4.mine_ref), channel_id=1, source_target_pairs={{0,1},{1,0},{2,3},{3,2},{4,5},{5,4},{6,7},{7,6},{8,9},{9,8},{10,11... | collective-permute-start | bytes 393224 | tf_op jit(solution)/shard_map/ppermute | solution.py:16
  48.0 1.1 collective-permute-start.7
  51.1 4.6 %collective-permute-done.7 = bf16[1024,128]{1,0:T(8,128)(2,1)S(1)} collective-permute-done((bf16[1024,128]{1,0:T(8,128)(2,1)S(1)}, bf16[1024,128]{1,0:T(8,128)(2,1)S(1)}, u32[]{:S(2)}, u32[]{:S(2)}) %collective-permute-start.7) | collective-permute-done | bytes 262176 | tf_op jit(solution)/shard_map/ppermute | solution.py:25
  55.7 0.8 add_convert_fusion
  56.4 4.9 %all-to-all-start.1 = ((bf16[32,32,128]{2,1,0:T(8,128)(2,1)}), bf16[32,32,128]{2,1,0:T(8,128)(2,1)S(1)}, u32[]{:S(2)}, u32[]{:S(2)}) async-start(bf16[32,32,128]{2,1,0:T(8,128)(2,1)} %bitcast.17), calls=%async_computation.1 | async-start | bytes 524288 | tf_op jit(solution)/shard_map/all_to_all | solution.py:39
  61.4 2.8 %collective-permute-start.11 = (bf16[2,32,1024]{2,1,0:T(8,128)(2,1)S(1)}, bf16[2,32,1024]{2,1,0:T(8,128)(2,1)S(1)}, u32[]{:S(2)}, u32[]{:S(2)}) collective-permute-start(bf16[2,32,1024]{2,1,0:T(8,128)(2,1)S(1)} %pad_maximum_fusion.3), channel_id=1, source_target_pairs={{0,130},{2,128},{1,131},{3,129},{4,134},{6,132},{5,135},{7,133},{8... | collective-permute-start | bytes 393224 | tf_op jit(solution)/shard_map/ppermute | solution.py:33
  64.7 6.4 %all-to-all-done.1.parts_ref = bf16[32,32,128]{2,1,0:T(8,128)(2,1)S(1)} async-done(((bf16[32,32,128]{2,1,0:T(8,128)(2,1)}), bf16[32,32,128]{2,1,0:T(8,128)(2,1)S(1)}, u32[]{:S(2)}, u32[]{:S(2)}) %all-to-all-start.1) | async-done | bytes 262176 | tf_op jit(solution)/shard_map/all_to_all | solution.py:39
  71.8 6.1 %all-to-all-start.2 = ((bf16[32,32,128]{2,1,0:T(8,128)(2,1)}), bf16[32,32,128]{2,1,0:T(8,128)(2,1)S(1)}, u32[]{:S(2)}, u32[]{:S(2)}) async-start(bf16[32,32,128]{2,1,0:T(8,128)(2,1)} %residual.1), calls=%async_computation.2 | async-start | bytes 524288 | tf_op jit(solution)/shard_map/all_to_all | solution.py:39
  78.0 1.1 collective-permute-start.9
  79.2 2.7 %collective-permute-done.9 = bf16[2,32,1024]{2,1,0:T(8,128)(2,1)S(1)} collective-permute-done((bf16[2,32,1024]{2,1,0:T(8,128)(2,1)S(1)}, bf16[2,32,1024]{2,1,0:T(8,128)(2,1)S(1)}, u32[]{:S(2)}, u32[]{:S(2)}) %collective-permute-start.9) | collective-permute-done | bytes 131104 | tf_op jit(solution)/shard_map/ppermute | solution.py:25
  82.0 5.6 %all-to-all-done.2 = bf16[32,32,128]{2,1,0:T(8,128)(2,1)S(1)} async-done(((bf16[32,32,128]{2,1,0:T(8,128)(2,1)}), bf16[32,32,128]{2,1,0:T(8,128)(2,1)S(1)}, u32[]{:S(2)}, u32[]{:S(2)}) %all-to-all-start.2) | async-done | bytes 262176 | tf_op jit(solution)/shard_map/all_to_all | solution.py:39
  87.9 3.8 %collective-permute-start.12 = (f32[128,128]{1,0:T(8,128)S(1)}, f32[128,128]{1,0:T(8,128)S(1)}, u32[]{:S(2)}, u32[]{:S(2)}) collective-permute-start(f32[128,128]{1,0:T(8,128)S(1)} %get-tuple-element.44), channel_id=1, source_target_pairs={{0,1},{1,0},{2,3},{3,2},{4,5},{5,4},{6,7},{7,6},{8,9},{9,8},{10,11... | collective-permute-start | bytes 196616 | tf_op jit(solution)/shard_map/ppermute | solution.py:16
  91.6 0.9 collective-permute-done.12
  92.6 2.6 %collective-permute-start.15 = (bf16[64,128]{1,0:T(8,128)(2,1)S(1)}, bf16[64,128]{1,0:T(8,128)(2,1)S(1)}, u32[]{:S(2)}, u32[]{:S(2)}) collective-permute-start(bf16[64,128]{1,0:T(8,128)(2,1)S(1)} %negate_convert_fusion), channel_id=1, source_target_pairs={{0,130},{2,128},{1,131},{3,129},{4,134},{6,132},{5,135},{7,133},{8... | collective-permute-start | bytes 49160 | tf_op jit(solution)/shard_map/ppermute | solution.py:33
  95.2 1.4 %collective-permute-start.13 = (bf16[64,128]{1,0:T(8,128)(2,1)S(1)}, bf16[64,128]{1,0:T(8,128)(2,1)S(1)}, u32[]{:S(2)}, u32[]{:S(2)}) collective-permute-start(bf16[64,128]{1,0:T(8,128)(2,1)S(1)} %negate_convert_fusion), channel_id=1, source_target_pairs={{0,2},{2,0},{1,3},{3,1},{4,6},{6,4},{5,7},{7,5},{8,10},{10,8},{9,1... | collective-permute-start | bytes 49160 | tf_op jit(solution)/shard_map/ppermute | solution.py:20
  96.5 2.9 %load.1.features_ref = bf16[1536,2048]{1,0:T(8,128)(2,1)S(1)} custom-call(bf16[2048,2048]{1,0:T(8,128)(2,1)} %features_hbm.3), custom_call_target="tpu_custom_call" | custom-call | tf_op jit(solution)/shard_map/load/pallas_call | solution.py:48
  99.6 17.0 %all_to_all.32 = bf16[32,64,128]{2,1,0:T(8,128)(2,1)S(1)} all-to-all(bf16[32,64,128]{2,1,0:T(8,128)(2,1)S(1)} %tile.2), channel_id=1, replica_groups={{0,4,8,12,16,20,24,28,32,36,40,44,48,52,56,60,64,68,72,76,80,84,88,92,9..., dimensions={0} | all-to-all | bytes 1048576 | tf_op jit(solution)/shard_map/all_to_all | solution.py:39
  116.6 1.3 far_scores.1
  117.9 5.2 %collective-permute-start.16 = (bf16[512,128]{1,0:T(8,128)(2,1)S(1)}, bf16[512,128]{1,0:T(8,128)(2,1)S(1)}, u32[]{:S(2)}, u32[]{:S(2)}) collective-permute-start(bf16[512,128]{1,0:T(8,128)(2,1)S(1)} %get-tuple-element.50), channel_id=1, source_target_pairs={{0,1},{1,0},{2,3},{3,2},{4,5},{5,4},{6,7},{7,6},{8,9},{9,8},{10,11... | collective-permute-start | bytes 393224 | tf_op jit(solution)/shard_map/ppermute | solution.py:16
  124.2 1.8 %collective-permute-start.19 = (bf16[512,128]{1,0:T(8,128)(2,1)S(1)}, bf16[512,128]{1,0:T(8,128)(2,1)S(1)}, u32[]{:S(2)}, u32[]{:S(2)}) collective-permute-start(bf16[512,128]{1,0:T(8,128)(2,1)S(1)} %add_convert_fusion.1), channel_id=1, source_target_pairs={{0,2},{2,0},{1,3},{3,1},{4,6},{6,4},{5,7},{7,5},{8,10},{10,8},{9,1... | collective-permute-start | bytes 393224 | tf_op jit(solution)/shard_map/ppermute | solution.py:20
  126.8 2.1 %keep_scores.1 = f32[512,128]{1,0:T(8,128)S(1)} custom-call(bf16[2048,2048]{1,0:T(8,128)(2,1)} %features_hbm.3, bf16[2048,128]{1,0:T(8,128)(2,1)S(1)} %get-tuple-element.53.cols_ref), custom_call_target="tpu_custom_call" | custom-call | tf_op jit(solution)/shard_map/keep_scores/pallas_call | solution.py:48
  128.9 1.6 %collective-permute-done.19 = bf16[512,128]{1,0:T(8,128)(2,1)S(1)} collective-permute-done((bf16[512,128]{1,0:T(8,128)(2,1)S(1)}, bf16[512,128]{1,0:T(8,128)(2,1)S(1)}, u32[]{:S(2)}, u32[]{:S(2)}) %collective-permute-start.19) | collective-permute-done | bytes 131104 | tf_op jit(solution)/shard_map/ppermute | solution.py:20
  (54 shorter events, 9.8 us)
Async XLA Ops:
  23.8 5.8 %collective-permute-start = (bf16[1024,128]{1,0:T(8,128)(2,1)S(1)}, bf16[1024,128]{1,0:T(8,128)(2,1)S(1)}, u32[]{:S(2)}, u32[]{:S(2)}) collective-permute-start(bf16[1024,128]{1,0:T(8,128)(2,1)S(1)} %bitcast.34), channel_id=1, source_target_pairs={{0,128},{4,132},{8,136},{12,140},{16,144},{20,148},{24,152},{28,15... | collective-permute-start | bytes 786440 | tf_op jit(solution)/shard_map/ppermute | solution.py:25
  30.4 5.3 %collective-permute-start.4 = (bf16[512,128]{1,0:T(8,128)(2,1)S(1)}, bf16[512,128]{1,0:T(8,128)(2,1)S(1)}, u32[]{:S(2)}, u32[]{:S(2)}) collective-permute-start(bf16[512,128]{1,0:T(8,128)(2,1)S(1)} %get-tuple-element.38), channel_id=1, source_target_pairs={{0,1},{1,0},{2,3},{3,2},{4,5},{5,4},{6,7},{7,6},{8,9},{9,8},{10,11... | collective-permute-start | bytes 393224 | tf_op jit(solution)/shard_map/ppermute | solution.py:16
  35.5 3.3 %collective-permute-start.1 = (bf16[512,128]{1,0:T(8,128)(2,1)S(1)}, bf16[512,128]{1,0:T(8,128)(2,1)S(1)}, u32[]{:S(2)}, u32[]{:S(2)}) collective-permute-start(bf16[512,128]{1,0:T(8,128)(2,1)S(1)} %get-tuple-element.36), channel_id=1, source_target_pairs={{0,1},{1,0},{2,3},{3,2},{4,5},{5,4},{6,7},{7,6},{8,9},{9,8},{10,11... | collective-permute-start | bytes 393224 | tf_op jit(solution)/shard_map/ppermute | solution.py:16
  35.8 6.3 %collective-permute-start.5 = (bf16[512,128]{1,0:T(8,128)(2,1)S(1)}, bf16[512,128]{1,0:T(8,128)(2,1)S(1)}, u32[]{:S(2)}, u32[]{:S(2)}) collective-permute-start(bf16[512,128]{1,0:T(8,128)(2,1)S(1)} %add_convert_fusion.3), channel_id=1, source_target_pairs={{0,2},{2,0},{1,3},{3,1},{4,6},{6,4},{5,7},{7,5},{8,10},{10,8},{9,1... | collective-permute-start | bytes 393224 | tf_op jit(solution)/shard_map/ppermute | solution.py:20
  38.8 6.0 %collective-permute-start.2 = (bf16[512,128]{1,0:T(8,128)(2,1)S(1)}, bf16[512,128]{1,0:T(8,128)(2,1)S(1)}, u32[]{:S(2)}, u32[]{:S(2)}) collective-permute-start(bf16[512,128]{1,0:T(8,128)(2,1)S(1)} %add_convert_fusion.5), channel_id=1, source_target_pairs={{0,2},{2,0},{1,3},{3,1},{4,6},{6,4},{5,7},{7,5},{8,10},{10,8},{9,1... | collective-permute-start | bytes 393224 | tf_op jit(solution)/shard_map/ppermute | solution.py:20
  42.1 4.3 %collective-permute-start.6 = (bf16[512,128]{1,0:T(8,128)(2,1)S(1)}, bf16[512,128]{1,0:T(8,128)(2,1)S(1)}, u32[]{:S(2)}, u32[]{:S(2)}) collective-permute-start(bf16[512,128]{1,0:T(8,128)(2,1)S(1)} %add_convert_fusion.2.mine_ref), channel_id=1, source_target_pairs={{0,1},{1,0},{2,3},{3,2},{4,5},{5,4},{6,7},{7,6},{8,9},{9,8},{10,11... | collective-permute-start | bytes 393224 | tf_op jit(solution)/shard_map/ppermute | solution.py:16
  44.9 2.6 %collective-permute-start.3 = (bf16[512,128]{1,0:T(8,128)(2,1)S(1)}, bf16[512,128]{1,0:T(8,128)(2,1)S(1)}, u32[]{:S(2)}, u32[]{:S(2)}) collective-permute-start(bf16[512,128]{1,0:T(8,128)(2,1)S(1)} %add_convert_fusion.4.mine_ref), channel_id=1, source_target_pairs={{0,1},{1,0},{2,3},{3,2},{4,5},{5,4},{6,7},{7,6},{8,9},{9,8},{10,11... | collective-permute-start | bytes 393224 | tf_op jit(solution)/shard_map/ppermute | solution.py:16
  48.0 7.6 %collective-permute-start.7 = (bf16[1024,128]{1,0:T(8,128)(2,1)S(1)}, bf16[1024,128]{1,0:T(8,128)(2,1)S(1)}, u32[]{:S(2)}, u32[]{:S(2)}) collective-permute-start(bf16[1024,128]{1,0:T(8,128)(2,1)S(1)} %far_gram_0.1), channel_id=1, source_target_pairs={{0,128},{4,132},{8,136},{12,140},{16,144},{20,148},{24,152},{28,15... | collective-permute-start | bytes 786440 | tf_op jit(solution)/shard_map/ppermute | solution.py:25
  49.2 7.2 %collective-permute-start.8 = (bf16[2,2,32,1024]{3,2,1,0:T(8,128)(2,1)S(1)}, bf16[2,2,32,1024]{3,2,1,0:T(8,128)(2,1)S(1)}, u32[]{:S(2)}, u32[]{:S(2)}) collective-permute-start(bf16[2,2,32,1024]{3,2,1,0:T(8,128)(2,1)S(1)} %get-tuple-element.39), channel_id=1, source_target_pairs={{0,1},{1,0},{2,3},{3,2},{4,5},{5,4},{6,7},{7,6},{8,9},{9,8},{10,11... | collective-permute-start | bytes 786440 | tf_op jit(solution)/shard_map/ppermute | solution.py:16
  56.4 14.6 %all-to-all-start.1 = ((bf16[32,32,128]{2,1,0:T(8,128)(2,1)}), bf16[32,32,128]{2,1,0:T(8,128)(2,1)S(1)}, u32[]{:S(2)}, u32[]{:S(2)}) async-start(bf16[32,32,128]{2,1,0:T(8,128)(2,1)} %bitcast.17), calls=%async_computation.1 | async-start | bytes 524288 | tf_op jit(solution)/shard_map/all_to_all | solution.py:39
  61.4 17.7 %collective-permute-start.11 = (bf16[2,32,1024]{2,1,0:T(8,128)(2,1)S(1)}, bf16[2,32,1024]{2,1,0:T(8,128)(2,1)S(1)}, u32[]{:S(2)}, u32[]{:S(2)}) collective-permute-start(bf16[2,32,1024]{2,1,0:T(8,128)(2,1)S(1)} %pad_maximum_fusion.3), channel_id=1, source_target_pairs={{0,130},{2,128},{1,131},{3,129},{4,134},{6,132},{5,135},{7,133},{8... | collective-permute-start | bytes 393224 | tf_op jit(solution)/shard_map/ppermute | solution.py:33
  64.2 14.9 %collective-permute-start.10 = (bf16[2,32,1024]{2,1,0:T(8,128)(2,1)S(1)}, bf16[2,32,1024]{2,1,0:T(8,128)(2,1)S(1)}, u32[]{:S(2)}, u32[]{:S(2)}) collective-permute-start(bf16[2,32,1024]{2,1,0:T(8,128)(2,1)S(1)} %pad_maximum_fusion.2), channel_id=1, source_target_pairs={{0,2},{2,0},{1,3},{3,1},{4,6},{6,4},{5,7},{7,5},{8,10},{10,8},{9,1... | collective-permute-start | bytes 393224 | tf_op jit(solution)/shard_map/ppermute | solution.py:20
  71.8 15.8 %all-to-all-start.2 = ((bf16[32,32,128]{2,1,0:T(8,128)(2,1)}), bf16[32,32,128]{2,1,0:T(8,128)(2,1)S(1)}, u32[]{:S(2)}, u32[]{:S(2)}) async-start(bf16[32,32,128]{2,1,0:T(8,128)(2,1)} %residual.1), calls=%async_computation.2 | async-start | bytes 524288 | tf_op jit(solution)/shard_map/all_to_all | solution.py:39
  78.0 3.9 %collective-permute-start.9 = (bf16[2,32,1024]{2,1,0:T(8,128)(2,1)S(1)}, bf16[2,32,1024]{2,1,0:T(8,128)(2,1)S(1)}, u32[]{:S(2)}, u32[]{:S(2)}) collective-permute-start(bf16[2,32,1024]{2,1,0:T(8,128)(2,1)S(1)} %pad_maximum_fusion.1), channel_id=1, source_target_pairs={{0,128},{4,132},{8,136},{12,140},{16,144},{20,148},{24,152},{28,15... | collective-permute-start | bytes 393224 | tf_op jit(solution)/shard_map/ppermute | solution.py:25
  87.9 4.7 %collective-permute-start.12 = (f32[128,128]{1,0:T(8,128)S(1)}, f32[128,128]{1,0:T(8,128)S(1)}, u32[]{:S(2)}, u32[]{:S(2)}) collective-permute-start(f32[128,128]{1,0:T(8,128)S(1)} %get-tuple-element.44), channel_id=1, source_target_pairs={{0,1},{1,0},{2,3},{3,2},{4,5},{5,4},{6,7},{7,6},{8,9},{9,8},{10,11... | collective-permute-start | bytes 196616 | tf_op jit(solution)/shard_map/ppermute | solution.py:16
  92.6 6.8 %collective-permute-start.15 = (bf16[64,128]{1,0:T(8,128)(2,1)S(1)}, bf16[64,128]{1,0:T(8,128)(2,1)S(1)}, u32[]{:S(2)}, u32[]{:S(2)}) collective-permute-start(bf16[64,128]{1,0:T(8,128)(2,1)S(1)} %negate_convert_fusion), channel_id=1, source_target_pairs={{0,130},{2,128},{1,131},{3,129},{4,134},{6,132},{5,135},{7,133},{8... | collective-permute-start | bytes 49160 | tf_op jit(solution)/shard_map/ppermute | solution.py:33
  95.2 4.3 %collective-permute-start.14 = (bf16[64,128]{1,0:T(8,128)(2,1)S(1)}, bf16[64,128]{1,0:T(8,128)(2,1)S(1)}, u32[]{:S(2)}, u32[]{:S(2)}) collective-permute-start(bf16[64,128]{1,0:T(8,128)(2,1)S(1)} %fusion.1), channel_id=1, source_target_pairs={{0,128},{4,132},{8,136},{12,140},{16,144},{20,148},{24,152},{28,15... | collective-permute-start | bytes 49160 | tf_op jit(solution)/shard_map/ppermute | solution.py:25
  95.2 4.3 %collective-permute-start.13 = (bf16[64,128]{1,0:T(8,128)(2,1)S(1)}, bf16[64,128]{1,0:T(8,128)(2,1)S(1)}, u32[]{:S(2)}, u32[]{:S(2)}) collective-permute-start(bf16[64,128]{1,0:T(8,128)(2,1)S(1)} %negate_convert_fusion), channel_id=1, source_target_pairs={{0,2},{2,0},{1,3},{3,1},{4,6},{6,4},{5,7},{7,5},{8,10},{10,8},{9,1... | collective-permute-start | bytes 49160 | tf_op jit(solution)/shard_map/ppermute | solution.py:20
  117.9 6.2 %collective-permute-start.16 = (bf16[512,128]{1,0:T(8,128)(2,1)S(1)}, bf16[512,128]{1,0:T(8,128)(2,1)S(1)}, u32[]{:S(2)}, u32[]{:S(2)}) collective-permute-start(bf16[512,128]{1,0:T(8,128)(2,1)S(1)} %get-tuple-element.50), channel_id=1, source_target_pairs={{0,1},{1,0},{2,3},{3,2},{4,5},{5,4},{6,7},{7,6},{8,9},{9,8},{10,11... | collective-permute-start | bytes 393224 | tf_op jit(solution)/shard_map/ppermute | solution.py:16
  124.2 6.3 %collective-permute-start.19 = (bf16[512,128]{1,0:T(8,128)(2,1)S(1)}, bf16[512,128]{1,0:T(8,128)(2,1)S(1)}, u32[]{:S(2)}, u32[]{:S(2)}) collective-permute-start(bf16[512,128]{1,0:T(8,128)(2,1)S(1)} %add_convert_fusion.1), channel_id=1, source_target_pairs={{0,2},{2,0},{1,3},{3,1},{4,6},{6,4},{5,7},{7,5},{8,10},{10,8},{9,1... | collective-permute-start | bytes 393224 | tf_op jit(solution)/shard_map/ppermute | solution.py:20
  126.0 2.9 %collective-permute-start.18 = (bf16[256,128]{1,0:T(8,128)(2,1)S(1)}, bf16[256,128]{1,0:T(8,128)(2,1)S(1)}, u32[]{:S(2)}, u32[]{:S(2)}) collective-permute-start(bf16[256,128]{1,0:T(8,128)(2,1)S(1)} %get-tuple-element.64), channel_id=1, source_target_pairs={{0,1},{1,0},{2,3},{3,2},{4,5},{5,4},{6,7},{7,6},{8,9},{9,8},{10,11... | collective-permute-start | bytes 196616 | tf_op jit(solution)/shard_map/ppermute | solution.py:16
  126.7 2.2 %collective-permute-start.17 = (bf16[256,128]{1,0:T(8,128)(2,1)S(1)}, bf16[256,128]{1,0:T(8,128)(2,1)S(1)}, u32[]{:S(2)}, u32[]{:S(2)}) collective-permute-start(bf16[256,128]{1,0:T(8,128)(2,1)S(1)} %get-tuple-element.63), channel_id=1, source_target_pairs={{0,1},{1,0},{2,3},{3,2},{4,5},{5,4},{6,7},{7,6},{8,9},{9,8},{10,11... | collective-permute-start | bytes 196616 | tf_op jit(solution)/shard_map/ppermute | solution.py:16
